TPU v7x, 256 devices: a whole 4x4x8 slice. The times are simulated.
256 devices in a mesh: segment: 4 (over x), dp: 8 (over z), tensor: 8 (over y, core).
Axes of the slice: x: 4, y: 4, z: 8, core: 2. Of those that a mesh axis runs over, the one named last changes fastest.
Arguments:
- inputs: bfloat16 [1, 64, 7168], P(None, ('dp', 'tensor')), may hold values from -6 to 6
- exit_at: int32 [1, 64], replicated, may hold values from 0 to 2
- targets: int32 [1, 64], replicated, may hold values from 0 to 25599
- repack: int32 [1, 2, 64], replicated, may hold values from 0 to 63, each once within a row
- norm_gain: float32 [4, 7168], P('segment'), may hold values from 0.5 to 1.5
- up_weight: bfloat16 [4, 14336, 7168], P('segment', ('dp', 'tensor')), may hold values from -0.0625 to 0.0625
- down_weight: bfloat16 [4, 14336, 7168], P('segment', ('dp', 'tensor')), may hold values from -0.046875 to 0.046875
- exit_gain: float32 [7168], replicated, may hold values from 0.5 to 1.5
- head: bfloat16 [25600, 7168], P(('dp', 'tensor')), may hold values from -0.21875 to 0.21875
Outputs:
- section_out: bfloat16 [4, 1, 64, 7168], P('segment', None, ('dp', 'tensor'))
- exit_logprob: float32 [1, 64], P(None, ('dp', 'tensor'))
Inputs may be any that keep to these rules, and one draw needn't show every extreme that they name: Each repack[m, k] is a permutation of the 64 positions.
All inputs are finite; a program needn't handle non-finite values.
Results may differ from a plain program's by a relative error of at most 0.015.
Values may be sent and summed in bfloat16 or wider, within the bound.
No kernel may reach another device: no remote copies, remote signals or barrier semaphores. Data moves between devices by JAX's collectives and lax.ppermute only.
A program may use at most 64 MiB of HBM per device.

v0:
```python
import jax
import jax.numpy as jnp
from jax import lax
from jax.sharding import PartitionSpec as P

EPSILON = 1e-05


def passed_along(value, axis, steps):
    count = lax.axis_size(axis)
    initial, last = (max(0, -steps), min(count, count - steps))
    return lax.ppermute(value, axis, [(source, source + steps) for source in range(initial, last)])


def layer_norm(buffer, scale):
    values = buffer.astype(jnp.float32)
    center = values - jnp.mean(values, axis=-1, keepdims=True)
    spread = jnp.mean(center * center, axis=-1, keepdims=True)
    return center * lax.rsqrt(spread + EPSILON) * scale


def contract(left, right):
    return lax.dot_general(
        left, right, (((1,), (1,)), ((), ())), preferred_element_type=jnp.float32
    )


def on_device(inputs, exit_at, targets, repack, norm_gain, up_weight, down_weight, exit_gain, head):
    section_index = lax.axis_index("segment")
    section_count = lax.axis_size("segment")
    group_index = lax.axis_index(("dp", "tensor"))
    slice_rows = inputs.shape[1]
    micro_count = inputs.shape[0]
    model_width = inputs.shape[2]
    row_count = slice_rows * lax.axis_size(("dp", "tensor"))
    vocab_cols = head.shape[0]
    norm_scale = norm_gain[0]
    up_matrix = up_weight[0]
    down_matrix = down_weight[0]
    tick_count = micro_count + section_count - 1
    positions = jnp.arange(row_count, dtype=jnp.int32)
    columns = jnp.arange(vocab_cols, dtype=jnp.int32) + group_index * vocab_cols
    needs_head = (section_index >= 1) & (section_index <= 2)

    def orders(batch_safe):
        first = repack[batch_safe, 0]
        second_source = repack[batch_safe, 1]
        second = first[second_source]
        before_table = jnp.stack([positions, positions, first, second])
        source_table = jnp.stack([positions, first, second_source, positions])
        before = before_table[section_index]
        source = source_table[section_index]
        return (before, source, before[source])

    def advance(tick, state_all):
        received, stored, scores = state_all
        batch_index = tick - section_index
        active = (batch_index >= 0) & (batch_index < micro_count)
        batch_safe = jnp.clip(batch_index, 0, micro_count - 1)
        before, source, after_order = orders(batch_safe)
        leaving = exit_at[batch_safe]
        fresh_rows = lax.dynamic_index_in_dim(inputs, batch_safe, 0, keepdims=False)
        own_rows = jnp.where(section_index == 0, fresh_rows, received)
        gathered = lax.all_gather(own_rows, ("dp", "tensor"), axis=0, tiled=True)
        wanted = targets[batch_safe][before]

        def head_terms(rows_in):
            exit_normed = layer_norm(rows_in, exit_gain).astype(jnp.bfloat16)
            logits = contract(exit_normed, head)
            exp_part = jnp.sum(jnp.exp(logits), axis=1)
            picked_part = jnp.sum(
                jnp.where(columns[None, :] == wanted[:, None], logits, 0.0), axis=1
            )
            return (exp_part, picked_part)

        def head_skipped(rows_in):
            return (jnp.ones((row_count,), jnp.float32), jnp.zeros((row_count,), jnp.float32))

        exp_total, picked = lax.cond(needs_head, head_terms, head_skipped, gathered)
        exp_total, picked = lax.psum((exp_total, picked), ("dp", "tensor"))
        chosen = (leaving[before] == section_index) & needs_head & active
        scored = jnp.where(chosen, picked - jnp.log(exp_total), 0.0)
        scores = scores.at[batch_safe, before].add(scored)
        normed = layer_norm(gathered, norm_scale).astype(jnp.bfloat16)
        hidden_old = jax.nn.gelu(contract(normed, up_matrix), approximate=False)
        exit_rank = leaving[after_order]
        living = (exit_rank == 0) | (exit_rank > section_index)
        hidden = jnp.where(living[:, None], hidden_old[source], 0.0).astype(jnp.bfloat16)
        own_source = lax.dynamic_slice_in_dim(source, group_index * slice_rows, slice_rows)
        own_living = lax.dynamic_slice_in_dim(living, group_index * slice_rows, slice_rows)
        residual = jnp.where(
            own_living[:, None],
            gathered[own_source],
            jnp.zeros((slice_rows, model_width), jnp.bfloat16),
        ).astype(jnp.float32)
        summed = lax.psum_scatter(
            jnp.dot(hidden, down_matrix, preferred_element_type=jnp.float32),
            ("dp", "tensor"),
            scatter_dimension=0,
            tiled=True,
        )
        result = (residual + summed).astype(jnp.bfloat16)
        stored = stored.at[batch_safe].set(jnp.where(active, result, stored[batch_safe]))
        passed = passed_along(result, "segment", 1)
        return (passed, stored, scores)

    initial = (
        jnp.zeros((slice_rows, model_width), jnp.bfloat16),
        jnp.zeros((micro_count, slice_rows, model_width), jnp.bfloat16),
        jnp.zeros((micro_count, row_count), jnp.float32),
    )
    received, stored, scores = lax.fori_loop(0, tick_count, advance, initial)
    own_scores = lax.dynamic_slice_in_dim(scores, group_index * slice_rows, slice_rows, 1)
    own_scores = lax.psum(own_scores, "segment")
    return (stored[None], own_scores)


def solution(mesh):
    placed = (
        P(None, ("dp", "tensor"), None),
        P(),
        P(),
        P(),
        P("segment", None),
        P("segment", ("dp", "tensor"), None),
        P("segment", ("dp", "tensor"), None),
        P(),
        P(("dp", "tensor"), None),
    )
    return jax.shard_map(
        on_device,
        mesh=mesh,
        in_specs=placed,
        out_specs=(P("segment", None, ("dp", "tensor"), None), P(None, ("dp", "tensor"))),
        check_vma=False,
    )
```

profile of v0, /device:TPU:2, one launch (start us, length us, event | category | flops | bytes accessed | tf_op | source)
XLA Modules:
  0.0 1051.3 jit_solution(109699895213309416)
XLA Ops:
  14.3 1020.7 %while.26 = (s32[]{:T(128)}, bf16[1,7168]{1,0:T(2,128)(2,1)S(1)}, bf16[1,1,7168]{2,1,0:T(2,128)(2,1)S(1)}, f32[1,64]{1,0:T(1,128)S(1)}, s32[64]{0:T(128)S(1)}, /...) while((s32[]{:T(128)}, bf16[1,7168]{1,0:T(2,128)(2,1)S(1)}, ...), condition=%wide.region_14.15_spmd.clone, body=%wide.region_0.14_spmd.clone.sunk | while | flops 789705216 | bytes 45827648 | solution.py:112
  15.2 54.2 %all-gather.3 = bf16[64,1,7168]{2,1,0:T(2,128)(2,1)S(1)} all-gather(bf16[1,1,7168]{2,1,0:T(2,128)(2,1)S(1)} %fusion.69), channel_id=1, replica_groups=mesh['segment'=4,'dp'=8,'tensor'=8] {'dp','tensor'}, dimensions={0}, use_global_device_ids=true | all-gather | bytes 931840 | tf_op jit(solution)/shard_map/while/body/eval_jaxpr/all_gather | solution.py:64
  73.3 3.9 fusion.73
  79.3 6.1 conditional.3
  80.7 4.6 select_reduce_fusion
  85.3 126.8 %all-reduce.6 = (f32[64]{0:T(128)S(1)}, f32[64]{0:T(128)S(1)}) all-reduce(f32[64]{0:T(128)S(1)} %get-tuple-element.1212, f32[64]{0:T(128)S(1)} %get-tuple-element.1213), channel_id=1, replica_groups=mesh['segment'=4,'dp'=8,'tensor'=8] {'dp','tensor'}, use_global_device_ids=true, to_apply=%region_11.11 | all-reduce | flops 128 | bytes 1024 | tf_op jit(solution)/shard_map/while/body/eval_jaxpr/psum | solution.py:80
  212.9 52.3 %all-reduce.9.cloned.1.call-done = f32[64,7168]{1,0:T(8,128)} async-done(((f32[64,7168]{1,0:T(8,128)}), f32[64,7168]{1,0:T(8,128)}) %all-reduce.9.cloned.1.call-update) | async-done | bytes 1835024 | tf_op jit(solution)/shard_map/while
  265.2 2.9 broadcast_select_fusion.7
  268.1 3.4 collective-permute-start
  274.6 48.6 %all-gather.3 = bf16[64,1,7168]{2,1,0:T(2,128)(2,1)S(1)} all-gather(bf16[1,1,7168]{2,1,0:T(2,128)(2,1)S(1)} %fusion.69), channel_id=1, replica_groups=mesh['segment'=4,'dp'=8,'tensor'=8] {'dp','tensor'}, dimensions={0}, use_global_device_ids=true | all-gather | bytes 931840 | tf_op jit(solution)/shard_map/while/body/eval_jaxpr/all_gather | solution.py:64
  327.2 3.9 fusion.73
  333.2 6.1 conditional.3
  334.7 4.6 select_reduce_fusion
  339.3 126.7 %all-reduce.6 = (f32[64]{0:T(128)S(1)}, f32[64]{0:T(128)S(1)}) all-reduce(f32[64]{0:T(128)S(1)} %get-tuple-element.1212, f32[64]{0:T(128)S(1)} %get-tuple-element.1213), channel_id=1, replica_groups=mesh['segment'=4,'dp'=8,'tensor'=8] {'dp','tensor'}, use_global_device_ids=true, to_apply=%region_11.11 | all-reduce | flops 128 | bytes 1024 | tf_op jit(solution)/shard_map/while/body/eval_jaxpr/psum | solution.py:80
  466.8 52.1 %all-reduce.9.cloned.1.call-done = f32[64,7168]{1,0:T(8,128)} async-done(((f32[64,7168]{1,0:T(8,128)}), f32[64,7168]{1,0:T(8,128)}) %all-reduce.9.cloned.1.call-update) | async-done | bytes 1835024 | tf_op jit(solution)/shard_map/while
  518.8 2.9 broadcast_select_fusion.7
  521.7 3.4 collective-permute-start
  528.3 48.6 %all-gather.3 = bf16[64,1,7168]{2,1,0:T(2,128)(2,1)S(1)} all-gather(bf16[1,1,7168]{2,1,0:T(2,128)(2,1)S(1)} %fusion.69), channel_id=1, replica_groups=mesh['segment'=4,'dp'=8,'tensor'=8] {'dp','tensor'}, dimensions={0}, use_global_device_ids=true | all-gather | bytes 931840 | tf_op jit(solution)/shard_map/while/body/eval_jaxpr/all_gather | solution.py:64
  580.9 3.9 fusion.73
  586.9 6.1 conditional.3
  588.3 4.6 select_reduce_fusion
  592.9 126.8 %all-reduce.6 = (f32[64]{0:T(128)S(1)}, f32[64]{0:T(128)S(1)}) all-reduce(f32[64]{0:T(128)S(1)} %get-tuple-element.1212, f32[64]{0:T(128)S(1)} %get-tuple-element.1213), channel_id=1, replica_groups=mesh['segment'=4,'dp'=8,'tensor'=8] {'dp','tensor'}, use_global_device_ids=true, to_apply=%region_11.11 | all-reduce | flops 128 | bytes 1024 | tf_op jit(solution)/shard_map/while/body/eval_jaxpr/psum | solution.py:80
  720.5 52.2 %all-reduce.9.cloned.1.call-done = f32[64,7168]{1,0:T(8,128)} async-done(((f32[64,7168]{1,0:T(8,128)}), f32[64,7168]{1,0:T(8,128)}) %all-reduce.9.cloned.1.call-update) | async-done | bytes 1835024 | tf_op jit(solution)/shard_map/while
  775.5 3.4 collective-permute-start
  782.1 48.6 %all-gather.3 = bf16[64,1,7168]{2,1,0:T(2,128)(2,1)S(1)} all-gather(bf16[1,1,7168]{2,1,0:T(2,128)(2,1)S(1)} %fusion.69), channel_id=1, replica_groups=mesh['segment'=4,'dp'=8,'tensor'=8] {'dp','tensor'}, dimensions={0}, use_global_device_ids=true | all-gather | bytes 931840 | tf_op jit(solution)/shard_map/while/body/eval_jaxpr/all_gather | solution.py:64
  834.6 3.9 fusion.73
  840.6 6.1 conditional.3
  842.1 4.6 select_reduce_fusion
  846.7 126.8 %all-reduce.6 = (f32[64]{0:T(128)S(1)}, f32[64]{0:T(128)S(1)}) all-reduce(f32[64]{0:T(128)S(1)} %get-tuple-element.1212, f32[64]{0:T(128)S(1)} %get-tuple-element.1213), channel_id=1, replica_groups=mesh['segment'=4,'dp'=8,'tensor'=8] {'dp','tensor'}, use_global_device_ids=true, to_apply=%region_11.11 | all-reduce | flops 128 | bytes 1024 | tf_op jit(solution)/shard_map/while/body/eval_jaxpr/psum | solution.py:80
  974.3 52.1 %all-reduce.9.cloned.1.call-done = f32[64,7168]{1,0:T(8,128)} async-done(((f32[64,7168]{1,0:T(8,128)}), f32[64,7168]{1,0:T(8,128)}) %all-reduce.9.cloned.1.call-update) | async-done | bytes 1835024 | tf_op jit(solution)/shard_map/while
  1029.3 3.4 collective-permute-start
  1035.6 9.2 psum.41
  (187 shorter events, 56.9 us)
Async XLA Ops:
  14.3 250.9 %all-reduce.9.cloned.1.call-start = ((), (), s32[]{:S(2)}) async-start(), calls=%async_computation | async-start | bytes 3670016 | tf_op jit(solution)/shard_map/while
  69.3 1.9 copy-start.4
  69.3 1.9 copy-start.5
  77.1 0.7 copy-start
  77.2 1.4 copy-start.6
  77.2 2.1 copy-start.1
  77.2 2.1 copy-start.3
  268.1 5.8 collective-permute-start
  273.8 245.0 %all-reduce.9.cloned.1.call-start = ((), (), s32[]{:S(2)}) async-start(), calls=%async_computation | async-start | bytes 3670016 | tf_op jit(solution)/shard_map/while
  323.3 1.9 copy-start.4
  323.3 1.9 copy-start.5
  331.1 1.4 copy-start.6
  331.1 2.1 copy-start.1
  331.1 2.1 copy-start.3
  521.7 5.8 collective-permute-start
  527.5 245.1 %all-reduce.9.cloned.1.call-start = ((), (), s32[]{:S(2)}) async-start(), calls=%async_computation | async-start | bytes 3670016 | tf_op jit(solution)/shard_map/while
  576.9 1.9 copy-start.4
  576.9 1.9 copy-start.5
  584.7 0.7 copy-start
  584.7 1.4 copy-start.6
  584.7 2.1 copy-start.1
  584.7 2.1 copy-start.3
  775.5 5.8 collective-permute-start
  781.3 245.1 %all-reduce.9.cloned.1.call-start = ((), (), s32[]{:S(2)}) async-start(), calls=%async_computation | async-start | bytes 3670016 | tf_op jit(solution)/shard_map/while
  830.7 1.9 copy-start.4
  830.7 1.9 copy-start.5
  838.5 0.7 copy-start
  838.5 1.4 copy-start.6
  838.5 2.1 copy-start.1
  838.5 2.1 copy-start.3
  1029.3 5.8 collective-permute-start
  1035.0 9.8 copy-start.2
  (1 other events, 0.7 us)
Sparse Core Ops, SparseCore 0:
  77.3 187.8 all-reduce.8
  331.2 187.5 all-reduce.8
  584.9 187.6 all-reduce.8
  838.7 187.6 all-reduce.8
where the time goes:
time: 1050 us
  blocking collectives  716 us (68%)
  waiting for transfers between devices  214 us (20%)
  matrix products  39.1 us (4%)
  other arithmetic  28.8 us (3%)
  local copies, waits for them, and re-layouts  23.1 us (2%)
  between operations  15.7 us (1%)
  starting transfers between devices  13.6 us (1%)
    psum x4, blocking collectives, advance(): exp_total, picked = lax.psum((exp_total, picked), ('dp', 'tensor'))  507 us
    while x8, waiting for transfers between devices  209 us
    all_gather x4, blocking collectives, advance(): gathered = lax.all_gather(own_rows, ('dp', 'tensor'), axis=0, tiled=True)  200 us
    dot_general x8, matrix products, contract(): lax.dot_general(left, right, (((1,), (1,)), ((), ())), preferred_element_...  23.5 us
  transfers between devices with their start and end apart: 8, of which 8 were waited for; matrix products, arithmetic and copies ran while one was open for 4% of the time, Pallas kernels for 0%

commit v1 on v0

v1 whole, which is shorter than its diff:
```python
import functools

import jax
import jax.numpy as jnp
from jax import lax
from jax.experimental import pallas as pl
from jax.experimental.pallas import tpu as pltpu
from jax.sharding import Mesh, PartitionSpec as P

EPSILON = 1e-05
SQRT_HALF = 0.7071067811865476
VMEM_LIMIT = 24 * 1024 * 1024
PLANE = ("dp", "y")
NT = (((1,), (1,)), ((), ()))


def normalise(own_ref, sib_ref, gain_ref, living, out_ref):
    blocks, half, cols = own_ref.shape
    width = blocks * cols
    for index, ref in enumerate((own_ref, sib_ref)):
        live = living[index * half : (index + 1) * half]

        def block(b, ref=ref, live=live):
            values = ref[b].astype(jnp.float32)
            return jnp.where(live, values, 0.0)

        total = jnp.zeros((half, cols), jnp.float32)
        for b in range(blocks):
            total += block(b)
        mean = jnp.sum(total, axis=1, keepdims=True) / width
        total = jnp.zeros((half, cols), jnp.float32)
        for b in range(blocks):
            center = block(b) - mean
            total += center * center
        scale = lax.rsqrt(jnp.sum(total, axis=1, keepdims=True) / width + EPSILON)
        for b in range(blocks):
            lanes = slice(b * cols, (b + 1) * cols)
            normed = (block(b) - mean) * scale * gain_ref[:, lanes]
            out_ref[index * half : (index + 1) * half, lanes] = normed.astype(jnp.bfloat16)


def section_kernel(
    section, last, own_ref, sib_ref, exit_ref, order_ref, gain_ref, up_ref, down_ref,
    keep_ref, send_ref, normed_ref
):
    blocks, half, cols = own_ref.shape
    rows = 2 * half
    rank = exit_ref[...]
    living = (rank == 0) | (rank > section)
    normalise(own_ref, sib_ref, gain_ref, living, normed_ref)
    pre = lax.dot_general(normed_ref[...], up_ref[...], NT, preferred_element_type=jnp.float32)
    hidden = (0.5 * pre * (1.0 + lax.erf(pre * SQRT_HALF))).astype(jnp.bfloat16)
    if last:
        slots = lax.broadcasted_iota(jnp.int32, (rows, rows), 1)
        choose = jnp.where(order_ref[...] == slots, 1.0, 0.0).astype(jnp.bfloat16)
        hidden = jnp.dot(choose, hidden, preferred_element_type=jnp.float32).astype(jnp.bfloat16)
    step = 2
    for b in range(0, blocks, step):
        part = jnp.dot(
            hidden, down_ref[:, b * cols : (b + step) * cols], preferred_element_type=jnp.float32
        ).astype(jnp.bfloat16)
        for k in range(step):
            keep_ref[b + k] = part[:half, k * cols : (k + 1) * cols]
            send_ref[b + k] = part[half:, k * cols : (k + 1) * cols]


def run_section(section, last, own, sib, ranks, order, gain, up_matrix, down_matrix):
    blocks, half, cols = own.shape
    vmem = pl.BlockSpec(memory_space=pltpu.VMEM)
    block = jax.ShapeDtypeStruct(own.shape, jnp.bfloat16)
    hidden = up_matrix.shape[0]
    return pl.pallas_call(
        functools.partial(section_kernel, section, last),
        out_shape=(block, block),
        in_specs=[vmem] * 7,
        out_specs=(vmem, vmem),
        scratch_shapes=[pltpu.VMEM((2 * half, blocks * cols), jnp.bfloat16)],
        compiler_params=pltpu.CompilerParams(vmem_limit_bytes=VMEM_LIMIT),
        cost_estimate=pl.CostEstimate(
            flops=8 * half * blocks * cols * hidden,
            bytes_accessed=4 * hidden * blocks * cols,
            transcendentals=2 * half * hidden,
        ),
        name="section",
    )(own, sib, ranks, order, gain, up_matrix, down_matrix)


def head_kernel(own_ref, sib_ref, wanted_ref, gain_ref, head_ref, out_ref, normed_ref):
    blocks, half, cols = own_ref.shape
    rows = 2 * half
    normalise(own_ref, sib_ref, gain_ref, jnp.full((rows, 1), True), normed_ref)
    logits = lax.dot_general(normed_ref[...], head_ref[...], NT, preferred_element_type=jnp.float32)
    exp_part = jnp.sum(jnp.exp(logits), axis=1, keepdims=True)
    columns = lax.broadcasted_iota(jnp.int32, logits.shape, 1)
    picked = jnp.sum(jnp.where(columns == wanted_ref[...], logits, 0.0), axis=1, keepdims=True)
    lane = lax.broadcasted_iota(jnp.int32, (rows, 128), 1)
    out_ref[...] = jnp.where(lane == 0, exp_part, jnp.where(lane == 1, picked, 0.0))


def run_head(own, sib, wanted, gain, head):
    blocks, half, cols = own.shape
    vmem = pl.BlockSpec(memory_space=pltpu.VMEM)
    return pl.pallas_call(
        head_kernel,
        out_shape=jax.ShapeDtypeStruct((2 * half, 128), jnp.float32),
        in_specs=[vmem] * 5,
        out_specs=vmem,
        scratch_shapes=[pltpu.VMEM((2 * half, blocks * cols), jnp.bfloat16)],
        compiler_params=pltpu.CompilerParams(vmem_limit_bytes=VMEM_LIMIT),
        cost_estimate=pl.CostEstimate(
            flops=4 * half * blocks * cols * head.shape[0],
            bytes_accessed=2 * head.shape[0] * blocks * cols,
            transcendentals=2 * half * head.shape[0],
        ),
        name="exit_head",
    )(own, sib, wanted, gain, head)


def swapped(value):
    return lax.ppermute(value, "core", [(0, 1), (1, 0)])


def exchanged(value):
    return lax.all_to_all(value, PLANE, 0, 0, tiled=True)


def on_device(inputs, exit_at, targets, repack, norm_gain, up_weight, down_weight, exit_gain, head):
    section_index = lax.axis_index("segment")
    section_count = lax.axis_size("segment")
    core = lax.axis_index("core")
    z_index = lax.axis_index("dp")
    y_index = lax.axis_index("y")
    blocks = lax.axis_size("dp")
    y_count = lax.axis_size("y")
    members = blocks * y_count
    width = inputs.shape[2]
    cols = width // blocks
    half = exit_at.shape[1] // 2
    sub = half // y_count
    place = z_index * y_count + y_index
    position = place * 2 + core
    group_index = position
    vocab_cols = head.shape[0]
    up_matrix, down_matrix = up_weight[0], down_weight[0]
    first, second_source = repack[0, 0], repack[0, 1]
    leaving = exit_at[0]

    def by_slot(values):
        pairs = values.reshape(half, 2)
        own = jnp.where(core == 0, pairs[:, 0], pairs[:, 1])
        sib = jnp.where(core == 0, pairs[:, 1], pairs[:, 0])
        return jnp.concatenate([own, sib])

    def slot_of(row):
        return row // 2 + half * (row % 2 != core).astype(jnp.int32)

    ranks = by_slot(leaving)[:, None]
    anchor_last = first[second_source]
    order = slot_of(by_slot(anchor_last))[:, None]
    wanted = by_slot(targets[0])[:, None] - group_index * vocab_cols
    own_anchor = jnp.where(
        section_index == 3,
        anchor_last[position],
        jnp.where(section_index == 2, first[position], position),
    )
    own_slot = slot_of(own_anchor)
    exit_scale = exit_gain[None, :]

    def row_of(own, sib):
        at = own_slot % half
        from_own = lax.dynamic_slice(own, (0, at, 0), (blocks, 1, cols))
        from_sib = lax.dynamic_slice(sib, (0, at, 0), (blocks, 1, cols))
        return jnp.where(own_slot < half, from_own, from_sib)[:, 0, :]

    def spread(chunk):
        return jnp.broadcast_to(chunk[None], (members, *chunk.shape))

    mine = inputs[0].reshape(blocks, cols)
    gathered = exchanged(spread(mine))
    own = jnp.swapaxes(gathered, 0, 1)
    chunk = lax.dynamic_slice(own, (z_index, y_index * sub, 0), (1, sub, cols))[0]
    kept = {}
    selected = jnp.zeros((blocks, cols), jnp.bfloat16)
    scores = None
    for section in range(4):
        last = section == 3
        if section:
            payload = spread(chunk)
            if last:

                def head_stats(own_in, sib_in):
                    stats = run_head(own_in, sib_in, wanted, exit_scale, head)[:, :2]
                    high = lax.reduce_precision(stats, 8, 7)
                    four = jnp.concatenate([high, stats - high], axis=1).astype(jnp.bfloat16)
                    four = jnp.stack([four[:half], four[half:]], axis=1)
                    return jnp.pad(four, ((0, 0), (0, sub - 2), (0, cols - 4)))

                payload = lax.switch(
                    section_index,
                    [
                        lambda: payload,
                        lambda: head_stats(*kept[1]),
                        lambda: head_stats(*kept[2]),
                        lambda: payload,
                    ],
                )
            own = exchanged(payload).reshape(blocks, half, cols)
        sib = swapped(own)
        if section:
            kept[section] = (own, sib)
            selected = jnp.where(section_index == section, row_of(own, sib), selected)
        if last:
            first_sums = own.reshape(members, sub, cols)[:, 0, :4].astype(jnp.float32)
            other_sums = sib.reshape(members, sub, cols)[:, 1, :4].astype(jnp.float32)
            sums = jnp.sum(first_sums + other_sums, axis=0)
            exp_total, picked = sums[0] + sums[2], sums[1] + sums[3]
            needs = (section_index >= 1) & (section_index <= 2)
            chosen = needs & (leaving[position] == section_index)
            score = jnp.where(chosen, picked - jnp.log(exp_total), 0.0)
            scores = lax.psum(score.reshape(1, 1), "segment")
        keep, send = run_section(
            section, last, own, sib, ranks, order, norm_gain, up_matrix, down_matrix
        )
        both = keep + swapped(send)
        if last:
            rank_here = leaving[own_anchor]
            living = (rank_here == 0) | (rank_here > section)
            summed = jnp.sum(exchanged(jnp.swapaxes(both, 0, 1)).astype(jnp.float32), axis=0)
            before = jnp.where(living, selected.astype(jnp.float32), 0.0)
            final = (before + summed).astype(jnp.bfloat16)
        else:
            rank_here = lax.dynamic_slice(ranks, (y_index * sub, 0), (sub, 1))
            living = (rank_here == 0) | (rank_here > section)
            parts = exchanged(both.reshape(members, sub, cols)).astype(jnp.float32)
            before = jnp.where(living, chunk.astype(jnp.float32), 0.0)
            result = (before + jnp.sum(parts, axis=0)).astype(jnp.bfloat16)
            chunk = lax.ppermute(
                result, "segment", [(i, i + 1) for i in range(section_count - 1)]
            )
    returned = lax.ppermute(selected, "segment", [(i + 1, i) for i in range(section_count - 1)])
    stored = jnp.where(section_index == section_count - 1, final, returned)
    return (stored.reshape(1, 1, 1, width), scores)


def solution(mesh):
    segments, groups, tensors = mesh.devices.shape
    fine = Mesh(
        mesh.devices.reshape(segments, groups, tensors // 2, 2), ("segment", "dp", "y", "core")
    )
    rows = ("dp", "y", "core")
    placed = (
        P(None, rows, None),
        P(),
        P(),
        P(),
        P("segment", None),
        P("segment", rows, None),
        P("segment", rows, None),
        P(),
        P(rows, None),
    )
    return jax.shard_map(
        on_device,
        mesh=fine,
        in_specs=placed,
        out_specs=(P("segment", None, rows, None), P(None, rows)),
        check_vma=False,
    )
```

time: 1050 us -> 256 us (0.24)
  blocking collectives: 716 us -> 88.6 us
  waiting for transfers between devices: 214 us -> 69.8 us
  matrix products: 39.1 us -> 0 us
  starting transfers between devices: 13.6 us -> 39.5 us
  Pallas kernels: 0 us -> 18.4 us
  other arithmetic: 28.8 us -> 12.2 us
    psum x5 -> x1, blocking collectives: 516 us -> 9.74 us  [on_device(): scores = lax.psum(score.reshape(1, 1), 'segment')]
    while x8 -> x0, waiting for transfers between devices: 209 us -> none
    all_gather x4 -> x0, blocking collectives: 200 us -> none  [advance(): gathered = lax.all_gather(own_rows, ('dp', 'tensor'), axis=0, tiled=True)]
    all_to_all x0 -> x4, blocking collectives: none -> 78.8 us  [exchanged(): return lax.all_to_all(value, PLANE, 0, 0, tiled=True)]
    all_to_all x0 -> x4, waiting for transfers between devices: none -> 48.9 us  [exchanged(): return lax.all_to_all(value, PLANE, 0, 0, tiled=True)]
    dot_general x12 -> x0, matrix products: 39.1 us -> none  [the longest x8 23.5 us: contract(): lax.dot_general(left, right, (((1,), (1,)), ((), ())), preferred_element_...]
    all_to_all x0 -> x4, starting transfers between devices: none -> 25 us  [exchanged(): return lax.all_to_all(value, PLANE, 0, 0, tiled=True)]
    pallas_call x0 -> x5, Pallas kernels: none -> 18.4 us  [the longest x4 13.1 us: run_section(): pl.pallas_call(functools.partial(section_kernel, section, last), out_shap...]
  transfers between devices with their start and end apart: 8 -> 16, of which waited for: 8 -> 14; matrix products, arithmetic and copies ran while one was open for 4% -> 4% of each run, Pallas kernels for 0% -> 0%
where the time goes in v1:
time: 256 us; the launch traced here: 254 us
  blocking collectives  88.6 us (35%)
  waiting for transfers between devices  69.8 us (27%)
  starting transfers between devices  39.5 us (15%)
  local copies, waits for them, and re-layouts  18.4 us (7%)
  Pallas kernels  18.4 us (7%)
  other arithmetic  12.2 us (5%)
  between operations  6.85 us (3%)
    all_to_all x4, blocking collectives, exchanged(): return lax.all_to_all(value, PLANE, 0, 0, tiled=True)  78.8 us
    all_to_all x4, waiting for transfers between devices, exchanged(): return lax.all_to_all(value, PLANE, 0, 0, tiled=True)  48.9 us
    all_to_all x4, starting transfers between devices, exchanged(): return lax.all_to_all(value, PLANE, 0, 0, tiled=True)  25 us
    pallas_call x4, Pallas kernels, run_section(): pl.pallas_call(functools.partial(section_kernel, section, last), out_shap...  13.1 us
    ppermute x8, waiting for transfers between devices, swapped(): return lax.ppermute(value, 'core', [(0, 1), (1, 0)])  11.9 us
    ppermute x3, starting transfers between devices, on_device(): lax.ppermute(result, 'segment', [(i, i + 1) for i in range(section_count...  10.2 us
    psum x1, blocking collectives, on_device(): scores = lax.psum(score.reshape(1, 1), 'segment')  9.74 us
    ppermute x3, waiting for transfers between devices, on_device(): lax.ppermute(result, 'segment', [(i, i + 1) for i in range(section_count...  6.51 us
  transfers between devices with their start and end apart: 16, of which 14 were waited for; matrix products, arithmetic and copies ran while one was open for 4% of the time, Pallas kernels for 0%

profile of v1, /device:TPU:2, one launch (start us, length us, event | category | flops | bytes accessed | tf_op | source)
XLA Modules:
  0.0 253.7 jit_solution(10896220209406656835)
XLA Ops:
  2.5 11.6 %all-to-all-start = ((bf16[32,8,896]{2,1,0:T(8,128)(2,1)}), bf16[32,8,896]{2,1,0:T(8,128)(2,1)}, u32[]{:S(2)}, u32[]{:S(2)}) async-start(bf16[32,8,896]{2,1,0:T(8,128)(2,1)} %broadcast_in_dim.75), calls=%async_computation | async-start | bytes 917504 | tf_op jit(solution)/shard_map/all_to_all | solution.py:124
  15.1 15.6 %all-to-all-done = bf16[32,8,896]{2,1,0:T(8,128)(2,1)} async-done(((bf16[32,8,896]{2,1,0:T(8,128)(2,1)}), bf16[32,8,896]{2,1,0:T(8,128)(2,1)}, u32[]{:S(2)}, u32[]{:S(2)}) %all-to-all-start) | async-done | bytes 458784 | tf_op jit(solution)/shard_map/all_to_all | solution.py:124
  30.7 1.8 copy.107
  35.2 1.9 copy-done.1
  37.1 4.1 %section.4 = (bf16[8,32,896]{2,1,0:T(8,128)(2,1)S(1)}, bf16[8,32,896]{2,1,0:T(8,128)(2,1)S(1)}) custom-call(bf16[8,32,896]{2,1,0:T(8,128)(2,1)} %bitcast.37.clone.2.own_ref, bf16[8,32,896]{2,1,0:T(8,128)(2,1)} %collective-permute-done.sib_ref, s32[64,1]{1,0:T(8,128)S(1)} %copy.90.exit_ref, s32[64,1]{1,0:T(8,128)S(1)} %fusion.12.order_ref, ...), custom_call_target="tpu_custom_call" | custom-call | flops 411041792 | bytes 6422528 | tf_op jit(solution)/shard_map/section/pallas_call | solution.py:72
  44.1 4.6 %all-to-all-start.1 = ((bf16[32,8,896]{2,1,0:T(8,128)(2,1)}), bf16[32,8,896]{2,1,0:T(8,128)(2,1)}, u32[]{:S(2)}, u32[]{:S(2)}) async-start(bf16[32,8,896]{2,1,0:T(8,128)(2,1)} %bitcast.62), calls=%async_computation.1 | async-start | bytes 917504 | tf_op jit(solution)/shard_map/all_to_all | solution.py:124
  48.9 17.2 %all-to-all-done.1 = bf16[32,8,896]{2,1,0:T(8,128)(2,1)} async-done(((bf16[32,8,896]{2,1,0:T(8,128)(2,1)}), bf16[32,8,896]{2,1,0:T(8,128)(2,1)}, u32[]{:S(2)}, u32[]{:S(2)}) %all-to-all-start.1) | async-done | bytes 458784 | tf_op jit(solution)/shard_map/all_to_all | solution.py:124
  68.0 3.4 %collective-permute-start.2 = (bf16[8,896]{1,0:T(8,128)(2,1)S(1)}, bf16[8,896]{1,0:T(8,128)(2,1)S(1)}, u32[]{:S(2)}, u32[]{:S(2)}) collective-permute-start(bf16[8,896]{1,0:T(8,128)(2,1)S(1)} %fusion.18), channel_id=1, source_target_pairs={{0,64},{64,128},{128,192},{1,65},{65,129},{129,193},{2,66},{66,130... | collective-permute-start | bytes 43016 | tf_op jit(solution)/shard_map/ppermute | solution.py:237
  71.4 2.2 collective-permute-done.2
  73.6 19.4 %all_to_all.40 = bf16[32,8,896]{2,1,0:T(8,128)(2,1)S(1)} all-to-all(bf16[32,8,896]{2,1,0:T(8,128)(2,1)S(1)} %broadcast_in_dim.78), channel_id=1, replica_groups=mesh['segment'=4,'dp'=8,'y'=4,'core'=2] {'dp','y'}, dimensions={0} | all-to-all | bytes 917504 | tf_op jit(solution)/shard_map/all_to_all | solution.py:124
  93.0 1.8 collective-permute-done.3.sib_ref
  94.8 1.9 copy-done.2
  96.7 2.9 %section.5 = (bf16[8,32,896]{2,1,0:T(8,128)(2,1)S(1)}, bf16[8,32,896]{2,1,0:T(8,128)(2,1)S(1)}) custom-call(bf16[8,32,896]{2,1,0:T(8,128)(2,1)S(1)} %bitcast.55, bf16[8,32,896]{2,1,0:T(8,128)(2,1)S(1)} %collective-permute-done.3.sib_ref, s32[64,1]{1,0:T(8,128)S(1)} %copy.90.exit_ref, s32[64,1]{1,0:T(8,128)S(1)} %fusion.12.order_ref, ...), custom_call_target="tpu_custom_call" | custom-call | flops 411041792 | bytes 6422528 | tf_op jit(solution)/shard_map/section/pallas_call | solution.py:72
  101.7 20.9 %all_to_all.41 = bf16[32,8,896]{2,1,0:T(8,128)(2,1)S(1)} all-to-all(bf16[32,8,896]{2,1,0:T(8,128)(2,1)S(1)} %bitcast.64), channel_id=1, replica_groups=mesh['segment'=4,'dp'=8,'y'=4,'core'=2] {'dp','y'}, dimensions={0} | all-to-all | bytes 917504 | tf_op jit(solution)/shard_map/all_to_all | solution.py:124
  122.7 3.4 %collective-permute-start.5 = (bf16[8,896]{1,0:T(8,128)(2,1)S(1)}, bf16[8,896]{1,0:T(8,128)(2,1)S(1)}, u32[]{:S(2)}, u32[]{:S(2)}) collective-permute-start(bf16[8,896]{1,0:T(8,128)(2,1)S(1)} %add_convert_fusion.2), channel_id=1, source_target_pairs={{0,64},{64,128},{128,192},{1,65},{65,129},{129,193},{2,66},{66,130... | collective-permute-start | bytes 43016 | tf_op jit(solution)/shard_map/ppermute | solution.py:237
  126.1 2.2 collective-permute-done.5
  128.4 19.1 %all_to_all.42 = bf16[32,8,896]{2,1,0:T(8,128)(2,1)S(1)} all-to-all(bf16[32,8,896]{2,1,0:T(8,128)(2,1)S(1)} %broadcast_in_dim.79), channel_id=1, replica_groups=mesh['segment'=4,'dp'=8,'y'=4,'core'=2] {'dp','y'}, dimensions={0} | all-to-all | bytes 917504 | tf_op jit(solution)/shard_map/all_to_all | solution.py:124
  149.3 2.9 %section.6 = (bf16[8,32,896]{2,1,0:T(8,128)(2,1)S(1)}, bf16[8,32,896]{2,1,0:T(8,128)(2,1)S(1)}) custom-call(bf16[8,32,896]{2,1,0:T(8,128)(2,1)S(1)} %bitcast.59, bf16[8,32,896]{2,1,0:T(8,128)(2,1)S(1)} %collective-permute-done.6.sib_ref, s32[64,1]{1,0:T(8,128)S(1)} %copy.90.exit_ref, s32[64,1]{1,0:T(8,128)S(1)} %fusion.12.order_ref, ...), custom_call_target="tpu_custom_call" | custom-call | flops 411041792 | bytes 6422528 | tf_op jit(solution)/shard_map/section/pallas_call | solution.py:72
  155.0 4.6 %all-to-all-start.5 = ((bf16[32,8,896]{2,1,0:T(8,128)(2,1)}), bf16[32,8,896]{2,1,0:T(8,128)(2,1)}, u32[]{:S(2)}, u32[]{:S(2)}) async-start(bf16[32,8,896]{2,1,0:T(8,128)(2,1)} %bitcast.63), calls=%async_computation.5 | async-start | bytes 917504 | tf_op jit(solution)/shard_map/all_to_all | solution.py:124
  160.7 16.1 %all-to-all-done.5 = bf16[32,8,896]{2,1,0:T(8,128)(2,1)} async-done(((bf16[32,8,896]{2,1,0:T(8,128)(2,1)}), bf16[32,8,896]{2,1,0:T(8,128)(2,1)}, u32[]{:S(2)}, u32[]{:S(2)}) %all-to-all-start.5) | async-done | bytes 458784 | tf_op jit(solution)/shard_map/all_to_all | solution.py:124
  177.9 3.4 %collective-permute-start.8 = (bf16[8,896]{1,0:T(8,128)(2,1)S(1)}, bf16[8,896]{1,0:T(8,128)(2,1)S(1)}, u32[]{:S(2)}, u32[]{:S(2)}) collective-permute-start(bf16[8,896]{1,0:T(8,128)(2,1)S(1)} %add_convert_fusion.1), channel_id=1, source_target_pairs={{0,64},{64,128},{128,192},{1,65},{65,129},{129,193},{2,66},{66,130... | collective-permute-start | bytes 43016 | tf_op jit(solution)/shard_map/ppermute | solution.py:237
  181.4 2.1 collective-permute-done.8
  183.5 7.3 %conditional.1 = (bf16[32,8,896]{0,2,1:T(8,128)(2,1)}) conditional(s32[]{:T(128)} %clamp.3, bf16[8,896]{1,0:T(8,128)(2,1)S(1)} %collective-permute-done.8, (bf16[8,32,896]{2,1,0:T(8,128)(2,1)}, bf16[8,32,896]{2,1,0:T(8,128)(2,1)}, s32[64,1]{0,1:T(1,128)S(1)}, f32[1,7168]{1,0:T(1,128)S(1)}, ...), branch_computations={%region_3.4_spmd, %region_4.5_spmd, %region_5.6_spmd, %region_6.7_... | conditional | flops 369526400 | bytes 6198792 | solution.py:198
  183.6 5.3 %exit_head.2 = f32[64,128]{1,0:T(8,128)S(1)} custom-call(bf16[8,32,896]{2,1,0:T(8,128)(2,1)} %get-tuple-element.31.own_ref, bf16[8,32,896]{2,1,0:T(8,128)(2,1)} %get-tuple-element.32.sib_ref, s32[64,1]{1,0:T(8,128)S(1)} %copy.95.wanted_ref, f32[1,7168]{1,0:T(1,128)S(1)} %get-tuple-element.34.gain_ref, bf16[400,7168]{1,0:T(8,128)(2,1)} %get-tuple-element.35.head_ref), custom_call_target="tpu_custom_call" | custom-call | flops 367001600 | bytes 5734400 | tf_op jit(solution)/shard_map/cond/branch_1_fun/exit_head/pallas_call | solution.py:103
  190.8 2.8 %copy.97 = bf16[32,8,896]{2,1,0:T(8,128)(2,1)} copy(bf16[32,8,896]{0,2,1:T(8,128)(2,1)} %get-tuple-element.115) | data formatting | bytes 917504 | tf_op jit(solution)/shard_map/cond | solution.py:198
  193.6 19.5 %all_to_all.43 = bf16[32,8,896]{2,1,0:T(8,128)(2,1)S(1)} all-to-all(bf16[32,8,896]{2,1,0:T(8,128)(2,1)} %copy.97), channel_id=1, replica_groups=mesh['segment'=4,'dp'=8,'y'=4,'core'=2] {'dp','y'}, dimensions={0} | all-to-all | bytes 917504 | tf_op jit(solution)/shard_map/all_to_all | solution.py:124
  214.9 1.9 copy-done.3
  216.9 3.2 %section.7 = (bf16[8,32,896]{2,1,0:T(8,128)(2,1)S(1)}, bf16[8,32,896]{2,1,0:T(8,128)(2,1)S(1)}) custom-call(bf16[8,32,896]{2,1,0:T(8,128)(2,1)S(1)} %bitcast.51, bf16[8,32,896]{2,1,0:T(8,128)(2,1)S(1)} %collective-permute-done.9.sib_ref, s32[64,1]{1,0:T(8,128)S(1)} %copy.90.exit_ref, s32[64,1]{1,0:T(8,128)S(1)} %fusion.12.order_ref, ...), custom_call_target="tpu_custom_call" | custom-call | flops 411041792 | bytes 6422528 | tf_op jit(solution)/shard_map/section/pallas_call | solution.py:72
  222.9 4.2 %all-to-all-start.7 = ((bf16[32,8,896]{2,1,0:T(8,128)(2,1)}), bf16[32,8,896]{2,1,0:T(8,128)(2,1)S(1)}, u32[]{:S(2)}, u32[]{:S(2)}) async-start(bf16[32,8,896]{2,1,0:T(8,128)(2,1)} %copy.99), calls=%async_computation.7 | async-start | bytes 917504 | tf_op jit(solution)/shard_map/all_to_all | solution.py:124
  236.3 9.7 %psum.7 = f32[1,1]{1,0:T(1,128)} all-reduce(f32[1,1]{1,0:T(1,128)} %bitcast.25), channel_id=1, replica_groups=mesh['segment'=4,'dp'=8,'y'=4,'core'=2] {'segment'}, use_global_device_ids=true, to_apply=%region_9.10 | all-reduce | flops 1 | bytes 8 | tf_op jit(solution)/shard_map/psum | solution.py:220
  247.5 3.0 %collective-permute-start.11 = (bf16[8,896]{1,0:T(8,128)(2,1)S(1)}, bf16[8,896]{1,0:T(8,128)(2,1)S(1)}, u32[]{:S(2)}, u32[]{:S(2)}) collective-permute-start(bf16[8,896]{1,0:T(8,128)(2,1)S(1)} %bitcast.67), channel_id=1, source_target_pairs={{64,0},{128,64},{192,128},{65,1},{129,65},{193,129},{66,2},{130,66... | collective-permute-start | bytes 43016 | tf_op jit(solution)/shard_map/ppermute | solution.py:240
  250.6 2.5 collective-permute-done.11
  (96 shorter events, 31.6 us)
Async XLA Ops:
  0.6 33.3 %copy-start.12 = (s32[1,64]{1,0:T(1,128)S(1)}, s32[1,64]{1,0:T(1,128)}, u32[]{:S(2)}) copy-start(s32[1,64]{1,0:T(1,128)} %param.14) | copy-start | bytes 772
  0.6 34.5 %copy-start = (bf16[1,224,7168]{2,1,0:T(8,128)(2,1)S(1)}, bf16[1,224,7168]{2,1,0:T(8,128)(2,1)}, u32[]{:S(2)}) copy-start(bf16[1,224,7168]{2,1,0:T(8,128)(2,1)} %param.18) | copy-start | bytes 9633796
  0.7 34.5 %copy-start.6 = (f32[1,7168]{1,0:T(1,128)S(1)}, f32[1,7168]{1,0:T(1,128)}, u32[]{:S(2)}) copy-start(f32[1,7168]{1,0:T(1,128)} %gain_ref.7) | copy-start | bytes 86020
  2.5 28.2 %all-to-all-start = ((bf16[32,8,896]{2,1,0:T(8,128)(2,1)}), bf16[32,8,896]{2,1,0:T(8,128)(2,1)}, u32[]{:S(2)}, u32[]{:S(2)}) async-start(bf16[32,8,896]{2,1,0:T(8,128)(2,1)} %broadcast_in_dim.75), calls=%async_computation | async-start | bytes 917504 | tf_op jit(solution)/shard_map/all_to_all | solution.py:124
  32.5 2.6 %collective-permute-start = (bf16[8,32,896]{2,1,0:T(8,128)(2,1)}, bf16[8,32,896]{2,1,0:T(8,128)(2,1)}, u32[]{:S(2)}, u32[]{:S(2)}) collective-permute-start(bf16[8,32,896]{2,1,0:T(8,128)(2,1)} %bitcast.37.clone.2.own_ref), channel_id=1, source_target_pairs={{0,1},{1,0},{2,3},{3,2},{4,5},{5,4},{6,7},{7,6},{8,9},{9,8},{10,11... | collective-permute-start | bytes 1376264 | tf_op jit(solution)/shard_map/ppermute | solution.py:120
  35.2 1.9 copy-start.1
  41.2 2.0 collective-permute-start.1
  44.1 22.0 %all-to-all-start.1 = ((bf16[32,8,896]{2,1,0:T(8,128)(2,1)}), bf16[32,8,896]{2,1,0:T(8,128)(2,1)}, u32[]{:S(2)}, u32[]{:S(2)}) async-start(bf16[32,8,896]{2,1,0:T(8,128)(2,1)} %bitcast.62), calls=%async_computation.1 | async-start | bytes 917504 | tf_op jit(solution)/shard_map/all_to_all | solution.py:124
  68.0 5.6 %collective-permute-start.2 = (bf16[8,896]{1,0:T(8,128)(2,1)S(1)}, bf16[8,896]{1,0:T(8,128)(2,1)S(1)}, u32[]{:S(2)}, u32[]{:S(2)}) collective-permute-start(bf16[8,896]{1,0:T(8,128)(2,1)S(1)} %fusion.18), channel_id=1, source_target_pairs={{0,64},{64,128},{128,192},{1,65},{65,129},{129,193},{2,66},{66,130... | collective-permute-start | bytes 43016 | tf_op jit(solution)/shard_map/ppermute | solution.py:237
  93.0 6.7 %copy-start.7 = (bf16[32,8,896]{2,1,0:T(8,128)(2,1)}, bf16[32,8,896]{2,1,0:T(8,128)(2,1)S(1)}, u32[]{:S(2)}) copy-start(bf16[32,8,896]{2,1,0:T(8,128)(2,1)S(1)} %all_to_all.40) | copy-start | bytes 1376260
  93.0 1.8 collective-permute-start.3
  94.8 1.9 copy-start.2
  96.7 2.9 %copy-start.9 = (bf16[8,32,896]{2,1,0:T(8,128)(2,1)}, bf16[8,32,896]{2,1,0:T(8,128)(2,1)S(1)}, u32[]{:S(2)}) copy-start(bf16[8,32,896]{2,1,0:T(8,128)(2,1)S(1)} %collective-permute-done.3.sib_ref) | copy-start | bytes 1376260
  99.7 1.9 collective-permute-start.4
  122.7 5.6 %collective-permute-start.5 = (bf16[8,896]{1,0:T(8,128)(2,1)S(1)}, bf16[8,896]{1,0:T(8,128)(2,1)S(1)}, u32[]{:S(2)}, u32[]{:S(2)}) collective-permute-start(bf16[8,896]{1,0:T(8,128)(2,1)S(1)} %add_convert_fusion.2), channel_id=1, source_target_pairs={{0,64},{64,128},{128,192},{1,65},{65,129},{129,193},{2,66},{66,130... | collective-permute-start | bytes 43016 | tf_op jit(solution)/shard_map/ppermute | solution.py:237
  147.4 4.8 %copy-start.8 = (bf16[32,8,896]{2,1,0:T(8,128)(2,1)}, bf16[32,8,896]{2,1,0:T(8,128)(2,1)S(1)}, u32[]{:S(2)}) copy-start(bf16[32,8,896]{2,1,0:T(8,128)(2,1)S(1)} %all_to_all.42) | copy-start | bytes 1376260
  147.4 1.8 collective-permute-start.6
  149.3 2.9 %copy-start.10 = (bf16[8,32,896]{2,1,0:T(8,128)(2,1)}, bf16[8,32,896]{2,1,0:T(8,128)(2,1)S(1)}, u32[]{:S(2)}) copy-start(bf16[8,32,896]{2,1,0:T(8,128)(2,1)S(1)} %collective-permute-done.6.sib_ref) | copy-start | bytes 1376260
  152.2 7.4 %copy-start.13 = (s32[1,64]{1,0:T(1,128)S(1)}, s32[1,64]{1,0:T(1,128)}, u32[]{:S(2)}) copy-start(s32[1,64]{1,0:T(1,128)} %param.15) | copy-start | bytes 772
  152.2 29.2 %copy-start.11 = (f32[7168]{0:T(1024)S(1)}, f32[7168]{0:T(1024)}, u32[]{:S(2)}) copy-start(f32[7168]{0:T(1024)} %param.20) | copy-start | bytes 86020
  152.2 1.9 collective-permute-start.7
  155.0 21.7 %all-to-all-start.5 = ((bf16[32,8,896]{2,1,0:T(8,128)(2,1)}), bf16[32,8,896]{2,1,0:T(8,128)(2,1)}, u32[]{:S(2)}, u32[]{:S(2)}) async-start(bf16[32,8,896]{2,1,0:T(8,128)(2,1)} %bitcast.63), calls=%async_computation.5 | async-start | bytes 917504 | tf_op jit(solution)/shard_map/all_to_all | solution.py:124
  177.9 5.6 %collective-permute-start.8 = (bf16[8,896]{1,0:T(8,128)(2,1)S(1)}, bf16[8,896]{1,0:T(8,128)(2,1)S(1)}, u32[]{:S(2)}, u32[]{:S(2)}) collective-permute-start(bf16[8,896]{1,0:T(8,128)(2,1)S(1)} %add_convert_fusion.1), channel_id=1, source_target_pairs={{0,64},{64,128},{128,192},{1,65},{65,129},{129,193},{2,66},{66,130... | collective-permute-start | bytes 43016 | tf_op jit(solution)/shard_map/ppermute | solution.py:237
  213.1 6.9 %copy-start.4 = (bf16[32,8,896]{2,1,0:T(8,128)(2,1)}, bf16[32,8,896]{2,1,0:T(8,128)(2,1)S(1)}, u32[]{:S(2)}) copy-start(bf16[32,8,896]{2,1,0:T(8,128)(2,1)S(1)} %all_to_all.43) | copy-start | bytes 1376260
  213.1 1.8 collective-permute-start.9
  214.9 1.9 copy-start.3
  216.8 3.2 %copy-start.5 = (bf16[8,32,896]{2,1,0:T(8,128)(2,1)}, bf16[8,32,896]{2,1,0:T(8,128)(2,1)S(1)}, u32[]{:S(2)}) copy-start(bf16[8,32,896]{2,1,0:T(8,128)(2,1)S(1)} %collective-permute-done.9.sib_ref) | copy-start | bytes 1376260
  220.0 1.9 collective-permute-start.10
  222.9 27.6 %all-to-all-start.7 = ((bf16[32,8,896]{2,1,0:T(8,128)(2,1)}), bf16[32,8,896]{2,1,0:T(8,128)(2,1)S(1)}, u32[]{:S(2)}, u32[]{:S(2)}) async-start(bf16[32,8,896]{2,1,0:T(8,128)(2,1)} %copy.99), calls=%async_computation.7 | async-start | bytes 917504 | tf_op jit(solution)/shard_map/all_to_all | solution.py:124
  247.5 5.6 %collective-permute-start.11 = (bf16[8,896]{1,0:T(8,128)(2,1)S(1)}, bf16[8,896]{1,0:T(8,128)(2,1)S(1)}, u32[]{:S(2)}, u32[]{:S(2)}) collective-permute-start(bf16[8,896]{1,0:T(8,128)(2,1)S(1)} %bitcast.67), channel_id=1, source_target_pairs={{64,0},{128,64},{192,128},{65,1},{129,65},{193,129},{66,2},{130,66... | collective-permute-start | bytes 43016 | tf_op jit(solution)/shard_map/ppermute | solution.py:240

commit v2 on v0

v2 whole, which is shorter than its diff:
```python
import functools

import jax
import jax.numpy as jnp
from jax import lax
from jax.experimental import pallas as pl
from jax.experimental.pallas import tpu as pltpu
from jax.sharding import Mesh, PartitionSpec as P

EPSILON = 1e-05
SQRT_HALF = 0.7071067811865476
VMEM_LIMIT = 16 * 1024 * 1024
SMALL_LIMIT = 4 * 1024 * 1024
PLANE = ("dp", "y")
NT = (((1,), (1,)), ((), ()))
VMEM = pl.BlockSpec(memory_space=pltpu.VMEM)
SMEM = pl.BlockSpec(memory_space=pltpu.SMEM)
ANY = pl.BlockSpec(memory_space=pl.ANY)
SMALL = pltpu.CompilerParams(vmem_limit_bytes=SMALL_LIMIT)


def prepare_kernel(
    exit_ref, target_ref, repack_ref, rank_ref, chunk_rank_ref, order_ref, wanted_ref, pick_ref, flag_ref
):
    half = rank_ref.shape[0]
    sub = chunk_rank_ref.shape[0]
    segment = lax.axis_index("segment")
    core = lax.axis_index("core")
    place = lax.axis_index("dp") * lax.axis_size("y") + lax.axis_index("y")
    first_row = lax.axis_index("y") * sub
    line = lax.broadcasted_iota(jnp.int32, (half, 1), 0)
    ranks = jnp.zeros((half, 1), jnp.int32)
    orders, wanteds = ranks, ranks
    for i in range(half):
        row = 2 * i + core
        anchor = repack_ref[0, 0, repack_ref[0, 1, row]]
        slot = anchor // 2 + jnp.where(anchor % 2 == core, 0, half)
        ranks = jnp.where(line == i, exit_ref[0, row], ranks)
        orders = jnp.where(line == i, slot, orders)
        wanteds = jnp.where(line == i, target_ref[0, row], wanteds)
    rank_ref[...] = ranks
    order_ref[...] = orders
    wanted_ref[...] = wanteds
    line = lax.broadcasted_iota(jnp.int32, (sub, 1), 0)
    ranks = jnp.zeros((sub, 1), jnp.int32)
    for i in range(sub):
        ranks = jnp.where(line == i, exit_ref[0, 2 * (first_row + i) + core], ranks)
    chunk_rank_ref[...] = ranks

    def anchor_of(position):
        first = repack_ref[0, 0, position]
        second = repack_ref[0, 0, repack_ref[0, 1, position]]
        return jnp.where(segment == 3, second, jnp.where(segment == 2, first, position))

    position = 2 * place + core
    mine = anchor_of(position)
    other = anchor_of(2 * place + 1 - core)
    lanes = lax.broadcasted_iota(jnp.int32, pick_ref.shape, 1)
    lines = lax.broadcasted_iota(jnp.int32, pick_ref.shape, 0)
    pick_ref[...] = (
        ((lines == 0) & (lanes == mine // 2)) | ((lines == 1) & (lanes == other // 2))
    ).astype(jnp.float32)
    chosen = (segment >= 1) & (segment <= 2) & (exit_ref[0, position] == segment)
    rank = exit_ref[0, mine]
    living = (rank == 0) | (rank > 3)
    lines = lax.broadcasted_iota(jnp.int32, flag_ref.shape, 0)
    flag_ref[...] = (
        ((lines == 0) & (mine % 2 == core)) | ((lines == 1) & chosen) | ((lines == 2) & living)
    ).astype(jnp.float32)


def prepare(exit_at, targets, repack, half, sub):
    column = jax.ShapeDtypeStruct((half, 1), jnp.int32)
    return pl.pallas_call(
        prepare_kernel,
        out_shape=(
            column,
            jax.ShapeDtypeStruct((sub, 1), jnp.int32),
            column,
            column,
            jax.ShapeDtypeStruct((8, half), jnp.float32),
            jax.ShapeDtypeStruct((8, 128), jnp.float32),
        ),
        in_specs=[SMEM] * 3,
        out_specs=(VMEM,) * 6,
        compiler_params=SMALL,
        name="prepare",
    )(exit_at, targets, repack)


def load_kernel(*refs):
    count = (len(refs) - 1) // 2
    sems = refs[-1]
    copies = [
        pltpu.make_async_copy(refs[i], refs[count + i], sems.at[i]) for i in range(count)
    ]
    for copy in copies:
        copy.start()
    for copy in copies:
        copy.wait()


def load(*arrays):
    return pl.pallas_call(
        load_kernel,
        out_shape=tuple(jax.ShapeDtypeStruct(a.shape, a.dtype) for a in arrays),
        in_specs=[ANY] * len(arrays),
        out_specs=(VMEM,) * len(arrays),
        scratch_shapes=[pltpu.SemaphoreType.DMA((len(arrays),))],
        compiler_params=SMALL,
        name="load",
    )(*arrays)


def normalise(rows_ref, gain_ref, living, out_ref):
    blocks, _, cols = rows_ref.shape
    width = blocks * cols

    def block(b):
        values = rows_ref[b].astype(jnp.float32)
        return values if living is None else jnp.where(living, values, 0.0)

    total = block(0)
    for b in range(1, blocks):
        total += block(b)
    mean = jnp.sum(total, axis=1, keepdims=True) / width
    total = jnp.zeros_like(total)
    for b in range(blocks):
        center = block(b) - mean
        total += center * center
    scale = lax.rsqrt(jnp.sum(total, axis=1, keepdims=True) / width + EPSILON)
    for b in range(blocks):
        lanes = slice(b * cols, (b + 1) * cols)
        normed = (block(b) - mean) * scale * gain_ref[:, lanes]
        out_ref[:, lanes] = normed.astype(jnp.bfloat16)


def hidden_of(normed, up_ref):
    pre = lax.dot_general(normed, up_ref[...], NT, preferred_element_type=jnp.float32)
    return (0.5 * pre * (1.0 + lax.erf(pre * SQRT_HALF))).astype(jnp.bfloat16)


def project(hidden_a, hidden_b, down_a_ref, down_b_ref, out_ref, step=2):
    blocks, _, cols = out_ref.shape
    for b in range(0, blocks, step):
        lanes = slice(b * cols, (b + step) * cols)
        part = jnp.dot(hidden_a, down_a_ref[:, lanes], preferred_element_type=jnp.float32)
        part += jnp.dot(hidden_b, down_b_ref[:, lanes], preferred_element_type=jnp.float32)
        part = part.astype(jnp.bfloat16)
        for k in range(step):
            out_ref[b + k] = part[:, k * cols : (k + 1) * cols]


def pick_rows(section, rows_ref, pick_ref, before_ref, picked_ref):
    here = lax.axis_index("segment") == section

    @pl.when(here)
    def _():
        pick = pick_ref[...].astype(jnp.bfloat16)
        for b in range(rows_ref.shape[0]):
            picked_ref[b] = jnp.dot(
                pick, rows_ref[b], preferred_element_type=jnp.float32
            ).astype(jnp.bfloat16)

    @pl.when(jnp.logical_not(here))
    def _():
        picked_ref[...] = before_ref[...]


def living_at(section, rank_ref):
    rank = rank_ref[...]
    return (rank == 0) | (rank > section)


def section_kernel(
    section, rows_ref, rank_ref, gain_ref, pick_ref, before_ref,
    up_a_ref, up_b_ref, down_a_ref, down_b_ref, out_ref, picked_ref, normed_ref
):
    normalise(rows_ref, gain_ref, living_at(section, rank_ref), normed_ref)
    normed = normed_ref[...]
    hidden_a = hidden_of(normed, up_a_ref)
    hidden_b = hidden_of(normed, up_b_ref)
    project(hidden_a, hidden_b, down_a_ref, down_b_ref, out_ref)
    pick_rows(section, rows_ref, pick_ref, before_ref, picked_ref)


def run_section(section, rows, ranks, gain, pick, before, weights):
    blocks, half, cols = rows.shape
    block = jax.ShapeDtypeStruct(rows.shape, jnp.bfloat16)
    hidden = 2 * weights[0].shape[0]
    return pl.pallas_call(
        functools.partial(section_kernel, section),
        out_shape=(block, jax.ShapeDtypeStruct(before.shape, jnp.bfloat16)),
        in_specs=[VMEM] * 9,
        out_specs=(VMEM, VMEM),
        scratch_shapes=[pltpu.VMEM((half, blocks * cols), jnp.bfloat16)],
        compiler_params=SMALL,
        cost_estimate=pl.CostEstimate(
            flops=4 * half * blocks * cols * hidden,
            bytes_accessed=4 * hidden * blocks * cols,
            transcendentals=half * hidden,
        ),
        name="section",
    )(rows, ranks, gain, pick, before, *weights)


def settle_kernel(section, parts_ref, chunk_ref, rank_ref, out_ref):
    total = jnp.where(living_at(section, rank_ref), chunk_ref[...].astype(jnp.float32), 0.0)
    summed = parts_ref[0].astype(jnp.float32)
    for k in range(1, parts_ref.shape[0]):
        summed += parts_ref[k].astype(jnp.float32)
    out_ref[...] = (total + summed).astype(jnp.bfloat16)


def settle(section, parts, chunk, chunk_ranks):
    return pl.pallas_call(
        functools.partial(settle_kernel, section),
        out_shape=jax.ShapeDtypeStruct(chunk.shape, jnp.bfloat16),
        in_specs=[VMEM] * 3,
        out_specs=VMEM,
        compiler_params=SMALL,
        name="settle",
    )(parts, chunk, chunk_ranks)


def spread_kernel(chunk_ref, out_ref):
    chunk = chunk_ref[...]
    for k in range(out_ref.shape[0]):
        out_ref[k] = chunk


def spread(members, chunk):
    return pl.pallas_call(
        spread_kernel,
        out_shape=jax.ShapeDtypeStruct((members, *chunk.shape), jnp.bfloat16),
        in_specs=[VMEM],
        out_specs=VMEM,
        compiler_params=SMALL,
        name="spread",
    )(chunk)


def last_up_kernel(
    section, rows_ref, rank_ref, gain_ref, pick_ref, before_ref, flag_ref,
    up_a_ref, up_b_ref, hidden_ref, picked_ref, score_ref, normed_ref
):
    blocks, half, _ = rows_ref.shape
    sub = half * blocks // (half * blocks // 8)
    normalise(rows_ref, gain_ref, living_at(section, rank_ref), normed_ref)
    normed = normed_ref[...]
    hidden_ref[0] = hidden_of(normed, up_a_ref)
    hidden_ref[1] = hidden_of(normed, up_b_ref)
    pick_rows(section, rows_ref, pick_ref, before_ref, picked_ref)
    sums = jnp.zeros((sub, 128), jnp.float32)
    for b in range(blocks):
        for r in range(0, half, sub):
            sums += rows_ref[b, r : r + sub, :128].astype(jnp.float32)
    exp_total = sums[0:1, 0:1] + sums[0:1, 2:3]
    picked = sums[0:1, 1:2] + sums[0:1, 3:4]
    score = jnp.where(flag_ref[1:2, 0:1] > 0.0, picked - jnp.log(exp_total), 0.0)
    score_ref[...] = jnp.broadcast_to(score, score_ref.shape)


def run_last_up(section, rows, ranks, gain, pick, before, flags, up_a, up_b):
    blocks, half, cols = rows.shape
    hidden = up_a.shape[0]
    return pl.pallas_call(
        functools.partial(last_up_kernel, section),
        out_shape=(
            jax.ShapeDtypeStruct((2, half, hidden), jnp.bfloat16),
            jax.ShapeDtypeStruct(before.shape, jnp.bfloat16),
            jax.ShapeDtypeStruct((8, 128), jnp.float32),
        ),
        in_specs=[VMEM] * 8,
        out_specs=(VMEM,) * 3,
        scratch_shapes=[pltpu.VMEM((half, blocks * cols), jnp.bfloat16)],
        compiler_params=SMALL,
        cost_estimate=pl.CostEstimate(
            flops=4 * half * blocks * cols * hidden,
            bytes_accessed=4 * hidden * blocks * cols,
            transcendentals=2 * half * hidden,
        ),
        name="last_up",
    )(rows, ranks, gain, pick, before, flags, up_a, up_b)


def last_down_kernel(own_ref, sib_ref, order_ref, down_a_ref, down_b_ref, out_ref):
    half = own_ref.shape[1]
    slots = lax.broadcasted_iota(jnp.int32, (half, half), 1)
    order = order_ref[...]
    from_own = jnp.where(order == slots, 1.0, 0.0).astype(jnp.bfloat16)
    from_sib = jnp.where(order == slots + half, 1.0, 0.0).astype(jnp.bfloat16)

    def chosen(own, sib):
        rows = jnp.dot(from_own, own, preferred_element_type=jnp.float32)
        rows += jnp.dot(from_sib, sib, preferred_element_type=jnp.float32)
        return rows.astype(jnp.bfloat16)

    hidden_a = chosen(own_ref[0], sib_ref[1])
    hidden_b = chosen(own_ref[1], sib_ref[0])
    project(hidden_a, hidden_b, down_a_ref, down_b_ref, out_ref)


def run_last_down(shape, own, sib, order, down_a, down_b):
    blocks, half, cols = shape
    hidden = down_a.shape[0]
    return pl.pallas_call(
        last_down_kernel,
        out_shape=jax.ShapeDtypeStruct(shape, jnp.bfloat16),
        in_specs=[VMEM] * 5,
        out_specs=VMEM,
        compiler_params=SMALL,
        cost_estimate=pl.CostEstimate(
            flops=4 * half * blocks * cols * hidden,
            bytes_accessed=4 * hidden * blocks * cols,
            transcendentals=0,
        ),
        name="last_down",
    )(own, sib, order, down_a, down_b)


def payload_kernel(
    chunk_ref, first_ref, second_ref, wanted_ref, gain_ref, head_a_ref, head_b_ref, out_ref,
    rows_ref, normed_ref, a_ref, b_ref, sems
):
    members = out_ref.shape[0]
    segment = lax.axis_index("segment")
    core = lax.axis_index("core")
    place = lax.axis_index("dp") * lax.axis_size("y") + lax.axis_index("y")
    scoring = (segment >= 1) & (segment <= 2)

    @pl.when(jnp.logical_not(scoring))
    def _():
        chunk = chunk_ref[...]
        for k in range(members):
            out_ref[k] = chunk

    @pl.when(scoring)
    def _():
        copy_a = pltpu.make_async_copy(head_a_ref, a_ref, sems.at[0])
        copy_b = pltpu.make_async_copy(head_b_ref, b_ref, sems.at[1])
        copy_a.start()
        copy_b.start()

        @pl.when(segment == 1)
        def _():
            copy = pltpu.make_async_copy(first_ref, rows_ref, sems.at[2])
            copy.start()
            copy.wait()

        @pl.when(segment == 2)
        def _():
            copy = pltpu.make_async_copy(second_ref, rows_ref, sems.at[2])
            copy.start()
            copy.wait()

        normalise(rows_ref, gain_ref, None, normed_ref)
        normed = normed_ref[...]
        half, vocab = normed.shape[0], a_ref.shape[0]
        wanted = wanted_ref[...]
        exp_part = jnp.zeros((half, 1), jnp.float32)
        picked = jnp.zeros((half, 1), jnp.float32)
        for copy, ref, shard in (
            (copy_a, a_ref, 2 * place + core),
            (copy_b, b_ref, 2 * place + 1 - core),
        ):
            copy.wait()
            logits = lax.dot_general(normed, ref[...], NT, preferred_element_type=jnp.float32)
            exp_part += jnp.sum(jnp.exp(logits), axis=1, keepdims=True)
            columns = lax.broadcasted_iota(jnp.int32, logits.shape, 1) + shard * vocab
            picked += jnp.sum(jnp.where(columns == wanted, logits, 0.0), axis=1, keepdims=True)
        lane = lax.broadcasted_iota(jnp.int32, (half, 128), 1)
        both = jnp.where(lane % 2 == 0, exp_part, picked)
        high = both.astype(jnp.bfloat16).astype(jnp.float32)
        stats = jnp.where(lane < 2, high, jnp.where(lane < 4, both - high, 0.0))
        out_ref[...] = jnp.zeros_like(out_ref)
        top = lax.broadcasted_iota(jnp.int32, (out_ref.shape[1], 128), 0) == 0
        for k in range(members):
            out_ref[k, :, :128] = jnp.where(top, stats[k : k + 1], 0.0).astype(jnp.bfloat16)


def run_payload(members, chunk, first, second, wanted, gain, head_a, head_b):
    blocks, half, cols = first.shape
    return pl.pallas_call(
        payload_kernel,
        out_shape=jax.ShapeDtypeStruct((members, *chunk.shape), jnp.bfloat16),
        in_specs=[VMEM, ANY, ANY, VMEM, VMEM, ANY, ANY],
        out_specs=VMEM,
        scratch_shapes=[
            pltpu.VMEM(first.shape, jnp.bfloat16),
            pltpu.VMEM((half, blocks * cols), jnp.bfloat16),
            pltpu.VMEM(head_a.shape, jnp.bfloat16),
            pltpu.VMEM(head_b.shape, jnp.bfloat16),
            pltpu.SemaphoreType.DMA((3,)),
        ],
        compiler_params=pltpu.CompilerParams(vmem_limit_bytes=VMEM_LIMIT),
        name="payload",
    )(chunk, first, second, wanted, gain, head_a, head_b)


def swapped(value):
    return lax.ppermute(value, "core", [(0, 1), (1, 0)])


def exchanged(value):
    return lax.all_to_all(value, PLANE, 0, 0, tiled=True)


def on_device(inputs, exit_at, targets, repack, norm_gain, up_weight, down_weight, exit_gain, head):
    section_index = lax.axis_index("segment")
    section_count = lax.axis_size("segment")
    z_index = lax.axis_index("dp")
    y_index = lax.axis_index("y")
    blocks = lax.axis_size("dp")
    y_count = lax.axis_size("y")
    members = blocks * y_count
    width = inputs.shape[2]
    cols = width // blocks
    half = exit_at.shape[1] // 2
    sub = half // y_count
    up_a, down_a = up_weight[0], down_weight[0]
    up_b, down_b = swapped(up_a), swapped(down_a)

    def hop(value, step):
        pairs = [(i, (i + step) % section_count) for i in range(section_count)]
        return lax.ppermute(value, "segment", pairs)

    mine = inputs[0].reshape(blocks, cols)
    rows = jnp.swapaxes(exchanged(spread(members, mine)), 0, 1)
    ranks, chunk_ranks, order, wanted, pick, flags = prepare(exit_at, targets, repack, half, sub)
    chunk = lax.dynamic_slice(rows, (z_index, y_index * sub, 0), (1, sub, cols))[0]
    rows, chunk, up_a, up_b, down_a, down_b = lax.optimization_barrier(
        (rows, chunk, up_a, up_b, down_a, down_b)
    )
    up_a, up_b, down_a, down_b = load(up_a, up_b, down_a, down_b)
    weights = (up_a, up_b, down_a, down_b)
    picked = jnp.zeros((blocks, 8, cols), jnp.bfloat16)
    kept = []
    for section in range(3):
        if section:
            rows = exchanged(spread(members, chunk)).reshape(blocks, half, cols)
            kept.append(rows)
        parts, picked = run_section(section, rows, ranks, norm_gain, pick, picked, weights)
        parts = exchanged(parts.reshape(members, sub, cols))
        chunk = hop(settle(section, parts, chunk, chunk_ranks), 1)
    head_sib = swapped(head)
    payload = run_payload(members, chunk, *kept, wanted, exit_gain[None, :], head, head_sib)
    rows = exchanged(payload).reshape(blocks, half, cols)
    hidden, picked, score = run_last_up(
        3, rows, ranks, norm_gain, pick, picked, flags, up_a, up_b
    )
    parts = run_last_down(rows.shape, hidden, swapped(hidden), order, down_a, down_b)
    parts = exchanged(jnp.swapaxes(parts, 0, 1)).astype(jnp.float32)
    score = score[:1, :1]
    scores = score + hop(score, 1) + hop(score, 2) + hop(score, 3)
    selected = jnp.where(flags[0:1, 0:1] > 0, picked[:, 0], swapped(picked[:, 1]))
    returned = hop(selected, -1)
    before = jnp.where(flags[2:3, 0:1] > 0, selected.astype(jnp.float32), 0.0)
    final = (before + jnp.sum(parts, axis=0)).astype(jnp.bfloat16)
    stored = jnp.where(section_index == section_count - 1, final, returned)
    return (stored.reshape(1, 1, 1, width), scores)


def solution(mesh):
    segments, groups, tensors = mesh.devices.shape
    fine = Mesh(
        mesh.devices.reshape(segments, groups, tensors // 2, 2), ("segment", "dp", "y", "core")
    )
    rows = ("dp", "y", "core")
    placed = (
        P(None, rows, None),
        P(),
        P(),
        P(),
        P("segment", None),
        P("segment", rows, None),
        P("segment", rows, None),
        P(),
        P(rows, None),
    )
    return jax.shard_map(
        on_device,
        mesh=fine,
        in_specs=placed,
        out_specs=(P("segment", None, rows, None), P(None, rows)),
        check_vma=False,
    )
```

time: 1050 us -> 208 us (0.20)
  blocking collectives: 716 us -> 109 us
  waiting for transfers between devices: 214 us -> 30.9 us
  matrix products: 39.1 us -> 0 us
  other arithmetic: 28.8 us -> 0.93 us
  Pallas kernels: 0 us -> 25.2 us
  local copies, waits for them, and re-layouts: 23.1 us -> 10.3 us
  starting transfers between devices: 13.6 us -> 25.4 us
    psum x5 -> x0, blocking collectives: 516 us -> none  [the longest x4 507 us: advance(): exp_total, picked = lax.psum((exp_total, picked), ('dp', 'tensor'))]
    while x8 -> x0, waiting for transfers between devices: 209 us -> none
    all_gather x4 -> x0, blocking collectives: 200 us -> none  [advance(): gathered = lax.all_gather(own_rows, ('dp', 'tensor'), axis=0, tiled=True)]
    all_to_all x0 -> x6, blocking collectives: none -> 109 us  [exchanged(): return lax.all_to_all(value, PLANE, 0, 0, tiled=True)]
    dot_general x12 -> x0, matrix products: 39.1 us -> none  [the longest x8 23.5 us: contract(): lax.dot_general(left, right, (((1,), (1,)), ((), ())), preferred_element_...]
    pallas_call x0 -> x14, Pallas kernels: none -> 25.2 us  [the longest x3 11.2 us: run_section(): pl.pallas_call(functools.partial(section_kernel, section), out_shape=(blo...]
    all_to_all x0 -> x2, waiting for transfers between devices: none -> 20 us  [exchanged(): return lax.all_to_all(value, PLANE, 0, 0, tiled=True)]
    all_to_all x0 -> x2, starting transfers between devices: none -> 15.8 us  [exchanged(): return lax.all_to_all(value, PLANE, 0, 0, tiled=True)]
  transfers between devices with their start and end apart: 8 -> 14, of which waited for: 8 -> 8; matrix products, arithmetic and copies ran while one was open for 4% -> 2% of each run, Pallas kernels for 0% -> 7%
where the time goes in v2:
time: 208 us; the launch traced here: 207 us
  blocking collectives  109 us (52%)
  waiting for transfers between devices  30.9 us (15%)
  starting transfers between devices  25.4 us (12%)
  Pallas kernels  25.2 us (12%)
  local copies, waits for them, and re-layouts  10.3 us (5%)
  between operations  5.79 us (3%)
    all_to_all x6, blocking collectives, exchanged(): return lax.all_to_all(value, PLANE, 0, 0, tiled=True)  109 us
    all_to_all x2, waiting for transfers between devices, exchanged(): return lax.all_to_all(value, PLANE, 0, 0, tiled=True)  20 us
    all_to_all x2, starting transfers between devices, exchanged(): return lax.all_to_all(value, PLANE, 0, 0, tiled=True)  15.8 us
    pallas_call x3, Pallas kernels, run_section(): pl.pallas_call(functools.partial(section_kernel, section), out_shape=(blo...  11.2 us
    ppermute x7, waiting for transfers between devices, hop(): return lax.ppermute(value, 'segment', pairs)  9.68 us
    ppermute x7, starting transfers between devices, hop(): return lax.ppermute(value, 'segment', pairs)  8.68 us
    unnamed x21, local copies, waits for them, and re-layouts  6.58 us
    pallas_call x1, Pallas kernels, run_payload(): pl.pallas_call(payload_kernel, out_shape=jax.ShapeDtypeStruct((members, *...  5.72 us
  transfers between devices with their start and end apart: 14, of which 8 were waited for; matrix products, arithmetic and copies ran while one was open for 2% of the time, Pallas kernels for 7%

profile of v2, /device:TPU:2, one launch (start us, length us, event | category | flops | bytes accessed | tf_op | source)
XLA Modules:
  0.0 207.1 jit_solution(9295504861912903153)
XLA Ops:
  3.0 11.6 %all-to-all-start = ((bf16[32,8,896]{2,1,0:T(8,128)(2,1)}), bf16[32,8,896]{2,1,0:T(8,128)(2,1)}, u32[]{:S(2)}, u32[]{:S(2)}) async-start(bf16[32,8,896]{2,1,0:T(8,128)(2,1)} %copy-done.2), calls=%async_computation | async-start | bytes 917504 | tf_op jit(solution)/shard_map/all_to_all | solution.py:406
  16.6 0.9 prepare.1
  17.6 14.1 %all-to-all-done = bf16[32,8,896]{2,1,0:T(8,128)(2,1)} async-done(((bf16[32,8,896]{2,1,0:T(8,128)(2,1)}), bf16[32,8,896]{2,1,0:T(8,128)(2,1)}, u32[]{:S(2)}, u32[]{:S(2)}) %all-to-all-start) | async-done | bytes 458784 | tf_op jit(solution)/shard_map/all_to_all | solution.py:406
  31.7 1.1 copy.27
  32.8 1.9 copy-done
  34.7 1.9 copy-done.1
  36.7 2.8 %load.1 = (bf16[224,7168]{1,0:T(8,128)(2,1)S(1)}, bf16[224,7168]{1,0:T(8,128)(2,1)S(1)}, bf16[224,7168]{1,0:T(8,128)(2,1)S(1)}, bf16[224,7168]{1,0:T(8,128)(2,1)S(1)}) custom-call(bf16[224,7168]{1,0:T(8,128)(2,1)S(1)} %bitcast.28, bf16[224,7168]{1,0:T(8,128)(2,1)S(1)} %collective-permute-done.refs_1_, bf16[224,7168]{1,0:T(8,128)(2,1)S(1)} %bitcast.30, ...), custom_call_target="tpu_custom_call" | custom-call | tf_op jit(solution)/shard_map/load/pallas_call | solution.py:104
  39.5 3.7 %section.3 = (bf16[8,32,896]{2,1,0:T(8,128)(2,1)S(1)}, bf16[8,8,896]{2,1,0:T(8,128)(2,1)S(1)}) custom-call(bf16[8,32,896]{2,1,0:T(8,128)(2,1)S(1)} %bitcast.31, s32[32,1]{1,0:T(8,128)S(1)} %get-tuple-element.29.rank_ref, f32[1,7168]{1,0:T(1,128)S(1)} %copy-done.3, f32[8,32]{1,0:T(8,128)S(1)} %get-tuple-element.30.pick_ref, ...), custom_call_target="tpu_custom_call" | custom-call | flops 411041792 | bytes 12845056 | tf_op jit(solution)/shard_map/section/pallas_call | solution.py:191
  43.2 20.2 %all_to_all.40.parts_ref = bf16[32,8,896]{2,1,0:T(8,128)(2,1)S(1)} all-to-all(bf16[32,8,896]{2,1,0:T(8,128)(2,1)S(1)} %bitcast.34), channel_id=1, replica_groups=mesh['segment'=4,'dp'=8,'y'=4,'core'=2] {'dp','y'}, dimensions={0} | all-to-all | bytes 917504 | tf_op jit(solution)/shard_map/all_to_all | solution.py:406
  63.5 1.6 collective-permute-start.2
  65.0 2.2 %collective-permute-done.2.chunk_ref = bf16[8,896]{1,0:T(8,128)(2,1)S(1)} collective-permute-done((bf16[8,896]{1,0:T(8,128)(2,1)S(1)}, bf16[8,896]{1,0:T(8,128)(2,1)S(1)}, u32[]{:S(2)}, u32[]{:S(2)}) %collective-permute-start.2) | collective-permute-done | bytes 14368 | tf_op jit(solution)/shard_map/ppermute | solution.py:426
  67.3 18.8 %all_to_all.41 = bf16[32,8,896]{2,1,0:T(8,128)(2,1)S(1)} all-to-all(bf16[32,8,896]{2,1,0:T(8,128)(2,1)S(1)} %spread.4), channel_id=1, replica_groups=mesh['segment'=4,'dp'=8,'y'=4,'core'=2] {'dp','y'}, dimensions={0} | all-to-all | bytes 917504 | tf_op jit(solution)/shard_map/all_to_all | solution.py:406
  86.1 3.9 %section.4 = (bf16[8,32,896]{2,1,0:T(8,128)(2,1)S(1)}, bf16[8,8,896]{2,1,0:T(8,128)(2,1)S(1)}) custom-call(bf16[8,32,896]{2,1,0:T(8,128)(2,1)S(1)} %bitcast.23, s32[32,1]{1,0:T(8,128)S(1)} %get-tuple-element.29.rank_ref, f32[1,7168]{1,0:T(1,128)S(1)} %copy-done.3, f32[8,32]{1,0:T(8,128)S(1)} %get-tuple-element.30.pick_ref, ...), custom_call_target="tpu_custom_call" | custom-call | flops 411041792 | bytes 12845056 | tf_op jit(solution)/shard_map/section/pallas_call | solution.py:191
  90.0 18.3 %all_to_all.42.parts_ref = bf16[32,8,896]{2,1,0:T(8,128)(2,1)S(1)} all-to-all(bf16[32,8,896]{2,1,0:T(8,128)(2,1)S(1)} %bitcast.35), channel_id=1, replica_groups=mesh['segment'=4,'dp'=8,'y'=4,'core'=2] {'dp','y'}, dimensions={0} | all-to-all | bytes 917504 | tf_op jit(solution)/shard_map/all_to_all | solution.py:406
  108.3 1.4 collective-permute-start.3
  109.7 2.4 %collective-permute-done.3.chunk_ref = bf16[8,896]{1,0:T(8,128)(2,1)S(1)} collective-permute-done((bf16[8,896]{1,0:T(8,128)(2,1)S(1)}, bf16[8,896]{1,0:T(8,128)(2,1)S(1)}, u32[]{:S(2)}, u32[]{:S(2)}) %collective-permute-start.3) | collective-permute-done | bytes 14368 | tf_op jit(solution)/shard_map/ppermute | solution.py:426
  112.2 17.2 %all_to_all.43 = bf16[32,8,896]{2,1,0:T(8,128)(2,1)S(1)} all-to-all(bf16[32,8,896]{2,1,0:T(8,128)(2,1)S(1)} %spread.5), channel_id=1, replica_groups=mesh['segment'=4,'dp'=8,'y'=4,'core'=2] {'dp','y'}, dimensions={0} | all-to-all | bytes 917504 | tf_op jit(solution)/shard_map/all_to_all | solution.py:406
  129.4 3.7 %section.5 = (bf16[8,32,896]{2,1,0:T(8,128)(2,1)S(1)}, bf16[8,8,896]{2,1,0:T(8,128)(2,1)S(1)}) custom-call(bf16[8,32,896]{2,1,0:T(8,128)(2,1)S(1)} %bitcast.25, s32[32,1]{1,0:T(8,128)S(1)} %get-tuple-element.29.rank_ref, f32[1,7168]{1,0:T(1,128)S(1)} %copy-done.3, f32[8,32]{1,0:T(8,128)S(1)} %get-tuple-element.30.pick_ref, ...), custom_call_target="tpu_custom_call" | custom-call | flops 411041792 | bytes 12845056 | tf_op jit(solution)/shard_map/section/pallas_call | solution.py:191
  133.1 17.0 %all_to_all.44.parts_ref = bf16[32,8,896]{2,1,0:T(8,128)(2,1)S(1)} all-to-all(bf16[32,8,896]{2,1,0:T(8,128)(2,1)S(1)} %bitcast.36), channel_id=1, replica_groups=mesh['segment'=4,'dp'=8,'y'=4,'core'=2] {'dp','y'}, dimensions={0} | all-to-all | bytes 917504 | tf_op jit(solution)/shard_map/all_to_all | solution.py:406
  150.1 1.6 collective-permute-start.4
  151.7 3.2 %collective-permute-done.4.chunk_ref = bf16[8,896]{1,0:T(8,128)(2,1)S(1)} collective-permute-done((bf16[8,896]{1,0:T(8,128)(2,1)S(1)}, bf16[8,896]{1,0:T(8,128)(2,1)S(1)}, u32[]{:S(2)}, u32[]{:S(2)}) %collective-permute-start.4) | collective-permute-done | bytes 14368 | tf_op jit(solution)/shard_map/ppermute | solution.py:426
  154.8 5.7 %payload.1 = bf16[32,8,896]{2,1,0:T(8,128)(2,1)S(1)} custom-call(bf16[8,896]{1,0:T(8,128)(2,1)S(1)} %collective-permute-done.4.chunk_ref, bf16[8,32,896]{2,1,0:T(8,128)(2,1)S(1)} %bitcast.24, bf16[8,32,896]{2,1,0:T(8,128)(2,1)S(1)} %bitcast.26, s32[32,1]{1,0:T(8,128)S(1)} %get-tuple-element.46.wanted_ref, f32[1,7168]{1,0:T(1,128)S(1)} %bitcast.37, ...), custom_call_target="tpu_custom_call" | custom-call | tf_op jit(solution)/shard_map/payload/pallas_call | solution.py:384
  160.6 17.1 %all_to_all.45 = bf16[32,8,896]{2,1,0:T(8,128)(2,1)S(1)} all-to-all(bf16[32,8,896]{2,1,0:T(8,128)(2,1)S(1)} %payload.1), channel_id=1, replica_groups=mesh['segment'=4,'dp'=8,'y'=4,'core'=2] {'dp','y'}, dimensions={0} | all-to-all | bytes 917504 | tf_op jit(solution)/shard_map/all_to_all | solution.py:406
  177.7 2.7 %last_up.1 = (bf16[2,32,224]{2,1,0:T(8,128)(2,1)S(1)}, bf16[8,8,896]{2,1,0:T(8,128)(2,1)S(1)}, f32[8,128]{1,0:T(8,128)S(1)}) custom-call(bf16[8,32,896]{2,1,0:T(8,128)(2,1)S(1)} %bitcast.32, s32[32,1]{1,0:T(8,128)S(1)} %get-tuple-element.29.rank_ref, f32[1,7168]{1,0:T(1,128)S(1)} %copy-done.3, f32[8,32]{1,0:T(8,128)S(1)} %get-tuple-element.30.pick_ref, ...), custom_call_target="tpu_custom_call" | custom-call | flops 205520896 | bytes 6422528 | tf_op jit(solution)/shard_map/last_up/pallas_call | solution.py:267
  180.5 1.2 collective-permute-done.7.sib_ref
  181.7 1.4 last_down.1
  183.2 0.9 copy.19
  184.1 4.2 %all-to-all-start.7 = ((bf16[32,8,896]{2,1,0:T(8,128)(2,1)}), bf16[32,8,896]{2,1,0:T(8,128)(2,1)S(1)}, u32[]{:S(2)}, u32[]{:S(2)}) async-start(bf16[32,8,896]{2,1,0:T(8,128)(2,1)} %copy.19), calls=%async_computation.7 | async-start | bytes 917504 | tf_op jit(solution)/shard_map/all_to_all | solution.py:406
  191.4 2.1 collective-permute-start.11
  193.4 1.0 collective-permute-done.9
  197.8 1.5 collective-permute-start.8
  199.4 5.8 %all-to-all-done.7 = bf16[32,8,896]{2,1,0:T(8,128)(2,1)S(1)} async-done(((bf16[32,8,896]{2,1,0:T(8,128)(2,1)}), bf16[32,8,896]{2,1,0:T(8,128)(2,1)S(1)}, u32[]{:S(2)}, u32[]{:S(2)}) %all-to-all-start.7) | async-done | bytes 458784 | tf_op jit(solution)/shard_map/all_to_all | solution.py:406
  (51 shorter events, 8.2 us)
Async XLA Ops:
  0.6 32.2 %collective-permute-start = (bf16[224,7168]{1,0:T(8,128)(2,1)}, bf16[224,7168]{1,0:T(8,128)(2,1)S(1)}, u32[]{:S(2)}, u32[]{:S(2)}) collective-permute-start(bf16[224,7168]{1,0:T(8,128)(2,1)} %bitcast.27), channel_id=1, source_target_pairs={{0,1},{1,0},{2,3},{3,2},{4,5},{5,4},{6,7},{7,6},{8,9},{9,8},{10,11... | collective-permute-start | bytes 9633800 | tf_op jit(solution)/shard_map/ppermute | solution.py:402
  0.7 32.1 %collective-permute-start.1 = (bf16[224,7168]{1,0:T(8,128)(2,1)}, bf16[224,7168]{1,0:T(8,128)(2,1)}, u32[]{:S(2)}, u32[]{:S(2)}) collective-permute-start(bf16[224,7168]{1,0:T(8,128)(2,1)} %bitcast.29), channel_id=1, source_target_pairs={{0,1},{1,0},{2,3},{3,2},{4,5},{5,4},{6,7},{7,6},{8,9},{9,8},{10,11... | collective-permute-start | bytes 9633800 | tf_op jit(solution)/shard_map/ppermute | solution.py:402
  1.2 150.4 %collective-permute-start.5 = (bf16[400,7168]{1,0:T(8,128)(2,1)}, bf16[400,7168]{1,0:T(8,128)(2,1)}, u32[]{:S(2)}, u32[]{:S(2)}) collective-permute-start(bf16[400,7168]{1,0:T(8,128)(2,1)} %head_a_ref.1), channel_id=1, source_target_pairs={{0,1},{1,0},{2,3},{3,2},{4,5},{5,4},{6,7},{7,6},{8,9},{9,8},{10,11... | collective-permute-start | bytes 17203208 | tf_op jit(solution)/shard_map/ppermute | solution.py:402
  2.3 0.8 copy-start.2
  3.0 28.7 %all-to-all-start = ((bf16[32,8,896]{2,1,0:T(8,128)(2,1)}), bf16[32,8,896]{2,1,0:T(8,128)(2,1)}, u32[]{:S(2)}, u32[]{:S(2)}) async-start(bf16[32,8,896]{2,1,0:T(8,128)(2,1)} %copy-done.2), calls=%async_computation | async-start | bytes 917504 | tf_op jit(solution)/shard_map/all_to_all | solution.py:406
  14.6 0.7 copy-start.5
  15.3 0.7 copy-start.6
  16.0 0.7 copy-start.7
  32.8 1.9 copy-start
  34.7 1.9 copy-start.1
  36.6 2.9 %copy-start.3 = (f32[1,7168]{1,0:T(1,128)S(1)}, f32[1,7168]{1,0:T(1,128)}, u32[]{:S(2)}) copy-start(f32[1,7168]{1,0:T(1,128)} %gain_ref.7) | copy-start | bytes 86020
  63.5 3.8 %collective-permute-start.2 = (bf16[8,896]{1,0:T(8,128)(2,1)S(1)}, bf16[8,896]{1,0:T(8,128)(2,1)S(1)}, u32[]{:S(2)}, u32[]{:S(2)}) collective-permute-start(bf16[8,896]{1,0:T(8,128)(2,1)S(1)} %settle.3), channel_id=1, source_target_pairs={{0,64},{64,128},{128,192},{192,0},{1,65},{65,129},{129,193},{193,1... | collective-permute-start | bytes 43016 | tf_op jit(solution)/shard_map/ppermute | solution.py:426
  108.3 3.8 %collective-permute-start.3 = (bf16[8,896]{1,0:T(8,128)(2,1)S(1)}, bf16[8,896]{1,0:T(8,128)(2,1)S(1)}, u32[]{:S(2)}, u32[]{:S(2)}) collective-permute-start(bf16[8,896]{1,0:T(8,128)(2,1)S(1)} %settle.4), channel_id=1, source_target_pairs={{0,64},{64,128},{128,192},{192,0},{1,65},{65,129},{129,193},{193,1... | collective-permute-start | bytes 43016 | tf_op jit(solution)/shard_map/ppermute | solution.py:426
  129.4 25.5 %slice-start = ((s8[5734400]{0:T(1024)(128)(4,1)}), s8[4194304]{0:T(1024)(128)(4,1)S(1)}, s32[]{:S(2)}) async-start(s8[5734400]{0:T(1024)(128)(4,1)} %bitcast.21), calls=%async_computation.8 | async-start | bytes 8388608
  129.4 25.5 %slice-start.1 = ((s8[5734400]{0:T(1024)(128)(4,1)}), s8[1540096]{0:T(1024)(128)(4,1)S(1)}, s32[]{:S(2)}) async-start(s8[5734400]{0:T(1024)(128)(4,1)} %bitcast.21), calls=%async_computation.9 | async-start | bytes 3080192
  129.4 25.5 %copy-start.4 = (f32[7168]{0:T(1024)S(1)}, f32[7168]{0:T(1024)}, u32[]{:S(2)}) copy-start(f32[7168]{0:T(1024)} %param.16) | copy-start | bytes 86020
  150.1 4.7 %collective-permute-start.4 = (bf16[8,896]{1,0:T(8,128)(2,1)S(1)}, bf16[8,896]{1,0:T(8,128)(2,1)S(1)}, u32[]{:S(2)}, u32[]{:S(2)}) collective-permute-start(bf16[8,896]{1,0:T(8,128)(2,1)S(1)} %settle.5), channel_id=1, source_target_pairs={{0,64},{64,128},{128,192},{192,0},{1,65},{65,129},{129,193},{193,1... | collective-permute-start | bytes 43016 | tf_op jit(solution)/shard_map/ppermute | solution.py:426
  180.4 1.3 collective-permute-start.7
  184.1 21.1 %all-to-all-start.7 = ((bf16[32,8,896]{2,1,0:T(8,128)(2,1)}), bf16[32,8,896]{2,1,0:T(8,128)(2,1)S(1)}, u32[]{:S(2)}, u32[]{:S(2)}) async-start(bf16[32,8,896]{2,1,0:T(8,128)(2,1)} %copy.19), calls=%async_computation.7 | async-start | bytes 917504 | tf_op jit(solution)/shard_map/all_to_all | solution.py:406
  188.4 9.4 %collective-permute-start.6 = (bf16[8,896]{1,0:T(8,128)(2,1)S(1)}, bf16[8,896]{1,0:T(8,128)(2,1)S(1)}, u32[]{:S(2)}, u32[]{:S(2)}) collective-permute-start(bf16[8,896]{1,0:T(8,128)(2,1)S(1)} %bitcast.38), channel_id=1, source_target_pairs={{0,1},{1,0},{2,3},{3,2},{4,5},{5,4},{6,7},{7,6},{8,9},{9,8},{10,11... | collective-permute-start | bytes 43016 | tf_op jit(solution)/shard_map/ppermute | solution.py:402
  190.8 3.6 %collective-permute-start.9 = (f32[1,1]{1,0:T(1,128)}, f32[1,1]{1,0:T(1,128)}, u32[]{:S(2)}, u32[]{:S(2)}) collective-permute-start(f32[1,1]{1,0:T(1,128)} %slice.19), channel_id=1, source_target_pairs={{0,64},{64,128},{128,192},{192,0},{1,65},{65,129},{129,193},{193,1... | collective-permute-start | bytes 20 | tf_op jit(solution)/shard_map/ppermute | solution.py:426
  191.4 5.3 %collective-permute-start.10 = (f32[1,1]{1,0:T(1,128)}, f32[1,1]{1,0:T(1,128)}, u32[]{:S(2)}, u32[]{:S(2)}) collective-permute-start(f32[1,1]{1,0:T(1,128)} %slice.19), channel_id=1, source_target_pairs={{0,128},{64,192},{128,0},{192,64},{1,129},{65,193},{129,1},{193,65... | collective-permute-start | bytes 20 | tf_op jit(solution)/shard_map/ppermute | solution.py:426
  191.4 5.8 %collective-permute-start.11 = (f32[1,1]{1,0:T(1,128)}, f32[1,1]{1,0:T(1,128)}, u32[]{:S(2)}, u32[]{:S(2)}) collective-permute-start(f32[1,1]{1,0:T(1,128)} %slice.19), channel_id=1, source_target_pairs={{0,192},{64,0},{128,64},{192,128},{1,193},{65,1},{129,65},{193,129... | collective-permute-start | bytes 20 | tf_op jit(solution)/shard_map/ppermute | solution.py:426
  197.8 7.5 %collective-permute-start.8 = (bf16[8,896]{1,0:T(8,128)(2,1)S(1)}, bf16[8,896]{1,0:T(8,128)(2,1)S(1)}, u32[]{:S(2)}, u32[]{:S(2)}) collective-permute-start(bf16[8,896]{1,0:T(8,128)(2,1)S(1)} %bitcast_select_fusion), channel_id=1, source_target_pairs={{0,192},{64,0},{128,64},{192,128},{1,193},{65,1},{129,65},{193,129... | collective-permute-start | bytes 43016 | tf_op jit(solution)/shard_map/ppermute | solution.py:426

commit v3 on v2

v3 whole, which is shorter than its diff:
```python
import functools

import jax
import jax.numpy as jnp
from jax import lax
from jax.experimental import pallas as pl
from jax.experimental.pallas import tpu as pltpu
from jax.sharding import Mesh, PartitionSpec as P

EPSILON = 1e-05
SQRT_HALF = 0.7071067811865476
PAYLOAD_LIMIT = 12 * 1024 * 1024
FIRST_LIMIT = 39 * 1024 * 1024
SMALL_LIMIT = 4 * 1024 * 1024
PLANE = ("dp", "y")
NT = (((1,), (1,)), ((), ()))
VMEM = pl.BlockSpec(memory_space=pltpu.VMEM)
SMEM = pl.BlockSpec(memory_space=pltpu.SMEM)
HBM = pl.BlockSpec(memory_space=pltpu.HBM)
SMALL = pltpu.CompilerParams(vmem_limit_bytes=SMALL_LIMIT)


def row_at(repack_ref, position):
    return repack_ref[0, 0, repack_ref[0, 1, position]]


def prepare_kernel(
    exit_ref, target_ref, repack_ref, gain_ref, rank_ref, chunk_rank_ref, wanted_ref, pick_ref,
    source_ref, flag_ref, ready_gain_ref
):
    half = rank_ref.shape[0]
    sub = chunk_rank_ref.shape[0]
    segment = lax.axis_index("segment")
    core = lax.axis_index("core")
    place = lax.axis_index("dp") * lax.axis_size("y") + lax.axis_index("y")
    first_row = lax.axis_index("y") * sub

    def source_of(position):
        first = repack_ref[0, 0, position]
        last = row_at(repack_ref, position)
        return jnp.where(segment == 3, last, jnp.where(segment == 2, first, position))

    mine = source_of(2 * place + core)
    other = source_of(2 * place + 1 - core)
    line = lax.broadcasted_iota(jnp.int32, (half, 1), 0)
    pick_line = lax.broadcasted_iota(jnp.int32, pick_ref.shape, 0)
    pick_lane = lax.broadcasted_iota(jnp.int32, pick_ref.shape, 1)
    ranks = jnp.zeros((half, 1), jnp.int32)
    wanteds = ranks
    sources = jnp.zeros(pick_ref.shape, jnp.int32)
    here, there = 0, 0
    for i in range(half):
        row = row_at(repack_ref, 2 * i + core)
        ranks = jnp.where(line == i, exit_ref[0, row], ranks)
        wanteds = jnp.where(line == i, target_ref[0, row], wanteds)
        sources = jnp.where(pick_lane == i, row, sources)
        here = jnp.where(row == 2 * place + core, 1, here)
        there = jnp.where(row == 2 * place + 1 - core, 1, there)
    rank_ref[...] = ranks
    wanted_ref[...] = wanteds
    source_ref[...] = sources
    ready_gain_ref[...] = gain_ref[...]
    pick_ref[...] = (
        ((pick_line == 0) & (sources == mine)) | ((pick_line == 1) & (sources == other))
    ).astype(jnp.float32)
    line = lax.broadcasted_iota(jnp.int32, (sub, 1), 0)
    ranks = jnp.zeros((sub, 1), jnp.int32)
    for i in range(sub):
        row = row_at(repack_ref, 2 * (first_row + i) + core)
        ranks = jnp.where(line == i, exit_ref[0, row], ranks)
    chunk_rank_ref[...] = ranks
    scoring = (segment >= 1) & (segment <= 2)
    chosen = scoring & (here == 1) & (exit_ref[0, 2 * place + core] == segment)
    other_chosen = scoring & (there == 1) & (exit_ref[0, 2 * place + 1 - core] == segment)
    rank = exit_ref[0, row_at(repack_ref, 2 * place + core)]
    living = (rank == 0) | (rank > 3)
    lines = lax.broadcasted_iota(jnp.int32, flag_ref.shape, 0)
    flag_ref[...] = (
        ((lines == 0) & chosen) | ((lines == 1) & other_chosen) | ((lines == 2) & living)
    ).astype(jnp.float32)


def prepare(exit_at, targets, repack, gain, half, sub):
    column = jax.ShapeDtypeStruct((half, 1), jnp.int32)
    return pl.pallas_call(
        prepare_kernel,
        out_shape=(
            column,
            jax.ShapeDtypeStruct((sub, 1), jnp.int32),
            column,
            jax.ShapeDtypeStruct((8, half), jnp.float32),
            jax.ShapeDtypeStruct((8, half), jnp.int32),
            jax.ShapeDtypeStruct((8, 128), jnp.float32),
            jax.ShapeDtypeStruct(gain.shape, gain.dtype),
        ),
        in_specs=[SMEM] * 3 + [VMEM],
        out_specs=(VMEM,) * 7,
        compiler_params=SMALL,
        name="prepare",
    )(exit_at, targets, repack, gain)


def normalise(rows_ref, gain_ref, living, out_ref):
    blocks, _, cols = rows_ref.shape
    width = blocks * cols
    total = rows_ref[0].astype(jnp.float32)
    for b in range(1, blocks):
        total += rows_ref[b].astype(jnp.float32)
    mean = jnp.sum(total, axis=1, keepdims=True) / width
    total = jnp.zeros_like(total)
    for b in range(blocks):
        lanes = slice(b * cols, (b + 1) * cols)
        center = rows_ref[b].astype(jnp.float32) - mean
        total += center * center
        out_ref[:, lanes] = (center * gain_ref[:, lanes]).astype(jnp.bfloat16)
    scale = lax.rsqrt(jnp.sum(total, axis=1, keepdims=True) / width + EPSILON)
    return scale if living is None else jnp.where(living, scale, 0.0)


def hidden_of(normed, scale, up_ref):
    pre = lax.dot_general(normed, up_ref[...], NT, preferred_element_type=jnp.float32) * scale
    return (0.5 * pre * (1.0 + lax.erf(pre * SQRT_HALF))).astype(jnp.bfloat16)


def project(hidden_a, hidden_b, down_a_ref, down_b_ref, out_ref, step=2):
    blocks, _, cols = out_ref.shape
    for b in range(0, blocks, step):
        lanes = slice(b * cols, (b + step) * cols)
        part = jnp.dot(hidden_a, down_a_ref[:, lanes], preferred_element_type=jnp.float32)
        part += jnp.dot(hidden_b, down_b_ref[:, lanes], preferred_element_type=jnp.float32)
        part = part.astype(jnp.bfloat16)
        for k in range(step):
            out_ref[b + k] = part[:, k * cols : (k + 1) * cols]


def pick_rows(section, rows_ref, pick_ref, before_ref, picked_ref):
    here = lax.axis_index("segment") == section

    def choose():
        pick = pick_ref[...].astype(jnp.bfloat16)
        for b in range(rows_ref.shape[0]):
            picked_ref[b] = jnp.dot(
                pick, rows_ref[b], preferred_element_type=jnp.float32
            ).astype(jnp.bfloat16)

    def keep():
        picked_ref[...] = before_ref[...]

    if before_ref is None:
        choose()
    else:
        pl.when(here)(choose)
        pl.when(jnp.logical_not(here))(keep)


def living_at(section, rank_ref):
    rank = rank_ref[...]
    return (rank == 0) | (rank > section)


def section_kernel(section, rows_ref, rank_ref, gain_ref, pick_ref, *refs):
    before_ref = refs[0] if len(refs) == 8 else None
    up_a_ref, up_b_ref, down_a_ref, down_b_ref, out_ref, picked_ref, normed_ref = refs[-7:]
    scale = normalise(rows_ref, gain_ref, living_at(section, rank_ref), normed_ref)
    normed = normed_ref[...]
    hidden_a = hidden_of(normed, scale, up_a_ref)
    hidden_b = hidden_of(normed, scale, up_b_ref)
    project(hidden_a, hidden_b, down_a_ref, down_b_ref, out_ref)
    pick_rows(section, rows_ref, pick_ref, before_ref, picked_ref)


def run_section(section, rows, ranks, gain, pick, before, weights):
    blocks, half, cols = rows.shape
    block = jax.ShapeDtypeStruct(rows.shape, jnp.bfloat16)
    hidden = 2 * weights[0].shape[0]
    return pl.pallas_call(
        functools.partial(section_kernel, section),
        out_shape=(block, jax.ShapeDtypeStruct((blocks, pick.shape[0], cols), jnp.bfloat16)),
        in_specs=[VMEM] * (8 + len(before)),
        out_specs=(VMEM, VMEM),
        scratch_shapes=[pltpu.VMEM((half, blocks * cols), jnp.bfloat16)],
        compiler_params=SMALL,
        cost_estimate=pl.CostEstimate(
            flops=4 * half * blocks * cols * hidden,
            bytes_accessed=4 * hidden * blocks * cols,
            transcendentals=half * hidden,
        ),
        name="section",
    )(rows, ranks, gain, pick, *before, *weights)


def settle_kernel(section, parts_ref, chunk_ref, rank_ref, out_ref):
    total = jnp.where(living_at(section, rank_ref), chunk_ref[...].astype(jnp.float32), 0.0)
    summed = parts_ref[0].astype(jnp.float32)
    for k in range(1, parts_ref.shape[0]):
        summed += parts_ref[k].astype(jnp.float32)
    out_ref[...] = (total + summed).astype(jnp.bfloat16)


def settle(section, parts, chunk, chunk_ranks):
    return pl.pallas_call(
        functools.partial(settle_kernel, section),
        out_shape=jax.ShapeDtypeStruct(chunk.shape, jnp.bfloat16),
        in_specs=[VMEM] * 3,
        out_specs=VMEM,
        compiler_params=SMALL,
        name="settle",
    )(parts, chunk, chunk_ranks)


def spread_kernel(chunk_ref, out_ref):
    chunk = chunk_ref[...]
    for k in range(out_ref.shape[0]):
        out_ref[k] = chunk


def spread(members, chunk):
    return pl.pallas_call(
        spread_kernel,
        out_shape=jax.ShapeDtypeStruct((members, *chunk.shape), jnp.bfloat16),
        in_specs=[VMEM],
        out_specs=VMEM,
        compiler_params=SMALL,
        name="spread",
    )(chunk)


def first_spread_kernel(row_ref, out_ref):
    members, blocks, cols = out_ref.shape
    row = row_ref[0].astype(jnp.float32)
    line = lax.broadcasted_iota(jnp.int32, (blocks, cols), 0)
    chunk = jnp.zeros((blocks, cols), jnp.float32)
    for b in range(blocks):
        chunk = jnp.where(line == b, row[:, b * cols : (b + 1) * cols], chunk)
    chunk = chunk.astype(jnp.bfloat16)
    for k in range(members):
        out_ref[k] = chunk


def first_spread(members, blocks, row):
    return pl.pallas_call(
        first_spread_kernel,
        out_shape=jax.ShapeDtypeStruct((members, blocks, row.shape[-1] // blocks), row.dtype),
        in_specs=[VMEM],
        out_specs=VMEM,
        compiler_params=SMALL,
        name="first_spread",
    )(row)


def first_section_kernel(own_ref, sib_ref, repack_ref, gain_ref, *refs):
    held_refs, (out_ref, chunk_ref), ready_refs = refs[:4], refs[4:6], refs[6:10]
    gathered_ref, rows_ref, normed_ref, sems = refs[10:]
    copies = [
        pltpu.make_async_copy(held, ready, sems.at[i])
        for i, (held, ready) in enumerate(zip(held_refs, ready_refs))
    ]
    copies[0].start()
    copies[1].start()
    members, blocks, cols = gathered_ref.shape
    sub = chunk_ref.shape[0]
    core = lax.axis_index("core")
    for i in range(members):
        row = row_at(repack_ref, 2 * i + core)
        gathered_ref[i] = jnp.where(row % 2 == core, own_ref[row // 2], sib_ref[row // 2])
    copies[2].start()
    copies[3].start()
    rows = jnp.swapaxes(gathered_ref[...].astype(jnp.float32), 0, 1)
    rows_ref[...] = rows.astype(jnp.bfloat16)
    scale = normalise(rows_ref, gain_ref, None, normed_ref)
    block = lax.axis_index("dp")
    first_row = lax.axis_index("y") * sub
    line = lax.broadcasted_iota(jnp.int32, (blocks, cols), 0)
    chunk = jnp.zeros((sub, cols), jnp.float32)
    for r in range(sub):
        tile = gathered_ref[first_row + r].astype(jnp.float32)
        row = jnp.sum(jnp.where(line == block, tile, 0.0), axis=0, keepdims=True)
        chunk = jnp.where(line[:sub] == r, row, chunk)
    chunk_ref[...] = chunk.astype(jnp.bfloat16)
    up_a_ref, up_b_ref, down_a_ref, down_b_ref = ready_refs
    normed = normed_ref[...]
    copies[0].wait()
    hidden_a = hidden_of(normed, scale, up_a_ref)
    copies[1].wait()
    hidden_b = hidden_of(normed, scale, up_b_ref)
    copies[2].wait()
    copies[3].wait()
    project(hidden_a, hidden_b, down_a_ref, down_b_ref, out_ref)


def run_first_section(own, sib, repack, gain, sub, weights):
    members, blocks, cols = own.shape
    shape = (blocks, members, cols)
    hidden = 2 * weights[0].shape[0]
    return pl.pallas_call(
        first_section_kernel,
        out_shape=(
            jax.ShapeDtypeStruct(shape, jnp.bfloat16),
            jax.ShapeDtypeStruct((sub, cols), jnp.bfloat16),
            *(jax.ShapeDtypeStruct(w.shape, w.dtype) for w in weights),
        ),
        in_specs=[VMEM, VMEM, SMEM, VMEM] + [HBM] * 4,
        out_specs=(VMEM,) * 6,
        scratch_shapes=[
            pltpu.VMEM(own.shape, jnp.bfloat16),
            pltpu.VMEM(shape, jnp.bfloat16),
            pltpu.VMEM((members, blocks * cols), jnp.bfloat16),
            pltpu.SemaphoreType.DMA((4,)),
        ],
        compiler_params=pltpu.CompilerParams(vmem_limit_bytes=FIRST_LIMIT),
        cost_estimate=pl.CostEstimate(
            flops=4 * members * blocks * cols * hidden,
            bytes_accessed=4 * hidden * blocks * cols,
            transcendentals=members * hidden,
        ),
        name="first_section",
    )(own, sib, repack, gain, *weights)


def last_section_kernel(
    section, rows_ref, rank_ref, gain_ref, pick_ref, before_ref, flag_ref,
    up_a_ref, up_b_ref, down_a_ref, down_b_ref,
    out_ref, mine_ref, other_ref, score_ref, other_score_ref, normed_ref, picked_ref, parts_ref
):
    blocks, half, cols = rows_ref.shape
    core = lax.axis_index("core")

    @pl.when(lax.axis_index("segment") == section)
    def _():
        section_kernel(
            section, rows_ref, rank_ref, gain_ref, pick_ref, None,
            up_a_ref, up_b_ref, down_a_ref, down_b_ref, parts_ref, picked_ref, normed_ref
        )
        parts = jnp.swapaxes(parts_ref[...].astype(jnp.float32), 0, 1)
        out_ref[...] = parts.astype(jnp.bfloat16)

    @pl.when(lax.axis_index("segment") != section)
    def _():
        picked_ref[...] = before_ref[...]

    line = lax.broadcasted_iota(jnp.int32, (blocks, cols), 0)
    mine = jnp.zeros((blocks, cols), jnp.float32)
    other = mine
    for b in range(blocks):
        tile = picked_ref[b].astype(jnp.float32)
        mine = jnp.where(line == b, tile[0:1], mine)
        other = jnp.where(line == b, tile[1:2], other)
    mine_ref[...] = mine.astype(jnp.bfloat16)
    other_ref[...] = other.astype(jnp.bfloat16)
    sub = flag_ref.shape[0]
    sums = jnp.zeros(flag_ref.shape, jnp.float32)
    for b in range(blocks):
        for r in range(0, half, sub):
            sums += rows_ref[b, r : r + sub, :128].astype(jnp.float32)
    for index, ref in enumerate((score_ref, other_score_ref)):
        stats = jnp.where(core == index, sums[0:1], sums[1:2])
        exp_total = stats[:, 0:1] + stats[:, 2:3]
        picked = stats[:, 1:2] + stats[:, 3:4]
        flag = flag_ref[index : index + 1, 0:1]
        score = jnp.where(flag > 0.0, picked - jnp.log(exp_total), 0.0)
        ref[...] = jnp.broadcast_to(score, ref.shape)


def run_last_section(section, rows, ranks, gain, pick, before, flags, weights):
    blocks, half, cols = rows.shape
    hidden = 2 * weights[0].shape[0]
    row = jax.ShapeDtypeStruct((blocks, cols), jnp.bfloat16)
    score = jax.ShapeDtypeStruct((1, 128), jnp.float32)
    return pl.pallas_call(
        functools.partial(last_section_kernel, section),
        out_shape=(
            jax.ShapeDtypeStruct((half, blocks, cols), jnp.bfloat16), row, row, score, score
        ),
        in_specs=[VMEM] * 10,
        out_specs=(VMEM,) * 5,
        scratch_shapes=[
            pltpu.VMEM((half, blocks * cols), jnp.bfloat16),
            pltpu.VMEM(before.shape, jnp.bfloat16),
            pltpu.VMEM(rows.shape, jnp.bfloat16),
        ],
        compiler_params=SMALL,
        cost_estimate=pl.CostEstimate(
            flops=4 * half * blocks * cols * hidden,
            bytes_accessed=4 * hidden * blocks * cols,
            transcendentals=half * hidden,
        ),
        name="last_section",
    )(rows, ranks, gain, pick, before, flags, *weights)


def finish_kernel(section, parts_ref, row_ref, returned_ref, flag_ref, out_ref):
    blocks, cols = row_ref.shape
    here = lax.axis_index("segment") == section

    @pl.when(here)
    def _():
        total = jnp.where(flag_ref[2:3, 0:1] > 0.0, row_ref[...].astype(jnp.float32), 0.0)
        summed = parts_ref[0].astype(jnp.float32)
        for k in range(1, parts_ref.shape[0]):
            summed += parts_ref[k].astype(jnp.float32)
        total += summed
        for b in range(blocks):
            out_ref[0, 0, :, b * cols : (b + 1) * cols] = total[b : b + 1].astype(jnp.bfloat16)

    @pl.when(jnp.logical_not(here))
    def _():
        total = returned_ref[...].astype(jnp.float32)
        for b in range(blocks):
            out_ref[0, 0, :, b * cols : (b + 1) * cols] = total[b : b + 1].astype(jnp.bfloat16)


def finish(section, parts, row, returned, flags):
    width = row.shape[0] * row.shape[1]
    return pl.pallas_call(
        functools.partial(finish_kernel, section),
        out_shape=jax.ShapeDtypeStruct((1, 1, 1, width), jnp.bfloat16),
        in_specs=[VMEM] * 4,
        out_specs=VMEM,
        compiler_params=SMALL,
        name="finish",
    )(parts, row, returned, flags)


def payload_kernel(
    chunk_ref, first_ref, second_ref, source_ref, wanted_ref, gain_ref, head_a_ref, head_b_ref,
    out_ref, rows_ref, normed_ref, held_ref, sem
):
    members = out_ref.shape[0]
    segment = lax.axis_index("segment")
    core = lax.axis_index("core")
    place = lax.axis_index("dp") * lax.axis_size("y") + lax.axis_index("y")
    scoring = (segment >= 1) & (segment <= 2)

    @pl.when(jnp.logical_not(scoring))
    def _():
        chunk = chunk_ref[...]
        for k in range(members):
            out_ref[k] = chunk

    @pl.when(segment == 1)
    def _():
        rows_ref[...] = first_ref[...]

    @pl.when(segment == 2)
    def _():
        rows_ref[...] = second_ref[...]

    @pl.when(scoring)
    def _():
        copy = pltpu.make_async_copy(head_b_ref, held_ref, sem)
        copy.start()
        scale = normalise(rows_ref, gain_ref, None, normed_ref)
        normed = normed_ref[...]
        half, vocab = normed.shape[0], head_a_ref.shape[0]
        wanted = wanted_ref[...]
        exp_part = jnp.zeros((half, 1), jnp.float32)
        picked = jnp.zeros((half, 1), jnp.float32)
        for ref, shard in (
            (head_a_ref, 2 * place + core),
            (held_ref, 2 * place + 1 - core),
        ):
            if ref is held_ref:
                copy.wait()
            logits = lax.dot_general(normed, ref[...], NT, preferred_element_type=jnp.float32)
            logits *= scale
            exp_part += jnp.sum(jnp.exp(logits), axis=1, keepdims=True)
            columns = lax.broadcasted_iota(jnp.int32, logits.shape, 1) + shard * vocab
            picked += jnp.sum(jnp.where(columns == wanted, logits, 0.0), axis=1, keepdims=True)
        lane = lax.broadcasted_iota(jnp.int32, (half, 128), 1)
        both = jnp.where(lane % 2 == 0, exp_part, picked)
        high = both.astype(jnp.bfloat16).astype(jnp.float32)
        stats = jnp.where(lane < 2, high, jnp.where(lane < 4, both - high, 0.0))
        out_ref[...] = jnp.zeros_like(out_ref)
        stats = stats.astype(jnp.bfloat16)
        target = 2 * lax.broadcasted_iota(jnp.int32, (members, half), 0)
        sorted_stats = [
            jnp.dot(
                jnp.where(source_ref[0:1, :] == target + parity, 1.0, 0.0).astype(jnp.bfloat16),
                stats,
                preferred_element_type=jnp.float32,
            )
            for parity in range(2)
        ]
        line = lax.broadcasted_iota(jnp.int32, (out_ref.shape[1], 128), 0)
        for k in range(members):
            even, odd = (part[k : k + 1] for part in sorted_stats)
            tile = jnp.where(line == 0, even, jnp.where(line == 1, odd, 0.0))
            out_ref[k, :, :128] = tile.astype(jnp.bfloat16)


def run_payload(members, chunk, first, second, sources, wanted, gain, head_a, head_b):
    blocks, half, cols = first.shape
    return pl.pallas_call(
        payload_kernel,
        out_shape=jax.ShapeDtypeStruct((members, *chunk.shape), jnp.bfloat16),
        in_specs=[VMEM] * 7 + [HBM],
        out_specs=VMEM,
        scratch_shapes=[
            pltpu.VMEM(first.shape, jnp.bfloat16),
            pltpu.VMEM((half, blocks * cols), jnp.bfloat16),
            pltpu.VMEM(head_b.shape, jnp.bfloat16),
            pltpu.SemaphoreType.DMA,
        ],
        compiler_params=pltpu.CompilerParams(vmem_limit_bytes=PAYLOAD_LIMIT),
        name="payload",
    )(chunk, first, second, sources, wanted, gain, head_a, head_b)


def swapped(value):
    return lax.ppermute(value, "core", [(0, 1), (1, 0)])


def exchanged(value):
    return lax.all_to_all(value, PLANE, 0, 0, tiled=True)


def on_device(inputs, exit_at, targets, repack, norm_gain, up_weight, down_weight, exit_gain, head):
    section_count = lax.axis_size("segment")
    blocks = lax.axis_size("dp")
    y_count = lax.axis_size("y")
    members = blocks * y_count
    cols = inputs.shape[2] // blocks
    half = exit_at.shape[1] // 2
    sub = half // y_count
    up_a, down_a = up_weight[0], down_weight[0]
    up_b, down_b = swapped(up_a), swapped(down_a)

    def hop(value, step):
        pairs = [(i, (i + step) % section_count) for i in range(section_count)]
        return lax.ppermute(value, "segment", pairs)

    gathered = exchanged(first_spread(members, blocks, inputs))
    gathered, *prepared = lax.optimization_barrier(
        (gathered, *prepare(exit_at, targets, repack, norm_gain, half, sub))
    )
    ranks, chunk_ranks, wanted, pick, sources, flags, gain = prepared
    parts, chunk, *weights = run_first_section(
        gathered, swapped(gathered), repack, gain, sub, (up_a, up_b, down_a, down_b)
    )
    kept, before = [], ()
    for section in range(3):
        if section:
            rows = exchanged(spread(members, chunk)).reshape(blocks, half, cols)
            kept.append(rows)
            parts, picked = run_section(section, rows, ranks, gain, pick, before, weights)
            before = (picked,)
        parts = exchanged(parts.reshape(members, sub, cols))
        chunk = hop(settle(section, parts, chunk, chunk_ranks), 1)
    head_sib = swapped(head)
    payload = run_payload(
        members, chunk, *kept, sources, wanted, exit_gain[None, :], head, head_sib
    )
    rows = exchanged(payload).reshape(blocks, half, cols)
    parts, mine, other, score, other_score = run_last_section(
        3, rows, ranks, gain, pick, picked, flags, weights
    )
    parts = exchanged(parts)
    selected = mine + swapped(other)
    score += swapped(other_score)
    selected, score = lax.optimization_barrier((selected, score))
    returned = hop(selected, -1)
    scores = score + hop(score, 1) + hop(score, 2) + hop(score, 3)
    return finish(3, parts, selected, returned, flags), scores[:, :1]


def solution(mesh):
    segments, groups, tensors = mesh.devices.shape
    fine = Mesh(
        mesh.devices.reshape(segments, groups, tensors // 2, 2), ("segment", "dp", "y", "core")
    )
    rows = ("dp", "y", "core")
    placed = (
        P(None, rows, None),
        P(),
        P(),
        P(),
        P("segment", None),
        P("segment", rows, None),
        P("segment", rows, None),
        P(),
        P(rows, None),
    )
    return jax.shard_map(
        on_device,
        mesh=fine,
        in_specs=placed,
        out_specs=(P("segment", None, rows, None), P(None, rows)),
        check_vma=False,
    )
```

time: 208 us -> 198 us (0.952)
  local copies, waits for them, and re-layouts: 10.3 us -> 4.17 us
  between operations: 5.79 us -> 0.77 us
    pallas_call x3 -> x2, Pallas kernels: 11.2 us -> 7.03 us  [run_section(): pl.pallas_call(functools.partial(section_kernel, section), out_shape=(blo...]
    pallas_call x3 -> x4, Pallas kernels: 6.98 us -> 9.87 us  [the longest x1 7.63 us: run_first_section(): pl.pallas_call(first_section_kernel, out_shape=(jax.ShapeDtypeStruct(shap...]
    unnamed x21 -> x18, local copies, waits for them, and re-layouts: 6.58 us -> 4.17 us
  transfers between devices with their start and end apart: 14 -> 15, of which waited for: 8 -> 9; matrix products, arithmetic and copies ran while one was open for 2% -> 0% of each run, Pallas kernels for 7% -> 8%
where the time goes in v3:
time: 198 us; the launch traced here: 197 us
  blocking collectives  110 us (56%)
  waiting for transfers between devices  29.1 us (15%)
  starting transfers between devices  27.3 us (14%)
  Pallas kernels  25.1 us (13%)
  local copies, waits for them, and re-layouts  4.17 us (2%)
    all_to_all x6, blocking collectives, exchanged(): return lax.all_to_all(value, PLANE, 0, 0, tiled=True)  110 us
    all_to_all x2, waiting for transfers between devices, exchanged(): return lax.all_to_all(value, PLANE, 0, 0, tiled=True)  18.1 us
    all_to_all x2, starting transfers between devices, exchanged(): return lax.all_to_all(value, PLANE, 0, 0, tiled=True)  15.7 us
    ppermute x7, starting transfers between devices, hop(): return lax.ppermute(value, 'segment', pairs)  10.4 us
    ppermute x7, waiting for transfers between devices, hop(): return lax.ppermute(value, 'segment', pairs)  8.33 us
    pallas_call x1, Pallas kernels, run_first_section(): pl.pallas_call(first_section_kernel, out_shape=(jax.ShapeDtypeStruct(shap...  7.63 us
    pallas_call x1, Pallas kernels, run_payload(): pl.pallas_call(payload_kernel, out_shape=jax.ShapeDtypeStruct((members, *...  7.08 us
    pallas_call x2, Pallas kernels, run_section(): pl.pallas_call(functools.partial(section_kernel, section), out_shape=(blo...  7.03 us
  transfers between devices with their start and end apart: 15, of which 9 were waited for; matrix products, arithmetic and copies ran while one was open for 0% of the time, Pallas kernels for 8%

profile of v3, /device:TPU:2, one launch (start us, length us, event | category | flops | bytes accessed | tf_op | source)
XLA Modules:
  0.0 197.2 jit_solution(6309505033495646059)
XLA Ops:
  1.2 0.7 copy-done.2
  2.0 0.8 first_spread.1
  2.8 11.5 %all-to-all-start = ((bf16[32,8,896]{2,1,0:T(8,128)(2,1)}), bf16[32,8,896]{2,1,0:T(8,128)(2,1)S(1)}, u32[]{:S(2)}, u32[]{:S(2)}) async-start(bf16[32,8,896]{2,1,0:T(8,128)(2,1)} %first_spread.1), calls=%async_computation | async-start | bytes 917504 | tf_op jit(solution)/shard_map/all_to_all | solution.py:514
  14.4 0.7 copy-done.1
  15.2 0.7 copy-done.3
  17.1 0.8 prepare.1
  17.9 13.2 %all-to-all-done.own_ref = bf16[32,8,896]{2,1,0:T(8,128)(2,1)S(1)} async-done(((bf16[32,8,896]{2,1,0:T(8,128)(2,1)}), bf16[32,8,896]{2,1,0:T(8,128)(2,1)S(1)}, u32[]{:S(2)}, u32[]{:S(2)}) %all-to-all-start) | async-done | bytes 458784 | tf_op jit(solution)/shard_map/all_to_all | solution.py:514
  31.1 1.8 collective-permute-done.sib_ref
  32.9 0.7 copy-done.4
  33.6 7.6 %first_section.1 = (bf16[8,32,896]{2,1,0:T(8,128)(2,1)S(1)}, bf16[8,896]{1,0:T(8,128)(2,1)S(1)}, bf16[224,7168]{1,0:T(8,128)(2,1)S(1)}, bf16[224,7168]{1,0:T(8,1...) custom-call(bf16[32,8,896]{2,1,0:T(8,128)(2,1)S(1)} %all-to-all-done.own_ref, ...), custom_call_target="tpu_custom_call" | custom-call | flops 411041792 | bytes 12845056 | tf_op jit(solution)/shard_map/first_section/pallas_call | solution.py:295
  41.2 21.1 %all_to_all.40.parts_ref = bf16[32,8,896]{2,1,0:T(8,128)(2,1)S(1)} all-to-all(bf16[32,8,896]{2,1,0:T(8,128)(2,1)S(1)} %bitcast.17), channel_id=1, replica_groups=mesh['segment'=4,'dp'=8,'y'=4,'core'=2] {'dp','y'}, dimensions={0} | all-to-all | bytes 917504 | tf_op jit(solution)/shard_map/all_to_all | solution.py:514
  62.4 1.6 collective-permute-start.3
  64.0 2.2 %collective-permute-done.3.chunk_ref = bf16[8,896]{1,0:T(8,128)(2,1)S(1)} collective-permute-done((bf16[8,896]{1,0:T(8,128)(2,1)S(1)}, bf16[8,896]{1,0:T(8,128)(2,1)S(1)}, u32[]{:S(2)}, u32[]{:S(2)}) %collective-permute-start.3) | collective-permute-done | bytes 14368 | tf_op jit(solution)/shard_map/ppermute | solution.py:530
  66.2 19.1 %all_to_all.41 = bf16[32,8,896]{2,1,0:T(8,128)(2,1)S(1)} all-to-all(bf16[32,8,896]{2,1,0:T(8,128)(2,1)S(1)} %spread.2), channel_id=1, replica_groups=mesh['segment'=4,'dp'=8,'y'=4,'core'=2] {'dp','y'}, dimensions={0} | all-to-all | bytes 917504 | tf_op jit(solution)/shard_map/all_to_all | solution.py:514
  85.3 3.6 %section.2 = (bf16[8,32,896]{2,1,0:T(8,128)(2,1)S(1)}, bf16[8,8,896]{2,1,0:T(8,128)(2,1)S(1)}) custom-call(bf16[8,32,896]{2,1,0:T(8,128)(2,1)S(1)} %bitcast.12, s32[32,1]{1,0:T(8,128)S(1)} %get-tuple-element.46.rank_ref, f32[1,7168]{1,0:T(1,128)S(1)} %get-tuple-element.42.gain_ref, f32[8,32]{1,0:T(8,128)S(1)} %get-tuple-element.47.pick_ref, ...), custom_call_target="tpu_custom_call" | custom-call | flops 411041792 | bytes 12845056 | tf_op jit(solution)/shard_map/section/pallas_call | solution.py:176
  88.9 18.5 %all_to_all.42.parts_ref = bf16[32,8,896]{2,1,0:T(8,128)(2,1)S(1)} all-to-all(bf16[32,8,896]{2,1,0:T(8,128)(2,1)S(1)} %bitcast.19), channel_id=1, replica_groups=mesh['segment'=4,'dp'=8,'y'=4,'core'=2] {'dp','y'}, dimensions={0} | all-to-all | bytes 917504 | tf_op jit(solution)/shard_map/all_to_all | solution.py:514
  107.5 1.6 collective-permute-start.4
  109.0 2.2 %collective-permute-done.4.chunk_ref = bf16[8,896]{1,0:T(8,128)(2,1)S(1)} collective-permute-done((bf16[8,896]{1,0:T(8,128)(2,1)S(1)}, bf16[8,896]{1,0:T(8,128)(2,1)S(1)}, u32[]{:S(2)}, u32[]{:S(2)}) %collective-permute-start.4) | collective-permute-done | bytes 14368 | tf_op jit(solution)/shard_map/ppermute | solution.py:530
  111.3 17.4 %all_to_all.43 = bf16[32,8,896]{2,1,0:T(8,128)(2,1)S(1)} all-to-all(bf16[32,8,896]{2,1,0:T(8,128)(2,1)S(1)} %spread.3), channel_id=1, replica_groups=mesh['segment'=4,'dp'=8,'y'=4,'core'=2] {'dp','y'}, dimensions={0} | all-to-all | bytes 917504 | tf_op jit(solution)/shard_map/all_to_all | solution.py:514
  128.7 3.5 %section.3 = (bf16[8,32,896]{2,1,0:T(8,128)(2,1)S(1)}, bf16[8,8,896]{2,1,0:T(8,128)(2,1)S(1)}) custom-call(bf16[8,32,896]{2,1,0:T(8,128)(2,1)S(1)} %bitcast.14, s32[32,1]{1,0:T(8,128)S(1)} %get-tuple-element.46.rank_ref, f32[1,7168]{1,0:T(1,128)S(1)} %get-tuple-element.42.gain_ref, f32[8,32]{1,0:T(8,128)S(1)} %get-tuple-element.47.pick_ref, ...), custom_call_target="tpu_custom_call" | custom-call | flops 411041792 | bytes 12845056 | tf_op jit(solution)/shard_map/section/pallas_call | solution.py:176
  132.2 17.1 %all_to_all.44.parts_ref = bf16[32,8,896]{2,1,0:T(8,128)(2,1)S(1)} all-to-all(bf16[32,8,896]{2,1,0:T(8,128)(2,1)S(1)} %bitcast.18), channel_id=1, replica_groups=mesh['segment'=4,'dp'=8,'y'=4,'core'=2] {'dp','y'}, dimensions={0} | all-to-all | bytes 917504 | tf_op jit(solution)/shard_map/all_to_all | solution.py:514
  149.3 1.7 collective-permute-start.5
  151.1 3.0 %collective-permute-done.5.chunk_ref = bf16[8,896]{1,0:T(8,128)(2,1)S(1)} collective-permute-done((bf16[8,896]{1,0:T(8,128)(2,1)S(1)}, bf16[8,896]{1,0:T(8,128)(2,1)S(1)}, u32[]{:S(2)}, u32[]{:S(2)}) %collective-permute-start.5) | collective-permute-done | bytes 14368 | tf_op jit(solution)/shard_map/ppermute | solution.py:530
  154.1 7.1 %payload.1 = bf16[32,8,896]{2,1,0:T(8,128)(2,1)S(1)} custom-call(bf16[8,896]{1,0:T(8,128)(2,1)S(1)} %collective-permute-done.5.chunk_ref, bf16[8,32,896]{2,1,0:T(8,128)(2,1)S(1)} %bitcast.13, bf16[8,32,896]{2,1,0:T(8,128)(2,1)S(1)} %bitcast.15, s32[8,32]{1,0:T(8,128)S(1)} %get-tuple-element.55.source_ref, s32[32,1]{1,0:T(8,128)S(1)} %get-tuple-element.56.wanted_ref, ...), custom_call_target="tpu_custom_call" | custom-call | tf_op jit(solution)/shard_map/payload/pallas_call | solution.py:493
  161.2 17.1 %all_to_all.45 = bf16[32,8,896]{2,1,0:T(8,128)(2,1)S(1)} all-to-all(bf16[32,8,896]{2,1,0:T(8,128)(2,1)S(1)} %payload.1), channel_id=1, replica_groups=mesh['segment'=4,'dp'=8,'y'=4,'core'=2] {'dp','y'}, dimensions={0} | all-to-all | bytes 917504 | tf_op jit(solution)/shard_map/all_to_all | solution.py:514
  178.3 0.8 last_section.1
  179.1 4.2 %all-to-all-start.7 = ((bf16[32,8,896]{2,1,0:T(8,128)(2,1)}), bf16[32,8,896]{2,1,0:T(8,128)(2,1)S(1)}, u32[]{:S(2)}, u32[]{:S(2)}) async-start(bf16[32,8,896]{2,1,0:T(8,128)(2,1)} %get-tuple-element.59), calls=%async_computation.7 | async-start | bytes 917504 | tf_op jit(solution)/shard_map/all_to_all | solution.py:514
  183.9 0.8 collective-permute-done.8
  184.7 0.8 collective-permute-start.10
  185.6 2.2 %collective-permute-start.12 = (f32[1,128]{1,0:T(1,128)S(1)}, f32[1,128]{1,0:T(1,128)S(1)}, u32[]{:S(2)}, u32[]{:S(2)}) collective-permute-start(f32[1,128]{1,0:T(1,128)S(1)} %add.16), channel_id=1, source_target_pairs={{0,192},{64,0},{128,64},{192,128},{1,193},{65,1},{129,65},{193,129... | collective-permute-start | bytes 1544 | tf_op jit(solution)/shard_map/ppermute | solution.py:530
  187.7 2.5 %collective-permute-start.9 = (bf16[8,896]{1,0:T(8,128)(2,1)S(1)}, bf16[8,896]{1,0:T(8,128)(2,1)S(1)}, u32[]{:S(2)}, u32[]{:S(2)}) collective-permute-start(bf16[8,896]{1,0:T(8,128)(2,1)S(1)} %add.15.row_ref), channel_id=1, source_target_pairs={{0,192},{64,0},{128,64},{192,128},{1,193},{65,1},{129,65},{193,129... | collective-permute-start | bytes 43016 | tf_op jit(solution)/shard_map/ppermute | solution.py:530
  191.7 4.9 %all-to-all-done.7.parts_ref = bf16[32,8,896]{2,1,0:T(8,128)(2,1)S(1)} async-done(((bf16[32,8,896]{2,1,0:T(8,128)(2,1)}), bf16[32,8,896]{2,1,0:T(8,128)(2,1)S(1)}, u32[]{:S(2)}, u32[]{:S(2)}) %all-to-all-start.7) | async-done | bytes 458784 | tf_op jit(solution)/shard_map/all_to_all | solution.py:514
  (39 shorter events, 5.0 us)
Async XLA Ops:
  0.6 32.3 %collective-permute-start.1 = (bf16[224,7168]{1,0:T(8,128)(2,1)}, bf16[224,7168]{1,0:T(8,128)(2,1)}, u32[]{:S(2)}, u32[]{:S(2)}) collective-permute-start(bf16[224,7168]{1,0:T(8,128)(2,1)} %bitcast.21), channel_id=1, source_target_pairs={{0,1},{1,0},{2,3},{3,2},{4,5},{5,4},{6,7},{7,6},{8,9},{9,8},{10,11... | collective-permute-start | bytes 9633800 | tf_op jit(solution)/shard_map/ppermute | solution.py:510
  0.7 32.2 %collective-permute-start.2 = (bf16[224,7168]{1,0:T(8,128)(2,1)}, bf16[224,7168]{1,0:T(8,128)(2,1)}, u32[]{:S(2)}, u32[]{:S(2)}) collective-permute-start(bf16[224,7168]{1,0:T(8,128)(2,1)} %bitcast.23), channel_id=1, source_target_pairs={{0,1},{1,0},{2,3},{3,2},{4,5},{5,4},{6,7},{7,6},{8,9},{9,8},{10,11... | collective-permute-start | bytes 9633800 | tf_op jit(solution)/shard_map/ppermute | solution.py:510
  1.2 0.7 copy-start.2
  2.8 28.3 %all-to-all-start = ((bf16[32,8,896]{2,1,0:T(8,128)(2,1)}), bf16[32,8,896]{2,1,0:T(8,128)(2,1)S(1)}, u32[]{:S(2)}, u32[]{:S(2)}) async-start(bf16[32,8,896]{2,1,0:T(8,128)(2,1)} %first_spread.1), calls=%async_computation | async-start | bytes 917504 | tf_op jit(solution)/shard_map/all_to_all | solution.py:514
  14.3 136.8 %collective-permute-start.6 = (bf16[400,7168]{1,0:T(8,128)(2,1)}, bf16[400,7168]{1,0:T(8,128)(2,1)}, u32[]{:S(2)}, u32[]{:S(2)}) collective-permute-start(bf16[400,7168]{1,0:T(8,128)(2,1)} %head_a_ref.1), channel_id=1, source_target_pairs={{0,1},{1,0},{2,3},{3,2},{4,5},{5,4},{6,7},{7,6},{8,9},{9,8},{10,11... | collective-permute-start | bytes 17203208 | tf_op jit(solution)/shard_map/ppermute | solution.py:510
  14.4 0.8 copy-start.1
  15.2 0.7 copy-start.3
  15.8 0.7 copy-start.5
  16.5 0.7 copy-start.6
  31.1 1.8 collective-permute-start
  32.9 0.7 copy-start.4
  62.4 3.8 %collective-permute-start.3 = (bf16[8,896]{1,0:T(8,128)(2,1)S(1)}, bf16[8,896]{1,0:T(8,128)(2,1)S(1)}, u32[]{:S(2)}, u32[]{:S(2)}) collective-permute-start(bf16[8,896]{1,0:T(8,128)(2,1)S(1)} %settle.3), channel_id=1, source_target_pairs={{0,64},{64,128},{128,192},{192,0},{1,65},{65,129},{129,193},{193,1... | collective-permute-start | bytes 43016 | tf_op jit(solution)/shard_map/ppermute | solution.py:530
  107.5 3.8 %collective-permute-start.4 = (bf16[8,896]{1,0:T(8,128)(2,1)S(1)}, bf16[8,896]{1,0:T(8,128)(2,1)S(1)}, u32[]{:S(2)}, u32[]{:S(2)}) collective-permute-start(bf16[8,896]{1,0:T(8,128)(2,1)S(1)} %settle.4), channel_id=1, source_target_pairs={{0,64},{64,128},{128,192},{192,0},{1,65},{65,129},{129,193},{193,1... | collective-permute-start | bytes 43016 | tf_op jit(solution)/shard_map/ppermute | solution.py:530
  128.7 25.3 %slice-start = ((s8[5734400]{0:T(1024)(128)(4,1)}), s8[4194304]{0:T(1024)(128)(4,1)S(1)}, s32[]{:S(2)}) async-start(s8[5734400]{0:T(1024)(128)(4,1)} %bitcast.10), calls=%async_computation.8 | async-start | bytes 8388608
  128.7 25.3 %slice-start.1 = ((s8[5734400]{0:T(1024)(128)(4,1)}), s8[1540096]{0:T(1024)(128)(4,1)S(1)}, s32[]{:S(2)}) async-start(s8[5734400]{0:T(1024)(128)(4,1)} %bitcast.10), calls=%async_computation.9 | async-start | bytes 3080192
  128.7 25.3 %copy-start = (f32[7168]{0:T(1024)S(1)}, f32[7168]{0:T(1024)}, u32[]{:S(2)}) copy-start(f32[7168]{0:T(1024)} %param.16) | copy-start | bytes 86020
  149.3 4.7 %collective-permute-start.5 = (bf16[8,896]{1,0:T(8,128)(2,1)S(1)}, bf16[8,896]{1,0:T(8,128)(2,1)S(1)}, u32[]{:S(2)}, u32[]{:S(2)}) collective-permute-start(bf16[8,896]{1,0:T(8,128)(2,1)S(1)} %settle.5), channel_id=1, source_target_pairs={{0,64},{64,128},{128,192},{192,0},{1,65},{65,129},{129,193},{193,1... | collective-permute-start | bytes 43016 | tf_op jit(solution)/shard_map/ppermute | solution.py:530
  179.1 17.5 %all-to-all-start.7 = ((bf16[32,8,896]{2,1,0:T(8,128)(2,1)}), bf16[32,8,896]{2,1,0:T(8,128)(2,1)S(1)}, u32[]{:S(2)}, u32[]{:S(2)}) async-start(bf16[32,8,896]{2,1,0:T(8,128)(2,1)} %get-tuple-element.59), calls=%async_computation.7 | async-start | bytes 917504 | tf_op jit(solution)/shard_map/all_to_all | solution.py:514
  183.3 1.4 collective-permute-start.7
  183.4 1.3 collective-permute-start.8
  184.7 5.5 %collective-permute-start.10 = (f32[1,128]{1,0:T(1,128)S(1)}, f32[1,128]{1,0:T(1,128)S(1)}, u32[]{:S(2)}, u32[]{:S(2)}) collective-permute-start(f32[1,128]{1,0:T(1,128)S(1)} %add.16), channel_id=1, source_target_pairs={{0,64},{64,128},{128,192},{192,0},{1,65},{65,129},{129,193},{193,1... | collective-permute-start | bytes 1544 | tf_op jit(solution)/shard_map/ppermute | solution.py:530
  185.6 5.0 %collective-permute-start.11 = (f32[1,128]{1,0:T(1,128)S(1)}, f32[1,128]{1,0:T(1,128)S(1)}, u32[]{:S(2)}, u32[]{:S(2)}) collective-permute-start(f32[1,128]{1,0:T(1,128)S(1)} %add.16), channel_id=1, source_target_pairs={{0,128},{64,192},{128,0},{192,64},{1,129},{65,193},{129,1},{193,65... | collective-permute-start | bytes 1544 | tf_op jit(solution)/shard_map/ppermute | solution.py:530
  185.6 5.0 %collective-permute-start.12 = (f32[1,128]{1,0:T(1,128)S(1)}, f32[1,128]{1,0:T(1,128)S(1)}, u32[]{:S(2)}, u32[]{:S(2)}) collective-permute-start(f32[1,128]{1,0:T(1,128)S(1)} %add.16), channel_id=1, source_target_pairs={{0,192},{64,0},{128,64},{192,128},{1,193},{65,1},{129,65},{193,129... | collective-permute-start | bytes 1544 | tf_op jit(solution)/shard_map/ppermute | solution.py:530
  187.7 4.0 %collective-permute-start.9 = (bf16[8,896]{1,0:T(8,128)(2,1)S(1)}, bf16[8,896]{1,0:T(8,128)(2,1)S(1)}, u32[]{:S(2)}, u32[]{:S(2)}) collective-permute-start(bf16[8,896]{1,0:T(8,128)(2,1)S(1)} %add.15.row_ref), channel_id=1, source_target_pairs={{0,192},{64,0},{128,64},{192,128},{1,193},{65,1},{129,65},{193,129... | collective-permute-start | bytes 43016 | tf_op jit(solution)/shard_map/ppermute | solution.py:530

commit v4 on v3

--- a/solution.py
+++ b/solution.py
@@ -9,9 +9,9 @@
 
 EPSILON = 1e-05
 SQRT_HALF = 0.7071067811865476
-PAYLOAD_LIMIT = 12 * 1024 * 1024
 FIRST_LIMIT = 39 * 1024 * 1024
 SMALL_LIMIT = 4 * 1024 * 1024
+WEIGHT_PARTS = 2
 PLANE = ("dp", "y")
 NT = (((1,), (1,)), ((), ()))
 VMEM = pl.BlockSpec(memory_space=pltpu.VMEM)
@@ -189,23 +189,26 @@
     )(rows, ranks, gain, pick, *before, *weights)
 
 
-def settle_kernel(section, parts_ref, chunk_ref, rank_ref, out_ref):
-    total = jnp.where(living_at(section, rank_ref), chunk_ref[...].astype(jnp.float32), 0.0)
+def settle_kernel(section, parts_ref, chunk_ref, *refs):
+    out_ref = refs[-1]
+    total = chunk_ref[...].astype(jnp.float32)
+    if len(refs) == 2:
+        total = jnp.where(living_at(section, refs[0]), total, 0.0)
     summed = parts_ref[0].astype(jnp.float32)
     for k in range(1, parts_ref.shape[0]):
         summed += parts_ref[k].astype(jnp.float32)
     out_ref[...] = (total + summed).astype(jnp.bfloat16)
 
 
-def settle(section, parts, chunk, chunk_ranks):
+def settle(section, parts, chunk, *chunk_ranks):
     return pl.pallas_call(
         functools.partial(settle_kernel, section),
         out_shape=jax.ShapeDtypeStruct(chunk.shape, jnp.bfloat16),
-        in_specs=[VMEM] * 3,
+        in_specs=[VMEM] * (2 + len(chunk_ranks)),
         out_specs=VMEM,
         compiler_params=SMALL,
         name="settle",
-    )(parts, chunk, chunk_ranks)
+    )(parts, chunk, *chunk_ranks)
 
 
 def spread_kernel(chunk_ref, out_ref):
@@ -248,23 +251,31 @@
     )(row)
 
 
-def first_section_kernel(own_ref, sib_ref, repack_ref, gain_ref, *refs):
-    held_refs, (out_ref, chunk_ref), ready_refs = refs[:4], refs[4:6], refs[6:10]
-    gathered_ref, rows_ref, normed_ref, sems = refs[10:]
-    copies = [
-        pltpu.make_async_copy(held, ready, sems.at[i])
-        for i, (held, ready) in enumerate(zip(held_refs, ready_refs))
+def copies_of(held_ref, ready_ref, sems, first, parts):
+    rows = held_ref.shape[0] // parts
+    return [
+        pltpu.make_async_copy(
+            held_ref.at[pl.ds(k * rows, rows)], ready_ref.at[pl.ds(k * rows, rows)], sems.at[first + k]
+        )
+        for k in range(parts)
     ]
-    copies[0].start()
-    copies[1].start()
+
+
+def first_section_kernel(
+    own_ref, sib_ref, repack_ref, gain_ref, up_b_ref, down_b_ref, held_up_ref, held_down_ref,
+    out_ref, chunk_ref, up_a_ref, down_a_ref, gathered_ref, rows_ref, normed_ref, sems
+):
+    core = lax.axis_index("core")
+    up_copies = copies_of(held_up_ref, up_a_ref, sems, 0, WEIGHT_PARTS)
+    down_copies = copies_of(held_down_ref, down_a_ref, sems, WEIGHT_PARTS, WEIGHT_PARTS)
+    for copy in up_copies + down_copies:
+        copy.start()
     members, blocks, cols = gathered_ref.shape
     sub = chunk_ref.shape[0]
-    core = lax.axis_index("core")
     for i in range(members):
         row = row_at(repack_ref, 2 * i + core)
-        gathered_ref[i] = jnp.where(row % 2 == core, own_ref[row // 2], sib_ref[row // 2])
-    copies[2].start()
-    copies[3].start()
+        place = lax.shift_right_logical(row, 1)
+        gathered_ref[i] = jnp.where(row & 1 == core, own_ref[place], sib_ref[place])
     rows = jnp.swapaxes(gathered_ref[...].astype(jnp.float32), 0, 1)
     rows_ref[...] = rows.astype(jnp.bfloat16)
     scale = normalise(rows_ref, gain_ref, None, normed_ref)
@@ -277,14 +288,13 @@
         row = jnp.sum(jnp.where(line == block, tile, 0.0), axis=0, keepdims=True)
         chunk = jnp.where(line[:sub] == r, row, chunk)
     chunk_ref[...] = chunk.astype(jnp.bfloat16)
-    up_a_ref, up_b_ref, down_a_ref, down_b_ref = ready_refs
     normed = normed_ref[...]
-    copies[0].wait()
+    hidden_b = hidden_of(normed, scale, up_b_ref)
+    for copy in up_copies:
+        copy.wait()
     hidden_a = hidden_of(normed, scale, up_a_ref)
-    copies[1].wait()
-    hidden_b = hidden_of(normed, scale, up_b_ref)
-    copies[2].wait()
-    copies[3].wait()
+    for copy in down_copies:
+        copy.wait()
     project(hidden_a, hidden_b, down_a_ref, down_b_ref, out_ref)
 
 
@@ -297,15 +307,15 @@
         out_shape=(
             jax.ShapeDtypeStruct(shape, jnp.bfloat16),
             jax.ShapeDtypeStruct((sub, cols), jnp.bfloat16),
-            *(jax.ShapeDtypeStruct(w.shape, w.dtype) for w in weights),
+            *(jax.ShapeDtypeStruct(w.shape, w.dtype) for w in weights[2:]),
         ),
-        in_specs=[VMEM, VMEM, SMEM, VMEM] + [HBM] * 4,
-        out_specs=(VMEM,) * 6,
+        in_specs=[VMEM, VMEM, SMEM] + [VMEM] * 3 + [HBM] * 2,
+        out_specs=(VMEM,) * 4,
         scratch_shapes=[
             pltpu.VMEM(own.shape, jnp.bfloat16),
             pltpu.VMEM(shape, jnp.bfloat16),
             pltpu.VMEM((members, blocks * cols), jnp.bfloat16),
-            pltpu.SemaphoreType.DMA((4,)),
+            pltpu.SemaphoreType.DMA((2 * WEIGHT_PARTS,)),
         ],
         compiler_params=pltpu.CompilerParams(vmem_limit_bytes=FIRST_LIMIT),
         cost_estimate=pl.CostEstimate(
@@ -423,7 +433,7 @@
 
 def payload_kernel(
     chunk_ref, first_ref, second_ref, source_ref, wanted_ref, gain_ref, head_a_ref, head_b_ref,
-    out_ref, rows_ref, normed_ref, held_ref, sem
+    out_ref, rows_ref, normed_ref
 ):
     members = out_ref.shape[0]
     segment = lax.axis_index("segment")
@@ -447,8 +457,6 @@
 
     @pl.when(scoring)
     def _():
-        copy = pltpu.make_async_copy(head_b_ref, held_ref, sem)
-        copy.start()
         scale = normalise(rows_ref, gain_ref, None, normed_ref)
         normed = normed_ref[...]
         half, vocab = normed.shape[0], head_a_ref.shape[0]
@@ -457,10 +465,8 @@
         picked = jnp.zeros((half, 1), jnp.float32)
         for ref, shard in (
             (head_a_ref, 2 * place + core),
-            (held_ref, 2 * place + 1 - core),
+            (head_b_ref, 2 * place + 1 - core),
         ):
-            if ref is held_ref:
-                copy.wait()
             logits = lax.dot_general(normed, ref[...], NT, preferred_element_type=jnp.float32)
             logits *= scale
             exp_part += jnp.sum(jnp.exp(logits), axis=1, keepdims=True)
@@ -493,15 +499,13 @@
     return pl.pallas_call(
         payload_kernel,
         out_shape=jax.ShapeDtypeStruct((members, *chunk.shape), jnp.bfloat16),
-        in_specs=[VMEM] * 7 + [HBM],
+        in_specs=[VMEM] * 8,
         out_specs=VMEM,
         scratch_shapes=[
             pltpu.VMEM(first.shape, jnp.bfloat16),
             pltpu.VMEM((half, blocks * cols), jnp.bfloat16),
-            pltpu.VMEM(head_b.shape, jnp.bfloat16),
-            pltpu.SemaphoreType.DMA,
         ],
-        compiler_params=pltpu.CompilerParams(vmem_limit_bytes=PAYLOAD_LIMIT),
+        compiler_params=SMALL,
         name="payload",
     )(chunk, first, second, sources, wanted, gain, head_a, head_b)
 
@@ -523,30 +527,34 @@
     half = exit_at.shape[1] // 2
     sub = half // y_count
     up_a, down_a = up_weight[0], down_weight[0]
-    up_b, down_b = swapped(up_a), swapped(down_a)
+    up_b, down_b, head_sib = lax.optimization_barrier(
+        (swapped(up_a), swapped(down_a), swapped(head))
+    )
 
     def hop(value, step):
         pairs = [(i, (i + step) % section_count) for i in range(section_count)]
         return lax.ppermute(value, "segment", pairs)
 
     gathered = exchanged(first_spread(members, blocks, inputs))
-    gathered, *prepared = lax.optimization_barrier(
-        (gathered, *prepare(exit_at, targets, repack, norm_gain, half, sub))
+    parts, chunk, up_a, down_a = run_first_section(
+        gathered, swapped(gathered), repack, norm_gain, sub, (up_b, down_b, up_a, down_a)
+    )
+    weights = (up_a, up_b, down_a, down_b)
+    parts = exchanged(parts.reshape(members, sub, cols))
+    chunk = settle(0, parts, chunk)
+    chunk, exit_at, targets, repack = lax.optimization_barrier((chunk, exit_at, targets, repack))
+    chunk, *prepared = lax.optimization_barrier(
+        (hop(chunk, 1), *prepare(exit_at, targets, repack, norm_gain, half, sub))
     )
     ranks, chunk_ranks, wanted, pick, sources, flags, gain = prepared
-    parts, chunk, *weights = run_first_section(
-        gathered, swapped(gathered), repack, gain, sub, (up_a, up_b, down_a, down_b)
-    )
     kept, before = [], ()
-    for section in range(3):
-        if section:
-            rows = exchanged(spread(members, chunk)).reshape(blocks, half, cols)
-            kept.append(rows)
-            parts, picked = run_section(section, rows, ranks, gain, pick, before, weights)
-            before = (picked,)
+    for section in (1, 2):
+        rows = exchanged(spread(members, chunk)).reshape(blocks, half, cols)
+        kept.append(rows)
+        parts, picked = run_section(section, rows, ranks, gain, pick, before, weights)
+        before = (picked,)
         parts = exchanged(parts.reshape(members, sub, cols))
         chunk = hop(settle(section, parts, chunk, chunk_ranks), 1)
-    head_sib = swapped(head)
     payload = run_payload(
         members, chunk, *kept, sources, wanted, exit_gain[None, :], head, head_sib
     )

time: 198 us -> 193 us (0.975)
  blocking collectives: 110 us -> 139 us
  waiting for transfers between devices: 29.1 us -> 16.1 us
  starting transfers between devices: 27.3 us -> 14.8 us
  Pallas kernels: 25.1 us -> 19.2 us
    all_to_all x6 -> x7, blocking collectives: 110 us -> 139 us  [exchanged(): return lax.all_to_all(value, PLANE, 0, 0, tiled=True)]
    all_to_all x2 -> x1, waiting for transfers between devices: 18.1 us -> 3.68 us  [exchanged(): return lax.all_to_all(value, PLANE, 0, 0, tiled=True)]
    all_to_all x2 -> x1, starting transfers between devices: 15.7 us -> 4.21 us  [exchanged(): return lax.all_to_all(value, PLANE, 0, 0, tiled=True)]
    pallas_call x1, Pallas kernels: 7.08 us -> 3.71 us  [run_payload(): pl.pallas_call(payload_kernel, out_shape=jax.ShapeDtypeStruct((members, *...]
    unnamed x18 -> x16, local copies, waits for them, and re-layouts: 4.17 us -> 2.2 us
  transfers between devices with their start and end apart: 15 -> 14, of which waited for: 9 -> 9; matrix products, arithmetic and copies ran while one was open for 0% -> 0% of each run, Pallas kernels for 8% -> 0%
where the time goes in v4:
time: 193 us; the launch traced here: 192 us
  blocking collectives  139 us (72%)
  Pallas kernels  19.2 us (10%)
  waiting for transfers between devices  16.1 us (8%)
  starting transfers between devices  14.8 us (8%)
  local copies, waits for them, and re-layouts  2.2 us (1%)
    all_to_all x7, blocking collectives, exchanged(): return lax.all_to_all(value, PLANE, 0, 0, tiled=True)  139 us
    ppermute x7, waiting for transfers between devices, hop(): return lax.ppermute(value, 'segment', pairs)  9.82 us
    ppermute x7, starting transfers between devices, hop(): return lax.ppermute(value, 'segment', pairs)  9.34 us
    pallas_call x2, Pallas kernels, run_section(): pl.pallas_call(functools.partial(section_kernel, section), out_shape=(blo...  7.04 us
    pallas_call x1, Pallas kernels, run_first_section(): pl.pallas_call(first_section_kernel, out_shape=(jax.ShapeDtypeStruct(shap...  5.93 us
    all_to_all x1, starting transfers between devices, exchanged(): return lax.all_to_all(value, PLANE, 0, 0, tiled=True)  4.21 us
  transfers between devices with their start and end apart: 14, of which 9 were waited for; matrix products, arithmetic and copies ran while one was open for 0% of the time, Pallas kernels for 0%

profile of v4, /device:TPU:2, one launch (start us, length us, event | category | flops | bytes accessed | tf_op | source)
XLA Modules:
  0.0 192.4 jit_solution(6711641292084103354)
XLA Ops:
  1.3 0.7 copy-done.2
  2.2 28.4 %all_to_all.40.own_ref = bf16[32,8,896]{2,1,0:T(8,128)(2,1)S(1)} all-to-all(bf16[32,8,896]{2,1,0:T(8,128)(2,1)S(1)} %first_spread.1), channel_id=1, replica_groups=mesh['segment'=4,'dp'=8,'y'=4,'core'=2] {'dp','y'}, dimensions={0} | all-to-all | bytes 917504 | tf_op jit(solution)/shard_map/all_to_all | solution.py:518
  30.5 1.8 collective-permute-done.sib_ref
  32.3 0.7 copy-done
  33.1 0.7 copy-done.3
  33.8 5.9 %first_section.1 = (bf16[8,32,896]{2,1,0:T(8,128)(2,1)S(1)}, bf16[8,896]{1,0:T(8,128)(2,1)S(1)}, bf16[224,7168]{1,0:T(8,128)(2,1)S(1)}, bf16[224,7168]{1,0:T(8,128)(2,1)S(1)}) custom-call(bf16[32,8,896]{2,1,0:T(8,128)(2,1)S(1)} %all_to_all.40.own_ref, bf16[32,8,896]{2,1,0:T(8,128)(2,1)S(1)} %collective-permute-done.sib_ref, s32[1,2,64]{2,1,0:T(2,128)S(1)} %copy-done.3, ...), custom_call_target="tpu_custom_call" | custom-call | flops 411041792 | bytes 12845056 | tf_op jit(solution)/shard_map/first_section/pallas_call | solution.py:305
  39.7 21.1 %all_to_all.41.parts_ref = bf16[32,8,896]{2,1,0:T(8,128)(2,1)S(1)} all-to-all(bf16[32,8,896]{2,1,0:T(8,128)(2,1)S(1)} %bitcast.17), channel_id=1, replica_groups=mesh['segment'=4,'dp'=8,'y'=4,'core'=2] {'dp','y'}, dimensions={0} | all-to-all | bytes 917504 | tf_op jit(solution)/shard_map/all_to_all | solution.py:518
  60.9 1.6 collective-permute-start.4
  62.5 0.8 prepare.1
  63.3 1.4 collective-permute-done.4.chunk_ref
  64.8 19.1 %all_to_all.42 = bf16[32,8,896]{2,1,0:T(8,128)(2,1)S(1)} all-to-all(bf16[32,8,896]{2,1,0:T(8,128)(2,1)S(1)} %spread.2), channel_id=1, replica_groups=mesh['segment'=4,'dp'=8,'y'=4,'core'=2] {'dp','y'}, dimensions={0} | all-to-all | bytes 917504 | tf_op jit(solution)/shard_map/all_to_all | solution.py:518
  83.9 3.6 %section.2 = (bf16[8,32,896]{2,1,0:T(8,128)(2,1)S(1)}, bf16[8,8,896]{2,1,0:T(8,128)(2,1)S(1)}) custom-call(bf16[8,32,896]{2,1,0:T(8,128)(2,1)S(1)} %bitcast.12, s32[32,1]{1,0:T(8,128)S(1)} %get-tuple-element.55.rank_ref, f32[1,7168]{1,0:T(1,128)S(1)} %get-tuple-element.56.gain_ref, f32[8,32]{1,0:T(8,128)S(1)} %get-tuple-element.57.pick_ref, ...), custom_call_target="tpu_custom_call" | custom-call | flops 411041792 | bytes 12845056 | tf_op jit(solution)/shard_map/section/pallas_call | solution.py:176
  87.4 18.5 %all_to_all.43.parts_ref = bf16[32,8,896]{2,1,0:T(8,128)(2,1)S(1)} all-to-all(bf16[32,8,896]{2,1,0:T(8,128)(2,1)S(1)} %bitcast.19), channel_id=1, replica_groups=mesh['segment'=4,'dp'=8,'y'=4,'core'=2] {'dp','y'}, dimensions={0} | all-to-all | bytes 917504 | tf_op jit(solution)/shard_map/all_to_all | solution.py:518
  106.0 1.6 collective-permute-start.5
  107.5 2.2 %collective-permute-done.5.chunk_ref = bf16[8,896]{1,0:T(8,128)(2,1)S(1)} collective-permute-done((bf16[8,896]{1,0:T(8,128)(2,1)S(1)}, bf16[8,896]{1,0:T(8,128)(2,1)S(1)}, u32[]{:S(2)}, u32[]{:S(2)}) %collective-permute-start.5) | collective-permute-done | bytes 14368 | tf_op jit(solution)/shard_map/ppermute | solution.py:536
  109.8 17.4 %all_to_all.44 = bf16[32,8,896]{2,1,0:T(8,128)(2,1)S(1)} all-to-all(bf16[32,8,896]{2,1,0:T(8,128)(2,1)S(1)} %spread.3), channel_id=1, replica_groups=mesh['segment'=4,'dp'=8,'y'=4,'core'=2] {'dp','y'}, dimensions={0} | all-to-all | bytes 917504 | tf_op jit(solution)/shard_map/all_to_all | solution.py:518
  127.2 3.5 %section.3 = (bf16[8,32,896]{2,1,0:T(8,128)(2,1)S(1)}, bf16[8,8,896]{2,1,0:T(8,128)(2,1)S(1)}) custom-call(bf16[8,32,896]{2,1,0:T(8,128)(2,1)S(1)} %bitcast.14, s32[32,1]{1,0:T(8,128)S(1)} %get-tuple-element.55.rank_ref, f32[1,7168]{1,0:T(1,128)S(1)} %get-tuple-element.56.gain_ref, f32[8,32]{1,0:T(8,128)S(1)} %get-tuple-element.57.pick_ref, ...), custom_call_target="tpu_custom_call" | custom-call | flops 411041792 | bytes 12845056 | tf_op jit(solution)/shard_map/section/pallas_call | solution.py:176
  130.7 17.1 %all_to_all.45.parts_ref = bf16[32,8,896]{2,1,0:T(8,128)(2,1)S(1)} all-to-all(bf16[32,8,896]{2,1,0:T(8,128)(2,1)S(1)} %bitcast.18), channel_id=1, replica_groups=mesh['segment'=4,'dp'=8,'y'=4,'core'=2] {'dp','y'}, dimensions={0} | all-to-all | bytes 917504 | tf_op jit(solution)/shard_map/all_to_all | solution.py:518
  147.9 1.8 collective-permute-start.6
  149.6 3.0 %collective-permute-done.6.chunk_ref = bf16[8,896]{1,0:T(8,128)(2,1)S(1)} collective-permute-done((bf16[8,896]{1,0:T(8,128)(2,1)S(1)}, bf16[8,896]{1,0:T(8,128)(2,1)S(1)}, u32[]{:S(2)}, u32[]{:S(2)}) %collective-permute-start.6) | collective-permute-done | bytes 14368 | tf_op jit(solution)/shard_map/ppermute | solution.py:536
  152.6 3.7 %payload.1 = bf16[32,8,896]{2,1,0:T(8,128)(2,1)S(1)} custom-call(bf16[8,896]{1,0:T(8,128)(2,1)S(1)} %collective-permute-done.6.chunk_ref, bf16[8,32,896]{2,1,0:T(8,128)(2,1)S(1)} %bitcast.13, bf16[8,32,896]{2,1,0:T(8,128)(2,1)S(1)} %bitcast.15, s32[8,32]{1,0:T(8,128)S(1)} %get-tuple-element.64.source_ref, s32[32,1]{1,0:T(8,128)S(1)} %get-tuple-element.65.wanted_ref, ...), custom_call_target="tpu_custom_call" | custom-call | tf_op jit(solution)/shard_map/payload/pallas_call | solution.py:499
  156.3 17.1 %all_to_all.46 = bf16[32,8,896]{2,1,0:T(8,128)(2,1)S(1)} all-to-all(bf16[32,8,896]{2,1,0:T(8,128)(2,1)S(1)} %payload.1), channel_id=1, replica_groups=mesh['segment'=4,'dp'=8,'y'=4,'core'=2] {'dp','y'}, dimensions={0} | all-to-all | bytes 917504 | tf_op jit(solution)/shard_map/all_to_all | solution.py:518
  173.5 0.8 last_section.1
  174.3 4.2 %all-to-all-start.7 = ((bf16[32,8,896]{2,1,0:T(8,128)(2,1)}), bf16[32,8,896]{2,1,0:T(8,128)(2,1)S(1)}, u32[]{:S(2)}, u32[]{:S(2)}) async-start(bf16[32,8,896]{2,1,0:T(8,128)(2,1)} %get-tuple-element.69), calls=%async_computation.7 | async-start | bytes 917504 | tf_op jit(solution)/shard_map/all_to_all | solution.py:518
  179.1 0.8 collective-permute-done.8
  180.0 2.2 %collective-permute-start.11 = (f32[1,128]{1,0:T(1,128)S(1)}, f32[1,128]{1,0:T(1,128)S(1)}, u32[]{:S(2)}, u32[]{:S(2)}) collective-permute-start(f32[1,128]{1,0:T(1,128)S(1)} %add.16), channel_id=1, source_target_pairs={{0,128},{64,192},{128,0},{192,64},{1,129},{65,193},{129,1},{193,65... | collective-permute-start | bytes 1544 | tf_op jit(solution)/shard_map/ppermute | solution.py:536
  182.2 2.2 %collective-permute-start.10 = (f32[1,128]{1,0:T(1,128)S(1)}, f32[1,128]{1,0:T(1,128)S(1)}, u32[]{:S(2)}, u32[]{:S(2)}) collective-permute-start(f32[1,128]{1,0:T(1,128)S(1)} %add.16), channel_id=1, source_target_pairs={{0,64},{64,128},{128,192},{192,0},{1,65},{65,129},{129,193},{193,1... | collective-permute-start | bytes 1544 | tf_op jit(solution)/shard_map/ppermute | solution.py:536
  184.4 0.8 collective-permute-done.11
  185.1 0.6 collective-permute-done.10
  186.2 1.8 collective-permute-done.9.returned_ref
  188.1 3.7 %all-to-all-done.7.parts_ref = bf16[32,8,896]{2,1,0:T(8,128)(2,1)S(1)} async-done(((bf16[32,8,896]{2,1,0:T(8,128)(2,1)}), bf16[32,8,896]{2,1,0:T(8,128)(2,1)S(1)}, u32[]{:S(2)}, u32[]{:S(2)}) %all-to-all-start.7) | async-done | bytes 458784 | tf_op jit(solution)/shard_map/all_to_all | solution.py:518
  191.8 0.6 finish.1
  (36 shorter events, 2.3 us)
Async XLA Ops:
  0.6 29.9 %collective-permute-start.3 = (bf16[400,7168]{1,0:T(8,128)(2,1)}, bf16[400,7168]{1,0:T(8,128)(2,1)S(1)}, u32[]{:S(2)}, u32[]{:S(2)}) collective-permute-start(bf16[400,7168]{1,0:T(8,128)(2,1)} %head_a_ref.1), channel_id=1, source_target_pairs={{0,1},{1,0},{2,3},{3,2},{4,5},{5,4},{6,7},{7,6},{8,9},{9,8},{10,11... | collective-permute-start | bytes 17203208 | tf_op jit(solution)/shard_map/ppermute | solution.py:514
  0.7 29.8 %collective-permute-start.1 = (bf16[224,7168]{1,0:T(8,128)(2,1)}, bf16[224,7168]{1,0:T(8,128)(2,1)S(1)}, u32[]{:S(2)}, u32[]{:S(2)}) collective-permute-start(bf16[224,7168]{1,0:T(8,128)(2,1)} %bitcast.21), channel_id=1, source_target_pairs={{0,1},{1,0},{2,3},{3,2},{4,5},{5,4},{6,7},{7,6},{8,9},{9,8},{10,11... | collective-permute-start | bytes 9633800 | tf_op jit(solution)/shard_map/ppermute | solution.py:514
  1.2 29.3 %collective-permute-start.2 = (bf16[224,7168]{1,0:T(8,128)(2,1)}, bf16[224,7168]{1,0:T(8,128)(2,1)S(1)}, u32[]{:S(2)}, u32[]{:S(2)}) collective-permute-start(bf16[224,7168]{1,0:T(8,128)(2,1)} %bitcast.23), channel_id=1, source_target_pairs={{0,1},{1,0},{2,3},{3,2},{4,5},{5,4},{6,7},{7,6},{8,9},{9,8},{10,11... | collective-permute-start | bytes 9633800 | tf_op jit(solution)/shard_map/ppermute | solution.py:514
  1.3 0.7 copy-start.2
  2.1 60.4 %copy-start.4 = (s32[1,64]{1,0:T(1,128)S(1)}, s32[1,64]{1,0:T(1,128)}, u32[]{:S(2)}) copy-start(s32[1,64]{1,0:T(1,128)} %exit_ref) | copy-start | bytes 772
  2.1 60.4 %copy-start.5 = (s32[1,64]{1,0:T(1,128)S(1)}, s32[1,64]{1,0:T(1,128)}, u32[]{:S(2)}) copy-start(s32[1,64]{1,0:T(1,128)} %target_ref) | copy-start | bytes 772
  30.5 1.8 collective-permute-start
  32.3 0.7 copy-start
  33.1 0.7 copy-start.3
  60.9 3.8 %collective-permute-start.4 = (bf16[8,896]{1,0:T(8,128)(2,1)S(1)}, bf16[8,896]{1,0:T(8,128)(2,1)S(1)}, u32[]{:S(2)}, u32[]{:S(2)}) collective-permute-start(bf16[8,896]{1,0:T(8,128)(2,1)S(1)} %settle.3), channel_id=1, source_target_pairs={{0,64},{64,128},{128,192},{192,0},{1,65},{65,129},{129,193},{193,1... | collective-permute-start | bytes 43016 | tf_op jit(solution)/shard_map/ppermute | solution.py:536
  106.0 3.8 %collective-permute-start.5 = (bf16[8,896]{1,0:T(8,128)(2,1)S(1)}, bf16[8,896]{1,0:T(8,128)(2,1)S(1)}, u32[]{:S(2)}, u32[]{:S(2)}) collective-permute-start(bf16[8,896]{1,0:T(8,128)(2,1)S(1)} %settle.4), channel_id=1, source_target_pairs={{0,64},{64,128},{128,192},{192,0},{1,65},{65,129},{129,193},{193,1... | collective-permute-start | bytes 43016 | tf_op jit(solution)/shard_map/ppermute | solution.py:536
  127.2 25.4 %slice-start = ((s8[5734400]{0:T(1024)(128)(4,1)}), s8[4194304]{0:T(1024)(128)(4,1)S(1)}, s32[]{:S(2)}) async-start(s8[5734400]{0:T(1024)(128)(4,1)} %bitcast.10), calls=%async_computation.8 | async-start | bytes 8388608
  127.2 25.4 %slice-start.1 = ((s8[5734400]{0:T(1024)(128)(4,1)}), s8[1540096]{0:T(1024)(128)(4,1)S(1)}, s32[]{:S(2)}) async-start(s8[5734400]{0:T(1024)(128)(4,1)} %bitcast.10), calls=%async_computation.9 | async-start | bytes 3080192
  127.2 25.4 %copy-start.1 = (f32[7168]{0:T(1024)S(1)}, f32[7168]{0:T(1024)}, u32[]{:S(2)}) copy-start(f32[7168]{0:T(1024)} %param.16) | copy-start | bytes 86020
  147.9 4.7 %collective-permute-start.6 = (bf16[8,896]{1,0:T(8,128)(2,1)S(1)}, bf16[8,896]{1,0:T(8,128)(2,1)S(1)}, u32[]{:S(2)}, u32[]{:S(2)}) collective-permute-start(bf16[8,896]{1,0:T(8,128)(2,1)S(1)} %settle.5), channel_id=1, source_target_pairs={{0,64},{64,128},{128,192},{192,0},{1,65},{65,129},{129,193},{193,1... | collective-permute-start | bytes 43016 | tf_op jit(solution)/shard_map/ppermute | solution.py:536
  174.3 17.5 %all-to-all-start.7 = ((bf16[32,8,896]{2,1,0:T(8,128)(2,1)}), bf16[32,8,896]{2,1,0:T(8,128)(2,1)S(1)}, u32[]{:S(2)}, u32[]{:S(2)}) async-start(bf16[32,8,896]{2,1,0:T(8,128)(2,1)} %get-tuple-element.69), calls=%async_computation.7 | async-start | bytes 917504 | tf_op jit(solution)/shard_map/all_to_all | solution.py:518
  178.5 1.4 collective-permute-start.7
  178.6 1.3 collective-permute-start.8
  179.9 4.5 %collective-permute-start.12 = (f32[1,128]{1,0:T(1,128)S(1)}, f32[1,128]{1,0:T(1,128)S(1)}, u32[]{:S(2)}, u32[]{:S(2)}) collective-permute-start(f32[1,128]{1,0:T(1,128)S(1)} %add.16), channel_id=1, source_target_pairs={{0,192},{64,0},{128,64},{192,128},{1,193},{65,1},{129,65},{193,129... | collective-permute-start | bytes 1544 | tf_op jit(solution)/shard_map/ppermute | solution.py:536
  180.0 5.1 %collective-permute-start.11 = (f32[1,128]{1,0:T(1,128)S(1)}, f32[1,128]{1,0:T(1,128)S(1)}, u32[]{:S(2)}, u32[]{:S(2)}) collective-permute-start(f32[1,128]{1,0:T(1,128)S(1)} %add.16), channel_id=1, source_target_pairs={{0,128},{64,192},{128,0},{192,64},{1,129},{65,193},{129,1},{193,65... | collective-permute-start | bytes 1544 | tf_op jit(solution)/shard_map/ppermute | solution.py:536
  182.2 3.5 %collective-permute-start.10 = (f32[1,128]{1,0:T(1,128)S(1)}, f32[1,128]{1,0:T(1,128)S(1)}, u32[]{:S(2)}, u32[]{:S(2)}) collective-permute-start(f32[1,128]{1,0:T(1,128)S(1)} %add.16), channel_id=1, source_target_pairs={{0,64},{64,128},{128,192},{192,0},{1,65},{65,129},{129,193},{193,1... | collective-permute-start | bytes 1544 | tf_op jit(solution)/shard_map/ppermute | solution.py:536
  184.4 3.7 %collective-permute-start.9 = (bf16[8,896]{1,0:T(8,128)(2,1)S(1)}, bf16[8,896]{1,0:T(8,128)(2,1)S(1)}, u32[]{:S(2)}, u32[]{:S(2)}) collective-permute-start(bf16[8,896]{1,0:T(8,128)(2,1)S(1)} %add.15.row_ref), channel_id=1, source_target_pairs={{0,192},{64,0},{128,64},{192,128},{1,193},{65,1},{129,65},{193,129... | collective-permute-start | bytes 43016 | tf_op jit(solution)/shard_map/ppermute | solution.py:536

commit v5 on v4

--- a/solution.py
+++ b/solution.py
@@ -11,7 +11,7 @@
 SQRT_HALF = 0.7071067811865476
 FIRST_LIMIT = 39 * 1024 * 1024
 SMALL_LIMIT = 4 * 1024 * 1024
-WEIGHT_PARTS = 2
+WEIGHT_PARTS = 7
 PLANE = ("dp", "y")
 NT = (((1,), (1,)), ((), ()))
 VMEM = pl.BlockSpec(memory_space=pltpu.VMEM)
@@ -268,7 +268,7 @@
     core = lax.axis_index("core")
     up_copies = copies_of(held_up_ref, up_a_ref, sems, 0, WEIGHT_PARTS)
     down_copies = copies_of(held_down_ref, down_a_ref, sems, WEIGHT_PARTS, WEIGHT_PARTS)
-    for copy in up_copies + down_copies:
+    for copy in up_copies:
         copy.start()
     members, blocks, cols = gathered_ref.shape
     sub = chunk_ref.shape[0]
@@ -278,6 +278,8 @@
         gathered_ref[i] = jnp.where(row & 1 == core, own_ref[place], sib_ref[place])
     rows = jnp.swapaxes(gathered_ref[...].astype(jnp.float32), 0, 1)
     rows_ref[...] = rows.astype(jnp.bfloat16)
+    for copy in down_copies:
+        copy.start()
     scale = normalise(rows_ref, gain_ref, None, normed_ref)
     block = lax.axis_index("dp")
     first_row = lax.axis_index("y") * sub

time: 193 us -> 193 us (level)
  no operation moved by 1% of the time
where the time goes in v5:
time: 193 us; the launch traced here: 192 us
  blocking collectives  139 us (72%)
  Pallas kernels  19.3 us (10%)
  waiting for transfers between devices  16.1 us (8%)
  starting transfers between devices  14.8 us (8%)
  local copies, waits for them, and re-layouts  2.2 us (1%)
    all_to_all x7, blocking collectives, exchanged(): return lax.all_to_all(value, PLANE, 0, 0, tiled=True)  139 us
    ppermute x7, waiting for transfers between devices, hop(): return lax.ppermute(value, 'segment', pairs)  9.84 us
    ppermute x7, starting transfers between devices, hop(): return lax.ppermute(value, 'segment', pairs)  9.31 us
    pallas_call x2, Pallas kernels, run_section(): pl.pallas_call(functools.partial(section_kernel, section), out_shape=(blo...  7.04 us
    pallas_call x1, Pallas kernels, run_first_section(): pl.pallas_call(first_section_kernel, out_shape=(jax.ShapeDtypeStruct(shap...  6.03 us
    all_to_all x1, starting transfers between devices, exchanged(): return lax.all_to_all(value, PLANE, 0, 0, tiled=True)  4.21 us
  transfers between devices with their start and end apart: 14, of which 9 were waited for; matrix products, arithmetic and copies ran while one was open for 0% of the time, Pallas kernels for 0%

profile of v5, /device:TPU:2, one launch (start us, length us, event | category | flops | bytes accessed | tf_op | source)
XLA Modules:
  0.0 192.5 jit_solution(11585054138069126170)
XLA Ops:
  1.3 0.7 copy-done.2
  2.2 28.4 %all_to_all.40.own_ref = bf16[32,8,896]{2,1,0:T(8,128)(2,1)S(1)} all-to-all(bf16[32,8,896]{2,1,0:T(8,128)(2,1)S(1)} %first_spread.1), channel_id=1, replica_groups=mesh['segment'=4,'dp'=8,'y'=4,'core'=2] {'dp','y'}, dimensions={0} | all-to-all | bytes 917504 | tf_op jit(solution)/shard_map/all_to_all | solution.py:520
  30.5 1.8 collective-permute-done.sib_ref
  32.3 0.7 copy-done
  33.1 0.7 copy-done.3
  33.8 6.0 %first_section.1 = (bf16[8,32,896]{2,1,0:T(8,128)(2,1)S(1)}, bf16[8,896]{1,0:T(8,128)(2,1)S(1)}, bf16[224,7168]{1,0:T(8,128)(2,1)S(1)}, bf16[224,7168]{1,0:T(8,128)(2,1)S(1)}) custom-call(bf16[32,8,896]{2,1,0:T(8,128)(2,1)S(1)} %all_to_all.40.own_ref, bf16[32,8,896]{2,1,0:T(8,128)(2,1)S(1)} %collective-permute-done.sib_ref, s32[1,2,64]{2,1,0:T(2,128)S(1)} %copy-done.3, ...), custom_call_target="tpu_custom_call" | custom-call | flops 411041792 | bytes 12845056 | tf_op jit(solution)/shard_map/first_section/pallas_call | solution.py:307
  39.8 21.1 %all_to_all.41.parts_ref = bf16[32,8,896]{2,1,0:T(8,128)(2,1)S(1)} all-to-all(bf16[32,8,896]{2,1,0:T(8,128)(2,1)S(1)} %bitcast.17), channel_id=1, replica_groups=mesh['segment'=4,'dp'=8,'y'=4,'core'=2] {'dp','y'}, dimensions={0} | all-to-all | bytes 917504 | tf_op jit(solution)/shard_map/all_to_all | solution.py:520
  61.0 1.6 collective-permute-start.4
  62.6 0.8 prepare.1
  63.4 1.4 collective-permute-done.4.chunk_ref
  64.9 19.1 %all_to_all.42 = bf16[32,8,896]{2,1,0:T(8,128)(2,1)S(1)} all-to-all(bf16[32,8,896]{2,1,0:T(8,128)(2,1)S(1)} %spread.2), channel_id=1, replica_groups=mesh['segment'=4,'dp'=8,'y'=4,'core'=2] {'dp','y'}, dimensions={0} | all-to-all | bytes 917504 | tf_op jit(solution)/shard_map/all_to_all | solution.py:520
  84.0 3.6 %section.2 = (bf16[8,32,896]{2,1,0:T(8,128)(2,1)S(1)}, bf16[8,8,896]{2,1,0:T(8,128)(2,1)S(1)}) custom-call(bf16[8,32,896]{2,1,0:T(8,128)(2,1)S(1)} %bitcast.12, s32[32,1]{1,0:T(8,128)S(1)} %get-tuple-element.55.rank_ref, f32[1,7168]{1,0:T(1,128)S(1)} %get-tuple-element.56.gain_ref, f32[8,32]{1,0:T(8,128)S(1)} %get-tuple-element.57.pick_ref, ...), custom_call_target="tpu_custom_call" | custom-call | flops 411041792 | bytes 12845056 | tf_op jit(solution)/shard_map/section/pallas_call | solution.py:176
  87.5 18.5 %all_to_all.43.parts_ref = bf16[32,8,896]{2,1,0:T(8,128)(2,1)S(1)} all-to-all(bf16[32,8,896]{2,1,0:T(8,128)(2,1)S(1)} %bitcast.19), channel_id=1, replica_groups=mesh['segment'=4,'dp'=8,'y'=4,'core'=2] {'dp','y'}, dimensions={0} | all-to-all | bytes 917504 | tf_op jit(solution)/shard_map/all_to_all | solution.py:520
  106.1 1.6 collective-permute-start.5
  107.6 2.2 %collective-permute-done.5.chunk_ref = bf16[8,896]{1,0:T(8,128)(2,1)S(1)} collective-permute-done((bf16[8,896]{1,0:T(8,128)(2,1)S(1)}, bf16[8,896]{1,0:T(8,128)(2,1)S(1)}, u32[]{:S(2)}, u32[]{:S(2)}) %collective-permute-start.5) | collective-permute-done | bytes 14368 | tf_op jit(solution)/shard_map/ppermute | solution.py:538
  109.9 17.4 %all_to_all.44 = bf16[32,8,896]{2,1,0:T(8,128)(2,1)S(1)} all-to-all(bf16[32,8,896]{2,1,0:T(8,128)(2,1)S(1)} %spread.3), channel_id=1, replica_groups=mesh['segment'=4,'dp'=8,'y'=4,'core'=2] {'dp','y'}, dimensions={0} | all-to-all | bytes 917504 | tf_op jit(solution)/shard_map/all_to_all | solution.py:520
  127.3 3.5 %section.3 = (bf16[8,32,896]{2,1,0:T(8,128)(2,1)S(1)}, bf16[8,8,896]{2,1,0:T(8,128)(2,1)S(1)}) custom-call(bf16[8,32,896]{2,1,0:T(8,128)(2,1)S(1)} %bitcast.14, s32[32,1]{1,0:T(8,128)S(1)} %get-tuple-element.55.rank_ref, f32[1,7168]{1,0:T(1,128)S(1)} %get-tuple-element.56.gain_ref, f32[8,32]{1,0:T(8,128)S(1)} %get-tuple-element.57.pick_ref, ...), custom_call_target="tpu_custom_call" | custom-call | flops 411041792 | bytes 12845056 | tf_op jit(solution)/shard_map/section/pallas_call | solution.py:176
  130.8 17.1 %all_to_all.45.parts_ref = bf16[32,8,896]{2,1,0:T(8,128)(2,1)S(1)} all-to-all(bf16[32,8,896]{2,1,0:T(8,128)(2,1)S(1)} %bitcast.18), channel_id=1, replica_groups=mesh['segment'=4,'dp'=8,'y'=4,'core'=2] {'dp','y'}, dimensions={0} | all-to-all | bytes 917504 | tf_op jit(solution)/shard_map/all_to_all | solution.py:520
  148.0 1.7 collective-permute-start.6
  149.7 3.0 %collective-permute-done.6.chunk_ref = bf16[8,896]{1,0:T(8,128)(2,1)S(1)} collective-permute-done((bf16[8,896]{1,0:T(8,128)(2,1)S(1)}, bf16[8,896]{1,0:T(8,128)(2,1)S(1)}, u32[]{:S(2)}, u32[]{:S(2)}) %collective-permute-start.6) | collective-permute-done | bytes 14368 | tf_op jit(solution)/shard_map/ppermute | solution.py:538
  152.7 3.7 %payload.1 = bf16[32,8,896]{2,1,0:T(8,128)(2,1)S(1)} custom-call(bf16[8,896]{1,0:T(8,128)(2,1)S(1)} %collective-permute-done.6.chunk_ref, bf16[8,32,896]{2,1,0:T(8,128)(2,1)S(1)} %bitcast.13, bf16[8,32,896]{2,1,0:T(8,128)(2,1)S(1)} %bitcast.15, s32[8,32]{1,0:T(8,128)S(1)} %get-tuple-element.64.source_ref, s32[32,1]{1,0:T(8,128)S(1)} %get-tuple-element.65.wanted_ref, ...), custom_call_target="tpu_custom_call" | custom-call | tf_op jit(solution)/shard_map/payload/pallas_call | solution.py:501
  156.4 17.1 %all_to_all.46 = bf16[32,8,896]{2,1,0:T(8,128)(2,1)S(1)} all-to-all(bf16[32,8,896]{2,1,0:T(8,128)(2,1)S(1)} %payload.1), channel_id=1, replica_groups=mesh['segment'=4,'dp'=8,'y'=4,'core'=2] {'dp','y'}, dimensions={0} | all-to-all | bytes 917504 | tf_op jit(solution)/shard_map/all_to_all | solution.py:520
  173.6 0.8 last_section.1
  174.4 4.2 %all-to-all-start.7 = ((bf16[32,8,896]{2,1,0:T(8,128)(2,1)}), bf16[32,8,896]{2,1,0:T(8,128)(2,1)S(1)}, u32[]{:S(2)}, u32[]{:S(2)}) async-start(bf16[32,8,896]{2,1,0:T(8,128)(2,1)} %get-tuple-element.69), calls=%async_computation.7 | async-start | bytes 917504 | tf_op jit(solution)/shard_map/all_to_all | solution.py:520
  179.2 0.8 collective-permute-done.8
  180.1 2.2 %collective-permute-start.11 = (f32[1,128]{1,0:T(1,128)S(1)}, f32[1,128]{1,0:T(1,128)S(1)}, u32[]{:S(2)}, u32[]{:S(2)}) collective-permute-start(f32[1,128]{1,0:T(1,128)S(1)} %add.16), channel_id=1, source_target_pairs={{0,128},{64,192},{128,0},{192,64},{1,129},{65,193},{129,1},{193,65... | collective-permute-start | bytes 1544 | tf_op jit(solution)/shard_map/ppermute | solution.py:538
  182.3 2.2 %collective-permute-start.10 = (f32[1,128]{1,0:T(1,128)S(1)}, f32[1,128]{1,0:T(1,128)S(1)}, u32[]{:S(2)}, u32[]{:S(2)}) collective-permute-start(f32[1,128]{1,0:T(1,128)S(1)} %add.16), channel_id=1, source_target_pairs={{0,64},{64,128},{128,192},{192,0},{1,65},{65,129},{129,193},{193,1... | collective-permute-start | bytes 1544 | tf_op jit(solution)/shard_map/ppermute | solution.py:538
  184.5 0.8 collective-permute-done.11
  185.2 0.6 collective-permute-done.10
  186.3 1.8 collective-permute-done.9.returned_ref
  188.2 3.7 %all-to-all-done.7.parts_ref = bf16[32,8,896]{2,1,0:T(8,128)(2,1)S(1)} async-done(((bf16[32,8,896]{2,1,0:T(8,128)(2,1)}), bf16[32,8,896]{2,1,0:T(8,128)(2,1)S(1)}, u32[]{:S(2)}, u32[]{:S(2)}) %all-to-all-start.7) | async-done | bytes 458784 | tf_op jit(solution)/shard_map/all_to_all | solution.py:520
  191.9 0.6 finish.1
  (36 shorter events, 2.3 us)
Async XLA Ops:
  0.6 29.9 %collective-permute-start.3 = (bf16[400,7168]{1,0:T(8,128)(2,1)}, bf16[400,7168]{1,0:T(8,128)(2,1)S(1)}, u32[]{:S(2)}, u32[]{:S(2)}) collective-permute-start(bf16[400,7168]{1,0:T(8,128)(2,1)} %head_a_ref.1), channel_id=1, source_target_pairs={{0,1},{1,0},{2,3},{3,2},{4,5},{5,4},{6,7},{7,6},{8,9},{9,8},{10,11... | collective-permute-start | bytes 17203208 | tf_op jit(solution)/shard_map/ppermute | solution.py:516
  0.7 29.8 %collective-permute-start.1 = (bf16[224,7168]{1,0:T(8,128)(2,1)}, bf16[224,7168]{1,0:T(8,128)(2,1)S(1)}, u32[]{:S(2)}, u32[]{:S(2)}) collective-permute-start(bf16[224,7168]{1,0:T(8,128)(2,1)} %bitcast.21), channel_id=1, source_target_pairs={{0,1},{1,0},{2,3},{3,2},{4,5},{5,4},{6,7},{7,6},{8,9},{9,8},{10,11... | collective-permute-start | bytes 9633800 | tf_op jit(solution)/shard_map/ppermute | solution.py:516
  1.2 29.3 %collective-permute-start.2 = (bf16[224,7168]{1,0:T(8,128)(2,1)}, bf16[224,7168]{1,0:T(8,128)(2,1)S(1)}, u32[]{:S(2)}, u32[]{:S(2)}) collective-permute-start(bf16[224,7168]{1,0:T(8,128)(2,1)} %bitcast.23), channel_id=1, source_target_pairs={{0,1},{1,0},{2,3},{3,2},{4,5},{5,4},{6,7},{7,6},{8,9},{9,8},{10,11... | collective-permute-start | bytes 9633800 | tf_op jit(solution)/shard_map/ppermute | solution.py:516
  1.3 0.7 copy-start.2
  2.1 60.5 %copy-start.4 = (s32[1,64]{1,0:T(1,128)S(1)}, s32[1,64]{1,0:T(1,128)}, u32[]{:S(2)}) copy-start(s32[1,64]{1,0:T(1,128)} %exit_ref) | copy-start | bytes 772
  2.1 60.5 %copy-start.5 = (s32[1,64]{1,0:T(1,128)S(1)}, s32[1,64]{1,0:T(1,128)}, u32[]{:S(2)}) copy-start(s32[1,64]{1,0:T(1,128)} %target_ref) | copy-start | bytes 772
  30.5 1.8 collective-permute-start
  32.3 0.7 copy-start
  33.1 0.7 copy-start.3
  61.0 3.8 %collective-permute-start.4 = (bf16[8,896]{1,0:T(8,128)(2,1)S(1)}, bf16[8,896]{1,0:T(8,128)(2,1)S(1)}, u32[]{:S(2)}, u32[]{:S(2)}) collective-permute-start(bf16[8,896]{1,0:T(8,128)(2,1)S(1)} %settle.3), channel_id=1, source_target_pairs={{0,64},{64,128},{128,192},{192,0},{1,65},{65,129},{129,193},{193,1... | collective-permute-start | bytes 43016 | tf_op jit(solution)/shard_map/ppermute | solution.py:538
  106.1 3.8 %collective-permute-start.5 = (bf16[8,896]{1,0:T(8,128)(2,1)S(1)}, bf16[8,896]{1,0:T(8,128)(2,1)S(1)}, u32[]{:S(2)}, u32[]{:S(2)}) collective-permute-start(bf16[8,896]{1,0:T(8,128)(2,1)S(1)} %settle.4), channel_id=1, source_target_pairs={{0,64},{64,128},{128,192},{192,0},{1,65},{65,129},{129,193},{193,1... | collective-permute-start | bytes 43016 | tf_op jit(solution)/shard_map/ppermute | solution.py:538
  127.3 25.3 %slice-start = ((s8[5734400]{0:T(1024)(128)(4,1)}), s8[4194304]{0:T(1024)(128)(4,1)S(1)}, s32[]{:S(2)}) async-start(s8[5734400]{0:T(1024)(128)(4,1)} %bitcast.10), calls=%async_computation.8 | async-start | bytes 8388608
  127.3 25.3 %slice-start.1 = ((s8[5734400]{0:T(1024)(128)(4,1)}), s8[1540096]{0:T(1024)(128)(4,1)S(1)}, s32[]{:S(2)}) async-start(s8[5734400]{0:T(1024)(128)(4,1)} %bitcast.10), calls=%async_computation.9 | async-start | bytes 3080192
  127.3 25.3 %copy-start.1 = (f32[7168]{0:T(1024)S(1)}, f32[7168]{0:T(1024)}, u32[]{:S(2)}) copy-start(f32[7168]{0:T(1024)} %param.16) | copy-start | bytes 86020
  148.0 4.7 %collective-permute-start.6 = (bf16[8,896]{1,0:T(8,128)(2,1)S(1)}, bf16[8,896]{1,0:T(8,128)(2,1)S(1)}, u32[]{:S(2)}, u32[]{:S(2)}) collective-permute-start(bf16[8,896]{1,0:T(8,128)(2,1)S(1)} %settle.5), channel_id=1, source_target_pairs={{0,64},{64,128},{128,192},{192,0},{1,65},{65,129},{129,193},{193,1... | collective-permute-start | bytes 43016 | tf_op jit(solution)/shard_map/ppermute | solution.py:538
  174.4 17.5 %all-to-all-start.7 = ((bf16[32,8,896]{2,1,0:T(8,128)(2,1)}), bf16[32,8,896]{2,1,0:T(8,128)(2,1)S(1)}, u32[]{:S(2)}, u32[]{:S(2)}) async-start(bf16[32,8,896]{2,1,0:T(8,128)(2,1)} %get-tuple-element.69), calls=%async_computation.7 | async-start | bytes 917504 | tf_op jit(solution)/shard_map/all_to_all | solution.py:520
  178.6 1.4 collective-permute-start.7
  178.7 1.3 collective-permute-start.8
  180.0 4.5 %collective-permute-start.12 = (f32[1,128]{1,0:T(1,128)S(1)}, f32[1,128]{1,0:T(1,128)S(1)}, u32[]{:S(2)}, u32[]{:S(2)}) collective-permute-start(f32[1,128]{1,0:T(1,128)S(1)} %add.16), channel_id=1, source_target_pairs={{0,192},{64,0},{128,64},{192,128},{1,193},{65,1},{129,65},{193,129... | collective-permute-start | bytes 1544 | tf_op jit(solution)/shard_map/ppermute | solution.py:538
  180.1 5.1 %collective-permute-start.11 = (f32[1,128]{1,0:T(1,128)S(1)}, f32[1,128]{1,0:T(1,128)S(1)}, u32[]{:S(2)}, u32[]{:S(2)}) collective-permute-start(f32[1,128]{1,0:T(1,128)S(1)} %add.16), channel_id=1, source_target_pairs={{0,128},{64,192},{128,0},{192,64},{1,129},{65,193},{129,1},{193,65... | collective-permute-start | bytes 1544 | tf_op jit(solution)/shard_map/ppermute | solution.py:538
  182.3 3.5 %collective-permute-start.10 = (f32[1,128]{1,0:T(1,128)S(1)}, f32[1,128]{1,0:T(1,128)S(1)}, u32[]{:S(2)}, u32[]{:S(2)}) collective-permute-start(f32[1,128]{1,0:T(1,128)S(1)} %add.16), channel_id=1, source_target_pairs={{0,64},{64,128},{128,192},{192,0},{1,65},{65,129},{129,193},{193,1... | collective-permute-start | bytes 1544 | tf_op jit(solution)/shard_map/ppermute | solution.py:538
  184.5 3.7 %collective-permute-start.9 = (bf16[8,896]{1,0:T(8,128)(2,1)S(1)}, bf16[8,896]{1,0:T(8,128)(2,1)S(1)}, u32[]{:S(2)}, u32[]{:S(2)}) collective-permute-start(bf16[8,896]{1,0:T(8,128)(2,1)S(1)} %add.15.row_ref), channel_id=1, source_target_pairs={{0,192},{64,0},{128,64},{192,128},{1,193},{65,1},{129,65},{193,129... | collective-permute-start | bytes 43016 | tf_op jit(solution)/shard_map/ppermute | solution.py:538
